TPU v7x, 256 devices: a whole 4x4x8 slice. The times are simulated.
256 devices in a mesh: seq: 64 (over x, y, z_lo, core), head: 4 (over z_hi).
Axes of the slice: x: 4, y: 4, z: 8 (z_hi: 4, z_lo: 2; z = z_hi * 2 + z_lo), core: 2. Of those that a mesh axis runs over, the one named last changes fastest.
Arguments:
- queries: bfloat16 [32768, 2048], P('seq', 'head'), may hold values from -7.5 to 7.5
- key_rows: bfloat16 [32768, 2048], P('seq', 'head'), may hold values from -7.5 to 7.5
- value_rows: bfloat16 [32768, 4096], P('seq', 'head'), may hold values from -6 to 6
- input_gate: float32 [32768, 8], P('seq', 'head'), may hold values from -3 to 220
- forget_gate: float32 [32768, 8], P('seq', 'head')
- out_weight: bfloat16 [4096, 4096], P('head', 'seq'), may hold values from -0.25 to 0.25
Outputs:
- projected: bfloat16 [32768, 4096], P('seq', 'head')
All inputs are finite; a program needn't handle non-finite values.
Results may differ from a plain program's by a relative error of at most 0.015.
Values may be sent and summed in bfloat16 or wider, within the bound.
No kernel may reach another device: no remote copies, remote signals or barrier semaphores. Data moves between devices by JAX's collectives and lax.ppermute only.
A program may use at most 192 MiB of HBM per device.

v0:
```python
import jax
import jax.numpy as jnp
from jax import lax
from jax.sharding import PartitionSpec as P

DH = 512
DK = 256


def entering(part, axis, combine, identity):
    place = lax.axis_index(axis)
    gathered = jax.tree.map(lambda a: lax.all_gather(a, axis), part)
    state = jax.tree.map(lambda a, e: jnp.zeros_like(a) + jnp.asarray(e, a.dtype), part, identity)

    def one(hop, state):
        return combine(
            state, jax.tree.map(lambda a: lax.dynamic_index_in_dim(a, hop, 0, False), gathered)
        )

    return lax.fori_loop(0, place, one, state)


def local_terms(queries, key_rows, value_rows, in_gate, forget):
    score_scale = DK ** (-0.5)
    decay_sum = jnp.cumsum(jax.nn.log_sigmoid(forget), axis=0)
    scores = (
        jnp.einsum("thd,jhd->htj", queries, key_rows, preferred_element_type=jnp.float32)
        * score_scale
    )
    length = queries.shape[0]
    causal = jnp.arange(length)[:, None] >= jnp.arange(length)[None, :]
    weight_logits = decay_sum.T[:, :, None] - decay_sum.T[:, None, :] + in_gate.T[:, None, :]
    weight_logits = jnp.where(causal[None], weight_logits, -jnp.inf)
    row_peak = jnp.max(weight_logits, axis=2)
    weights = (jnp.exp(weight_logits - row_peak[:, :, None]) * scores).astype(jnp.bfloat16)
    intra_numer = jnp.einsum(
        "htj,jhd->thd", weights, value_rows, preferred_element_type=jnp.float32
    )
    intra_denom = jnp.sum(weights.astype(jnp.float32), axis=2).T
    shard_decay = decay_sum[-1]
    log_source = shard_decay[None, :] - decay_sum + in_gate
    local_peak = jnp.max(log_source, axis=0)
    scaled_keys = (
        key_rows.astype(jnp.float32) * jnp.exp(log_source - local_peak[None, :])[:, :, None]
    )
    local_normal = jnp.sum(scaled_keys, axis=0)
    weighted_keys = scaled_keys.astype(jnp.bfloat16)
    local_memory = jnp.einsum(
        "jhd,jhe->hde", weighted_keys, value_rows, preferred_element_type=jnp.float32
    )
    return (
        (intra_numer, intra_denom, row_peak.T, decay_sum),
        (shard_decay, local_memory, local_normal, local_peak),
    )


def combine(earlier, latter):
    running_maximum = jnp.maximum(earlier[3] + latter[0], latter[3])
    prior_scale = jnp.exp(earlier[3] + latter[0] - running_maximum)
    local_scale = jnp.exp(latter[3] - running_maximum)
    memory = earlier[1] * prior_scale[:, None, None] + latter[1] * local_scale[:, None, None]
    normal = earlier[2] * prior_scale[:, None] + latter[2] * local_scale[:, None]
    return (earlier[0] + latter[0], memory, normal, running_maximum)


def empty_state(heads, peak_value):
    return (
        jnp.zeros((heads,), jnp.float32),
        jnp.zeros((heads, DK, DH), jnp.float32),
        jnp.zeros((heads, DK), jnp.float32),
        jnp.full((heads,), peak_value, jnp.float32),
    )


def readout(queries, pieces, carried):
    intra_numer, intra_denom, row_peak, decay_sum = pieces
    score_scale = DK ** (-0.5)
    prior = decay_sum + carried[3][None, :]
    running_maximum = jnp.maximum(prior, row_peak)
    prior_scale = jnp.exp(prior - running_maximum)
    local_scale = jnp.exp(row_peak - running_maximum)
    memory_read = carried[1].astype(jnp.bfloat16)
    from_memory = (
        jnp.einsum("thd,hde->the", queries, memory_read, preferred_element_type=jnp.float32)
        * score_scale
    )
    from_normal = (
        jnp.einsum(
            "thd,hd->th", queries.astype(jnp.float32), carried[2], precision=lax.Precision.HIGHEST
        )
        * score_scale
    )
    numerator = prior_scale[:, :, None] * from_memory + local_scale[:, :, None] * intra_numer
    denominator = prior_scale * from_normal + local_scale * intra_denom
    floor_value = jnp.maximum(jnp.abs(denominator), 1.0)
    hidden = (numerator / floor_value[:, :, None]).astype(jnp.bfloat16)
    return hidden.reshape(hidden.shape[0], hidden.shape[1] * DH)


def split_heads(rows, width):
    return rows.reshape(rows.shape[0], rows.shape[1] // width, width)


def per_device(queries, key_rows, value_rows, input_gate, forget_gate, out_weight):
    heads = input_gate.shape[1]
    query_heads = split_heads(queries, DK)
    pieces, summary = local_terms(
        query_heads, split_heads(key_rows, DK), split_heads(value_rows, DH), input_gate, forget_gate
    )
    prefix = entering(summary, "seq", combine, empty_state(heads, -1e30))
    carried = combine(empty_state(heads, 0.0), prefix)
    hidden = readout(query_heads, pieces, carried)
    partial_contributions = jnp.dot(
        hidden,
        lax.all_gather(out_weight, "seq", axis=1, tiled=True),
        preferred_element_type=jnp.float32,
    )
    return lax.psum_scatter(
        partial_contributions.astype(jnp.bfloat16), "head", scatter_dimension=1, tiled=True
    )


def solution(mesh):
    in_specs = (
        P("seq", "head"),
        P("seq", "head"),
        P("seq", "head"),
        P("seq", "head"),
        P("seq", "head"),
        P("head", "seq"),
    )
    out_specs = P("seq", "head")
    return jax.shard_map(
        per_device, mesh=mesh, in_specs=in_specs, out_specs=out_specs, check_vma=False
    )
```

profile of v0, /device:TPU:32, one launch (start us, length us, event | category | flops | bytes accessed | tf_op | source)
XLA Modules:
  0.0 594.8 jit_solution(12063925799830107454)
XLA Ops:
  6.5 0.8 fusion.19
  7.3 0.6 reduce-window.6
  8.6 1.5 copy.48
  10.6 1.4 fusion.11
  12.1 0.7 all-gather.6.cloned.1.call-update
  13.0 0.3 copy.46
  13.4 1.2 multiply_reduce_fusion
  14.6 0.6 dynamic-slice
  16.1 138.9 %all-reduce = f32[128]{0:T(128)S(1)} all-reduce(f32[128]{0:T(128)S(1)} %dynamic-update-slice), channel_id=2, replica_groups=mesh['seq'=64,'head'=4] {'seq'}, use_global_device_ids=true, to_apply=%add | all-reduce | flops 128 | bytes 1024
  155.1 1.3 copy.49
  156.4 82.3 %all-gather.2 = f32[64,1,2]{2,1,0:T(1,128)S(1)} all-gather(f32[1,1,2]{2,1,0:T(1,128)S(1)} %bitcast.130), channel_id=1, replica_groups=mesh['seq'=64,'head'=4] {'seq'}, dimensions={0}, use_global_device_ids=true | all-gather | bytes 520 | tf_op jit(solution)/shard_map/all_gather | solution.py:12
  238.7 77.0 %all_gather.27 = f32[64,2,256]{2,1,0:T(2,128)S(1)} all-gather(f32[1,2,256]{2,1,0:T(2,128)S(1)} %all_gather.26), channel_id=1, replica_groups=mesh['seq'=64,'head'=4] {'seq'}, dimensions={0}, use_global_device_ids=true | all-gather | bytes 133120 | tf_op jit(solution)/shard_map/all_gather | solution.py:12
  315.8 0.4 fusion.10
  316.2 2.1 convert_reduce_fusion
  318.3 63.4 %all-gather.8.cloned.1.call-done = f32[128,256,512]{2,1,0:T(8,128)} async-done(((f32[2,256,512]{2,1,0:T(8,128)}), f32[128,256,512]{2,1,0:T(8,128)}) %all-gather.8.cloned.1.call-update) | async-done | bytes 67108880 | tf_op jit(solution)/shard_map/all_gather | solution.py:12
  381.9 3.7 while.16
  382.0 1.7 fusion.41
  383.9 1.7 fusion.41
  385.8 0.3 fusion.23
  386.3 0.6 fusion.12
  387.1 0.8 fusion.9
  387.8 108.6 %all-gather.6.cloned.1.call-done = bf16[1024,4096]{0,1:T(8,128)(2,1)} async-done(((bf16[1024,64]{0,1:T(8,128)(2,1)}), bf16[1024,4096]{0,1:T(8,128)(2,1)}) %all-gather.6.cloned.1.call-update) | async-done | bytes 8388624 | tf_op jit(solution)/shard_map/all_gather | solution.py:115
  496.5 9.6 %convolution_convert_fusion = bf16[512,4096]{1,0:T(8,128)(2,1)} fusion(bf16[512,1024]{0,1:T(8,128)(2,1)S(1)} %bitcast.131, bf16[1024,4096]{0,1:T(8,128)(2,1)} %all-gather.6.cloned.1.call-done), kind=kOutput, calls=%fused_computation.13 | convolution fusion | flops 4297064448 | bytes 13631488 | tf_op jit(solution)/shard_map/dot_general | solution.py:113
  506.1 82.1 %reduce-scatter.2.cloned.1.call-done = bf16[512,1024]{1,0:T(8,128)(2,1)} async-done(((bf16[512,4096]{1,0:T(8,128)(2,1)}), bf16[512,1024]{1,0:T(8,128)(2,1)}) %reduce-scatter.2.cloned.1.call-update) | async-done | bytes 1048592 | tf_op jit(solution)/shard_map/reduce_scatter | solution.py:118
  (47 shorter events, 2.7 us)
Async XLA Ops:
  6.5 3.5 copy-start.2
  6.5 3.8 copy-start.3
  6.5 375.2 %all-gather.8.cloned.1.call-start = ((), (), s32[]{:S(2)}) async-start(), calls=%async_computation.3 | async-start | bytes 68157440 | tf_op jit(solution)/shard_map/all_gather | solution.py:12
  10.3 2.6 copy-start
  12.0 484.4 %all-gather.6.cloned.1.call-start = ((), (), s32[]{:S(2)}) async-start(), calls=%async_computation.1 | async-start | bytes 8519680 | tf_op jit(solution)/shard_map/all_gather | solution.py:115
  12.8 575.4 %reduce-scatter.2.cloned.1.call-start = ((), (), s32[]{:S(2)}) async-start(), calls=%async_computation.2 | async-start | bytes 5242880 | tf_op jit(solution)/shard_map/reduce_scatter | solution.py:118
  13.0 1.6 copy-start.4
  13.3 302.9 %copy-start.1 = (bf16[512,512]{0,1:T(8,128)(2,1)S(1)}, bf16[512,512]{0,1:T(8,128)(2,1)}, u32[]{:S(2)}) copy-start(bf16[512,512]{0,1:T(8,128)(2,1)} %copy-done) | copy-start | bytes 1572868
  385.8 1.2 copy-start.5
Sparse Core Ops, SparseCore 0:
  12.2 369.5 all-gather.7
  383.6 112.7 all-gather.5
  506.2 81.9 reduce-scatter.1
where the time goes:
time: 602 us; the launch traced here: 595 us
  blocking collectives  298 us (50%)
  waiting for transfers between devices  255 us (42%)
  matrix products  14.9 us (2%)
  between operations  13.9 us (2%)
  other arithmetic  7.58 us (1%)
    all_gather x2, blocking collectives, entering(): gathered = jax.tree.map(lambda a: lax.all_gather(a, axis), part)  159 us
    unnamed x1, blocking collectives  139 us
    all_gather x1, waiting for transfers between devices, per_device(): lax.all_gather(out_weight, 'seq', axis=1, tiled=True)  109 us
    reduce_scatter x1, waiting for transfers between devices, per_device(): lax.psum_scatter(partial_contributions.astype(jnp.bfloat16), 'head', scat...  82.1 us
    all_gather x1, waiting for transfers between devices, entering(): gathered = jax.tree.map(lambda a: lax.all_gather(a, axis), part)  63.4 us
  transfers between devices with their start and end apart: 3, of which 3 were waited for; matrix products, arithmetic and copies ran while one was open for 2% of the time, Pallas kernels for 0%

commit v1 on v0

v1 whole, which is shorter than its diff:
```python
import jax
import jax.numpy as jnp
from jax import lax
from jax.experimental import pallas as pl
from jax.experimental.pallas import tpu as pltpu
from jax.sharding import Mesh, PartitionSpec as P

DH = 512
DK = 256
T = 512
BLOCKS = 64
SLICE = 8
EXT = DH + 128
SEQ = ("x", "y", "z", "c")
CHUNKS = 4
F32 = jnp.float32
BF16 = jnp.bfloat16
SCALE = DK ** (-0.5)
LOWEST = -1e30
HBM = pltpu.MemorySpace.HBM


def split3(a):
    hi = a.astype(BF16).astype(F32)
    rest = a - hi
    mid = rest.astype(BF16).astype(F32)
    return hi, mid, rest - mid


def lanes(shape):
    return lax.broadcasted_iota(jnp.int32, shape, len(shape) - 1)


def rows(shape):
    return lax.broadcasted_iota(jnp.int32, shape, 0)


def place(columns, shape):
    lane = lanes(shape)
    out = jnp.zeros(shape, F32)
    for i, column in enumerate(columns):
        out = jnp.where(lane == i, column, out)
    return out


def pick(tile, first, count):
    lane = lanes(tile.shape)
    keep = (lane >= first) & (lane < first + count)
    return jnp.sum(jnp.where(keep, tile, 0.0), axis=1, keepdims=True)


def running_sum(a):
    width = a.shape[1]
    lane = lanes(a.shape)
    step = 1
    while step < width:
        a = a + jnp.where(lane >= step, pltpu.roll(a, step, 1), 0.0)
        step *= 2
    return a


def suffix_sum(a):
    width = a.shape[1]
    lane = lanes(a.shape)
    step = 1
    while step < width:
        a = a + jnp.where(lane < width - step, pltpu.roll(a, width - step, 1), 0.0)
        step *= 2
    return a


def decay_rows(forget):
    return running_sum(jnp.minimum(forget, 0.0) - jnp.log1p(jnp.exp(-jnp.abs(forget))))


def to_columns(tile):
    full = jnp.concatenate([tile, jnp.zeros((120, tile.shape[1]), F32)], axis=0)
    return full.T


def summary_kernel(k_ref, v_ref, ig_ref, fg_ref, out_ref):
    decay = decay_rows(fg_ref[...])
    total = decay[:, T - 1 : T]
    source = total - decay + ig_ref[...]
    peak = jnp.max(source, axis=1, keepdims=True)
    scale = jnp.exp(source - peak)
    for h in range(2):
        keys = k_ref[:, h * DK : (h + 1) * DK].astype(F32).T
        scaled = keys * scale[h : h + 1]
        normal = jnp.sum(scaled, axis=1, keepdims=True)
        memory = jnp.dot(
            scaled.astype(BF16), v_ref[:, h * DH : (h + 1) * DH], preferred_element_type=F32
        )
        held = slice(h * DK, (h + 1) * DK)
        out_ref[held, :DH] = memory.astype(BF16)
        ones = jnp.ones((DK, 1), F32)
        parts = split3(normal)
        parts += split3(ones * jnp.maximum(total[h : h + 1], LOWEST))
        parts += split3(ones * peak[h : h + 1])
        out_ref[held, DH:] = place(parts, (DK, 128)).astype(BF16)


def combine_kernel(in_ref, out_ref):
    size = BLOCKS * SLICE
    tile = in_ref[:, DH:].astype(F32)
    across = tile.T
    decay = (across[3:4] + across[4:5]) + across[5:6]
    peak = (across[6:7] + across[7:8]) + across[8:9]
    shape = (BLOCKS, size)
    block, lane = rows(shape), lanes(shape)
    source = lax.shift_right_logical(lane, 3)
    earlier = source < block
    head_lane = (lane & (SLICE - 1)) == 0
    held = jnp.where(earlier & head_lane, decay, 0.0)
    total = jnp.sum(held, axis=1, keepdims=True)
    after = suffix_sum(jnp.where(lane < size - 1, pltpu.roll(held, size - 1, 1), 0.0))
    weight = peak + after
    running = jnp.maximum(
        total, jnp.max(jnp.where(earlier, weight, LOWEST), axis=1, keepdims=True)
    )
    factor = jnp.where(earlier, jnp.exp(jnp.minimum(weight - running, 0.0)), 0.0)
    spread = (
        lax.shift_right_logical(rows((size, BLOCKS)), 3) == lanes((size, BLOCKS))
    ).astype(BF16)
    same = (rows((size, size)) & (SLICE - 1)) == (lanes((size, size)) & (SLICE - 1))
    memory = jnp.zeros((size, DH), F32)
    scalars = jnp.zeros((size, 128), F32)
    for i, part in enumerate(split3(factor)):
        wide = jnp.dot(spread, part.astype(BF16), preferred_element_type=F32)
        wide = jnp.where(same, wide, 0.0).astype(BF16)
        scalars += jnp.dot(wide, in_ref[:, DH:], preferred_element_type=F32)
        if i < 2:
            memory += jnp.dot(wide, in_ref[:, :DH], preferred_element_type=F32)
    out_ref[:, :DH] = memory.astype(BF16)
    peaks = place(split3(running), (BLOCKS, 128)).astype(BF16)
    peaks = jnp.dot(spread, peaks, preferred_element_type=F32)
    normal = pick(scalars, 0, 3)
    entries = split3(normal) + split3(pick(peaks, 0, 3))
    out_ref[:, DH:] = place(entries, (size, 128)).astype(BF16)


def intra_kernel(q_ref, k_ref, v_ref, ig_ref, fg_ref, numer_ref, terms_ref):
    decay = decay_rows(fg_ref[...])
    offset = ig_ref[...]
    columns = to_columns(jnp.concatenate([decay, jnp.zeros((6, T), F32)], axis=0))
    causal = rows((T, T)) >= lanes((T, T))
    terms = []
    for h in range(2):
        scores = (
            lax.dot_general(
                q_ref[:, h * DK : (h + 1) * DK],
                k_ref[:, h * DK : (h + 1) * DK],
                (((1,), (1,)), ((), ())),
                preferred_element_type=F32,
            )
            * SCALE
        )
        own = columns[:, h : h + 1]
        logits = own - decay[h : h + 1] + offset[h : h + 1]
        logits = jnp.where(causal, logits, -jnp.inf)
        row_peak = jnp.max(logits, axis=1, keepdims=True)
        weights = (jnp.exp(logits - row_peak) * scores).astype(BF16)
        numer_ref[:, h * DH : (h + 1) * DH] = jnp.dot(
            weights, v_ref[:, h * DH : (h + 1) * DH], preferred_element_type=F32
        )
        terms += [own, row_peak, jnp.sum(weights.astype(F32), axis=1, keepdims=True)]
    terms_ref[...] = place(terms, (T, 128))


def readout_kernel(q_ref, m_ref, numer_ref, terms_ref, out_ref):
    terms = terms_ref[...]
    for h in range(2):
        own, row_peak, denom = (terms[:, 3 * h + i : 3 * h + i + 1] for i in range(3))
        held = slice(h * DK, (h + 1) * DK)
        peak = pick(m_ref[h * DK : h * DK + 8, DH:].astype(F32), 3, 3)[:1]
        read = jnp.dot(q_ref[:, held], m_ref[held], preferred_element_type=F32) * SCALE
        prior = own + peak
        ceiling = jnp.maximum(prior, row_peak)
        prior_scale = jnp.exp(prior - ceiling)
        local_scale = jnp.exp(row_peak - ceiling)
        columns = slice(h * DH, (h + 1) * DH)
        numerator = prior_scale * read[:, :DH] + local_scale * numer_ref[:, columns]
        denominator = prior_scale * pick(read[:, DH:], 0, 3) + local_scale * denom
        floor_value = jnp.maximum(jnp.abs(denominator), 1.0)
        out_ref[:, columns] = (numerator / floor_value).astype(BF16)


def project_kernel(where_ref, own_ref, other_ref, *refs):
    pieces, (send_ref, keep_ref, held, sems) = refs[:8], refs[8:]
    x, c = where_ref[0], where_ref[1]
    copies = []
    for half in range(2):
        for r in range(4):
            dst = held.at[(c + half) & 1, (x + r) & 3]
            copy = pltpu.make_async_copy(pieces[half * 4 + r], dst, sems.at[half * 4 + r])
            copy.start()
            copies.append(copy)
    for copy in copies:
        copy.wait()

    def part(rows_ref, half, block):
        return lax.dot_general(
            rows_ref[:, half * 512 : (half + 1) * 512],
            held[half, block],
            (((1,), (1,)), ((), ())),
            preferred_element_type=F32,
        )

    def total(own_block, other_block):
        out = part(own_ref, 0, own_block) + part(own_ref, 1, own_block)
        return out + part(other_ref, 0, other_block) + part(other_ref, 1, other_block)

    send_ref[...] = total(where_ref[2], where_ref[3]).astype(BF16)
    keep_ref[...] = total(where_ref[4], where_ref[5])


def call(kernel, out_shape, *operands, **kwargs):
    return pl.pallas_call(
        kernel,
        out_shape=out_shape,
        compiler_params=pltpu.CompilerParams(vmem_limit_bytes=48 * 1024 * 1024),
        **kwargs,
    )(*operands)


def shape(rows_, columns, dtype):
    return jax.ShapeDtypeStruct((rows_, columns), dtype)


def exchange_blocks(a):
    pairs = []
    for x in range(4):
        for h in range(4):
            outer = h in (0, 3)
            if outer and x in (1, 2):
                to = ({1: 0, 2: 3}[x], h ^ 1)
            elif not outer and x in (0, 3):
                to = ({0: 1, 3: 2}[x], h ^ 1)
            else:
                to = (x, h)
            pairs.append((x * 4 + h, to[0] * 4 + to[1]))
    return lax.ppermute(a, ("x", "h"), pairs)


def shifted(a, axis, by, size=4):
    return lax.ppermute(a, axis, [((i + by) % size, i) for i in range(size)])


def weight_pieces(out_weight):
    y, z, c = (lax.axis_index(n) for n in ("y", "z", "c"))
    columns = exchange_blocks(out_weight.T)
    low, high = columns[:, :512], columns[:, 512:]
    mine = jnp.where(c == 0, low, high)
    others = jnp.where(c == 0, high, low)
    place_of = [(zz, cc) for zz in range(2) for cc in range(2)]

    def swap(a, dz, dc):
        moves = [
            (i, place_of.index(((zz + dz) % 2, (cc + dc) % 2))) for i, (zz, cc) in enumerate(place_of)
        ]
        return lax.ppermute(a, ("z", "c"), moves)

    near = swap(others, 0, 1)
    far_same = swap(mine, 1, 0)
    far_other = swap(others, 1, 1)
    here = jnp.where(c == 0, jnp.concatenate([mine, near]), jnp.concatenate([near, mine]))
    there = jnp.where(
        c == 0, jnp.concatenate([far_same, far_other]), jnp.concatenate([far_other, far_same])
    )
    group = jnp.where(z == 0, jnp.concatenate([here, there]), jnp.concatenate([there, here]))
    ring = [group] + [shifted(group, "y", by) for by in (1, 2, 3)]
    ring = jnp.stack(ring + ring[:3])
    plane = lax.dynamic_slice_in_dim(ring, (4 - y) % 4, 4, 0).reshape(1024, 512)
    first = [plane] + [shifted(plane, "x", by) for by in (1, 2, 3)]
    second = [lax.ppermute(a, "c", [(0, 1), (1, 0)]) for a in first]
    return first + second


def per_device(queries, key_rows, value_rows, input_gate, forget_gate, out_weight):
    pieces = weight_pieces(out_weight)
    gate_in, gate_forget = input_gate.T, forget_gate.T
    summary = call(
        summary_kernel, shape(T, EXT, BF16), key_rows, value_rows, gate_in, gate_forget
    )
    grouped = lax.all_to_all(summary.reshape(BLOCKS, SLICE, EXT), SEQ, 0, 0, tiled=True)
    entering = call(combine_kernel, shape(T, EXT, BF16), grouped.reshape(T, EXT))
    carried = lax.all_to_all(entering.reshape(BLOCKS, SLICE, EXT), SEQ, 0, 0, tiled=True)
    carried = carried.reshape(T, EXT)
    numer, terms = call(
        intra_kernel,
        (shape(T, 2 * DH, F32), shape(T, 128, F32)),
        queries, key_rows, value_rows, gate_in, gate_forget,
    )

    x, c, h = (lax.axis_index(n) for n in ("x", "c", "h"))
    outer = (h == 0) | (h == 3)
    keep = (h >= 2).astype(jnp.int32)

    def block(half, is_outer):
        return jnp.where(is_outer, 3 * half, 1 + half)

    where = jnp.stack(
        [x, c, block(1 - keep, outer), block(1 - keep, ~outer), block(keep, outer), block(keep, ~outer)]
    ).astype(jnp.int32)
    size = T // CHUNKS
    any_spec = pl.BlockSpec(memory_space=pl.ANY)
    vmem = pl.BlockSpec(memory_space=pltpu.VMEM)
    outs = []
    for i in range(CHUNKS):
        rows_of = lambda a: lax.slice_in_dim(a, i * size, (i + 1) * size, axis=0)
        hidden = call(
            readout_kernel, shape(size, 2 * DH, BF16),
            rows_of(queries), carried, rows_of(numer), rows_of(terms),
        )
        other = lax.ppermute(hidden, "h", [(j, j ^ 1) for j in range(4)])
        send, kept = call(
            project_kernel,
            (shape(size, 1024, BF16), shape(size, 1024, F32)),
            where, hidden, other, *pieces,
            in_specs=[pl.BlockSpec(memory_space=pltpu.SMEM), vmem, vmem] + [any_spec] * 8,
            out_specs=(vmem, vmem),
            scratch_shapes=[
                pltpu.VMEM((2, 4, 1024, 512), BF16),
                pltpu.SemaphoreType.DMA((8,)),
            ],
        )
        arrived = lax.ppermute(send, "h", [(j, 3 - j) for j in range(4)])
        outs.append((kept + arrived.astype(F32)).astype(BF16))
    return jnp.concatenate(outs, axis=0)


def solution(mesh):
    fine = Mesh(mesh.devices.reshape(4, 4, 2, 2, 4), SEQ + ("h",))
    both = P(SEQ, "h")
    return jax.shard_map(
        per_device,
        mesh=fine,
        in_specs=(both,) * 5 + (P("h", SEQ),),
        out_specs=both,
        check_vma=False,
    )
```

time: 602 us -> 218 us (0.36)
  blocking collectives: 298 us -> 0 us
  waiting for transfers between devices: 255 us -> 103 us
  starting transfers between devices: 0.08 us -> 54.8 us
  Pallas kernels: 0 us -> 40.7 us
  matrix products: 14.9 us -> 0 us
  between operations: 13.9 us -> 0.3 us
  local copies, waits for them, and re-layouts: 5.15 us -> 16.2 us
  other arithmetic: 7.58 us -> 1.51 us
    all_gather x2 -> x0, waiting for transfers between devices: 172 us -> none  [the longest x1 109 us: per_device(): lax.all_gather(out_weight, 'seq', axis=1, tiled=True)]
    all_gather x2 -> x0, blocking collectives: 159 us -> none  [entering(): gathered = jax.tree.map(lambda a: lax.all_gather(a, axis), part)]
    unnamed x1 -> x0, blocking collectives: 139 us -> none
    ppermute x0 -> x22, waiting for transfers between devices: none -> 103 us  [the longest x6 58.4 us: shifted(): return lax.ppermute(a, axis, [((i + by) % size, i) for i in range(size)])]
    reduce_scatter x1 -> x0, waiting for transfers between devices: 82.1 us -> none  [per_device(): lax.psum_scatter(partial_contributions.astype(jnp.bfloat16), 'head', scat...]
    pallas_call x0 -> x11, Pallas kernels: none -> 40.7 us  [call(): pl.pallas_call(kernel, out_shape=out_shape, compiler_params=pltpu.Compile...]
    ppermute x0 -> x22, starting transfers between devices: none -> 32.6 us  [the longest x4 11 us: per_device(): arrived = lax.ppermute(send, 'h', [(j, 3 - j) for j in range(4)])]
    all_to_all x0 -> x2, starting transfers between devices: none -> 22.2 us  [the longest x1 16.3 us: per_device(): lax.all_to_all(summary.reshape(BLOCKS, SLICE, EXT), SEQ, 0, 0, tiled=True)]
  transfers between devices with their start and end apart: 3 -> 24, of which waited for: 3 -> 10; matrix products, arithmetic and copies ran while one was open for 2% -> 2% of each run, Pallas kernels for 0% -> 19%
where the time goes in v1:
time: 218 us; the launch traced here: 217 us
  waiting for transfers between devices  103 us (47%)
  starting transfers between devices  54.8 us (25%)
  Pallas kernels  40.7 us (19%)
  local copies, waits for them, and re-layouts  16.2 us (7%)
    ppermute x6, waiting for transfers between devices, shifted(): return lax.ppermute(a, axis, [((i + by) % size, i) for i in range(size)])  58.4 us
    pallas_call x11, Pallas kernels, call(): pl.pallas_call(kernel, out_shape=out_shape, compiler_params=pltpu.Compile...  40.7 us
    ppermute x4, waiting for transfers between devices, per_device(): arrived = lax.ppermute(send, 'h', [(j, 3 - j) for j in range(4)])  25.1 us
    all_to_all x1, starting transfers between devices, per_device(): lax.all_to_all(summary.reshape(BLOCKS, SLICE, EXT), SEQ, 0, 0, tiled=True)  16.3 us
    ppermute x4, waiting for transfers between devices, per_device(): other = lax.ppermute(hidden, 'h', [(j, j ^ 1) for j in range(4)])  15 us
    unnamed x42, local copies, waits for them, and re-layouts  13.2 us
    ppermute x4, starting transfers between devices, per_device(): arrived = lax.ppermute(send, 'h', [(j, 3 - j) for j in range(4)])  11 us
    ppermute x6, starting transfers between devices, shifted(): return lax.ppermute(a, axis, [((i + by) % size, i) for i in range(size)])  10.5 us
  transfers between devices with their start and end apart: 24, of which 10 were waited for; matrix products, arithmetic and copies ran while one was open for 2% of the time, Pallas kernels for 19%

profile of v1, /device:TPU:32, one launch (start us, length us, event | category | flops | bytes accessed | tf_op | source)
XLA Modules:
  0.0 216.5 jit_solution(13607346021588062913)
XLA Ops:
  4.0 3.0 %collective-permute-done.4 = bf16[64,512]{1,0:T(8,128)(2,1)S(1)} collective-permute-done((bf16[64,512]{1,0:T(8,128)(2,1)S(1)}, bf16[64,512]{1,0:T(8,128)(2,1)S(1)}, u32[]{:S(2)}, u32[]{:S(2)}) %collective-permute-start.4) | collective-permute-done | bytes 65568 | tf_op jit(solution)/shard_map/ppermute | solution.py:261
  8.5 2.4 %collective-permute-start.5 = (bf16[256,512]{1,0:T(8,128)(2,1)S(1)}, bf16[256,512]{1,0:T(8,128)(2,1)S(1)}, u32[]{:S(2)}, u32[]{:S(2)}) collective-permute-start(bf16[256,512]{1,0:T(8,128)(2,1)S(1)} %maximum_select_fusion.1), channel_id=1, source_target_pairs={{16,0},{32,16},{48,32},{0,48},{17,1},{33,17},{49,33},{1,49},{18,2}... | collective-permute-start | bytes 786440 | tf_op jit(solution)/shard_map/ppermute | solution.py:246
  15.3 16.3 %all-to-all-start = ((bf16[64,8,640]{2,1,0:T(8,128)(2,1)}), bf16[64,8,640]{2,1,0:T(8,128)(2,1)}, u32[]{:S(2)}, u32[]{:S(2)}) async-start(bf16[64,8,640]{2,1,0:T(8,128)(2,1)} %bitcast.8), calls=%async_computation | async-start | bytes 1310720 | tf_op jit(solution)/shard_map/all_to_all | solution.py:285
  31.7 3.1 %collective-permute-start.6 = (bf16[256,512]{1,0:T(8,128)(2,1)S(1)}, bf16[256,512]{1,0:T(8,128)(2,1)S(1)}, u32[]{:S(2)}, u32[]{:S(2)}) collective-permute-start(bf16[256,512]{1,0:T(8,128)(2,1)S(1)} %maximum_select_fusion.1), channel_id=1, source_target_pairs={{32,0},{48,16},{0,32},{16,48},{33,1},{49,17},{1,33},{17,49},{34,2}... | collective-permute-start | bytes 786440 | tf_op jit(solution)/shard_map/ppermute | solution.py:246
  35.4 13.3 %collective-permute-done.6 = bf16[256,512]{1,0:T(8,128)(2,1)S(1)} collective-permute-done((bf16[256,512]{1,0:T(8,128)(2,1)S(1)}, bf16[256,512]{1,0:T(8,128)(2,1)S(1)}, u32[]{:S(2)}, u32[]{:S(2)}) %collective-permute-start.6) | collective-permute-done | bytes 262176 | tf_op jit(solution)/shard_map/ppermute | solution.py:246
  48.8 5.1 %collective-permute-done.7 = bf16[256,512]{1,0:T(8,128)(2,1)S(1)} collective-permute-done((bf16[256,512]{1,0:T(8,128)(2,1)S(1)}, bf16[256,512]{1,0:T(8,128)(2,1)S(1)}, u32[]{:S(2)}, u32[]{:S(2)}) %collective-permute-start.7) | collective-permute-done | bytes 262176 | tf_op jit(solution)/shard_map/ppermute | solution.py:246
  54.1 2.6 %collective-permute-start.8 = (bf16[1024,512]{1,0:T(8,128)(2,1)S(1)}, bf16[1024,512]{1,0:T(8,128)(2,1)S(1)}, u32[]{:S(2)}, u32[]{:S(2)}) collective-permute-start(bf16[1024,512]{1,0:T(8,128)(2,1)S(1)} %bitcast.24), channel_id=1, source_target_pairs={{64,0},{128,64},{192,128},{0,192},{65,1},{129,65},{193,129},{1,193... | collective-permute-start | bytes 3145736 | tf_op jit(solution)/shard_map/ppermute | solution.py:246
  58.6 3.5 %shard_map.65 = bf16[512,640]{1,0:T(8,128)(2,1)S(1)} custom-call(bf16[512,640]{1,0:T(8,128)(2,1)} %bitcast.9.in_ref), custom_call_target="tpu_custom_call" | custom-call | tf_op jit(solution)/shard_map/pallas_call | solution.py:218
  63.0 5.9 %all-to-all-start.1 = ((bf16[64,8,640]{2,1,0:T(8,128)(2,1)}), bf16[64,8,640]{2,1,0:T(8,128)(2,1)}, u32[]{:S(2)}, u32[]{:S(2)}) async-start(bf16[64,8,640]{2,1,0:T(8,128)(2,1)} %bitcast.32), calls=%async_computation.1 | async-start | bytes 1310720 | tf_op jit(solution)/shard_map/all_to_all | solution.py:287
  69.1 38.4 %collective-permute-done.8.refs_1_ = bf16[1024,512]{1,0:T(8,128)(2,1)S(1)} collective-permute-done((bf16[1024,512]{1,0:T(8,128)(2,1)S(1)}, bf16[1024,512]{1,0:T(8,128)(2,1)S(1)}, u32[]{:S(2)}, u32[]{:S(2)}) %collective-permute-start.8) | collective-permute-done | bytes 1048608 | tf_op jit(solution)/shard_map/ppermute | solution.py:246
  112.9 2.1 shard_map.66
  119.0 2.4 %shard_map.73.own_ref = bf16[128,1024]{1,0:T(8,128)(2,1)} custom-call(bf16[128,512]{1,0:T(8,128)(2,1)S(1)} %get-tuple-element.31.q_ref, bf16[512,640]{1,0:T(8,128)(2,1)} %bitcast.11.m_ref, f32[128,1024]{1,0:T(8,128)S(1)} %copy-done.9, f32[128,128]{1,0:T(8,128)S(1)} %get-tuple-element.34.terms_ref), custom_call_target="tpu_custom_call" | custom-call | tf_op jit(solution)/shard_map/pallas_call | solution.py:218
  121.5 3.3 %collective-permute-start.20 = (bf16[128,1024]{1,0:T(8,128)(2,1)}, bf16[128,1024]{1,0:T(8,128)(2,1)}, u32[]{:S(2)}, u32[]{:S(2)}) collective-permute-start(bf16[128,1024]{1,0:T(8,128)(2,1)} %shard_map.73.own_ref), channel_id=1, source_target_pairs={{0,1},{1,0},{2,3},{3,2},{4,5},{5,4},{6,7},{7,6},{8,9},{9,8},{10,11... | collective-permute-start | bytes 786440 | tf_op jit(solution)/shard_map/ppermute | solution.py:315
  133.0 3.0 %collective-permute-start.16 = (bf16[128,1024]{1,0:T(8,128)(2,1)S(1)}, bf16[128,1024]{1,0:T(8,128)(2,1)S(1)}, u32[]{:S(2)}, u32[]{:S(2)}) collective-permute-start(bf16[128,1024]{1,0:T(8,128)(2,1)S(1)} %shard_map.69.own_ref), channel_id=1, source_target_pairs={{0,1},{1,0},{2,3},{3,2},{4,5},{5,4},{6,7},{7,6},{8,9},{9,8},{10,11... | collective-permute-start | bytes 786440 | tf_op jit(solution)/shard_map/ppermute | solution.py:315
  138.7 15.0 %collective-permute-done.20.other_ref = bf16[128,1024]{1,0:T(8,128)(2,1)} collective-permute-done((bf16[128,1024]{1,0:T(8,128)(2,1)}, bf16[128,1024]{1,0:T(8,128)(2,1)}, u32[]{:S(2)}, u32[]{:S(2)}) %collective-permute-start.20) | collective-permute-done | bytes 262176 | tf_op jit(solution)/shard_map/ppermute | solution.py:315
  153.7 6.6 %shard_map.74 = (bf16[128,1024]{1,0:T(8,128)(2,1)S(1)}, f32[128,1024]{1,0:T(8,128)S(1)}) custom-call(s32[6]{0:T(128)S(1)} %stack.43.where_ref, bf16[128,1024]{1,0:T(8,128)(2,1)} %shard_map.73.own_ref, bf16[128,1024]{1,0:T(8,128)(2,1)} %collective-permute-done.20.other_ref, bf16[1024,512]{1,0:T(8,128)(2,1)S(1)} %bitcast.28, ...), custom_call_target="tpu_custom_call" | custom-call | tf_op jit(solution)/shard_map/pallas_call | solution.py:218
  160.3 6.3 %collective-permute-start.21 = (bf16[128,1024]{1,0:T(8,128)(2,1)S(1)}, bf16[128,1024]{1,0:T(8,128)(2,1)S(1)}, u32[]{:S(2)}, u32[]{:S(2)}) collective-permute-start(bf16[128,1024]{1,0:T(8,128)(2,1)S(1)} %get-tuple-element.24), channel_id=1, source_target_pairs={{0,3},{1,2},{2,1},{3,0},{4,7},{5,6},{6,5},{7,4},{8,11},{9,10},{10,... | collective-permute-start | bytes 786440 | tf_op jit(solution)/shard_map/ppermute | solution.py:327
  166.6 6.5 %shard_map.72 = (bf16[128,1024]{1,0:T(8,128)(2,1)S(1)}, f32[128,1024]{1,0:T(8,128)S(1)}) custom-call(s32[6]{0:T(128)S(1)} %stack.43.where_ref, bf16[128,1024]{1,0:T(8,128)(2,1)S(1)} %shard_map.71.own_ref, bf16[128,1024]{1,0:T(8,128)(2,1)} %collective-permute-done.18.other_ref, bf16[1024,512]{1,0:T(8,128)(2,1)S(1)} %bitcast.29, ...), custom_call_target="tpu_custom_call" | custom-call | tf_op jit(solution)/shard_map/pallas_call | solution.py:218
  173.3 6.1 %shard_map.70 = (bf16[128,1024]{1,0:T(8,128)(2,1)S(1)}, f32[128,1024]{1,0:T(8,128)S(1)}) custom-call(s32[6]{0:T(128)S(1)} %stack.43.where_ref, bf16[128,1024]{1,0:T(8,128)(2,1)S(1)} %shard_map.69.own_ref, bf16[128,1024]{1,0:T(8,128)(2,1)S(1)} %collective-permute-done.16.other_ref, bf16[1024,512]{1,0:T(8,128)(2,1)S(1)} %bitcast.30, ...), custom_call_target="tpu_custom_call" | custom-call | tf_op jit(solution)/shard_map/pallas_call | solution.py:218
  179.4 4.4 %collective-permute-start.17 = (bf16[128,1024]{1,0:T(8,128)(2,1)S(1)}, bf16[128,1024]{1,0:T(8,128)(2,1)S(1)}, u32[]{:S(2)}, u32[]{:S(2)}) collective-permute-start(bf16[128,1024]{1,0:T(8,128)(2,1)S(1)} %get-tuple-element.20), channel_id=1, source_target_pairs={{0,3},{1,2},{2,1},{3,0},{4,7},{5,6},{6,5},{7,4},{8,11},{9,10},{10,... | collective-permute-start | bytes 786440 | tf_op jit(solution)/shard_map/ppermute | solution.py:327
  183.8 6.1 %shard_map.68 = (bf16[128,1024]{1,0:T(8,128)(2,1)S(1)}, f32[128,1024]{1,0:T(8,128)S(1)}) custom-call(s32[6]{0:T(128)S(1)} %stack.43.where_ref, bf16[128,1024]{1,0:T(8,128)(2,1)S(1)} %shard_map.67.own_ref, bf16[128,1024]{1,0:T(8,128)(2,1)S(1)} %collective-permute-done.other_ref, bf16[1024,512]{1,0:T(8,128)(2,1)S(1)} %bitcast.31, ...), custom_call_target="tpu_custom_call" | custom-call | tf_op jit(solution)/shard_map/pallas_call | solution.py:218
  190.2 14.1 %collective-permute-done.19 = bf16[128,1024]{1,0:T(8,128)(2,1)S(1)} collective-permute-done((bf16[128,1024]{1,0:T(8,128)(2,1)S(1)}, bf16[128,1024]{1,0:T(8,128)(2,1)S(1)}, u32[]{:S(2)}, u32[]{:S(2)}) %collective-permute-start.19) | collective-permute-done | bytes 262176 | tf_op jit(solution)/shard_map/ppermute | solution.py:327
  204.3 5.5 %collective-permute-done.17 = bf16[128,1024]{1,0:T(8,128)(2,1)S(1)} collective-permute-done((bf16[128,1024]{1,0:T(8,128)(2,1)S(1)}, bf16[128,1024]{1,0:T(8,128)(2,1)S(1)}, u32[]{:S(2)}, u32[]{:S(2)}) %collective-permute-start.17) | collective-permute-done | bytes 262176 | tf_op jit(solution)/shard_map/ppermute | solution.py:327
  209.9 5.5 %collective-permute-done.15 = bf16[128,1024]{1,0:T(8,128)(2,1)S(1)} collective-permute-done((bf16[128,1024]{1,0:T(8,128)(2,1)S(1)}, bf16[128,1024]{1,0:T(8,128)(2,1)S(1)}, u32[]{:S(2)}, u32[]{:S(2)}) %collective-permute-start.15) | collective-permute-done | bytes 262176 | tf_op jit(solution)/shard_map/ppermute | solution.py:327
  (94 shorter events, 35.5 us)
Async XLA Ops:
  0.0 1.7 collective-permute-start.1
  1.7 2.3 %collective-permute-start.2 = (bf16[64,512]{1,0:T(8,128)(2,1)S(1)}, bf16[64,512]{1,0:T(8,128)(2,1)S(1)}, u32[]{:S(2)}, u32[]{:S(2)}) collective-permute-start(bf16[64,512]{1,0:T(8,128)(2,1)S(1)} %get-tuple-element.38), channel_id=1, source_target_pairs={{0,4},{4,0},{8,12},{12,8},{1,5},{5,1},{9,13},{13,9},{2,6},{6,2},{1... | collective-permute-start | bytes 196616 | tf_op jit(solution)/shard_map/ppermute | solution.py:261
  1.8 5.2 %collective-permute-start.4 = (bf16[64,512]{1,0:T(8,128)(2,1)S(1)}, bf16[64,512]{1,0:T(8,128)(2,1)S(1)}, u32[]{:S(2)}, u32[]{:S(2)}) collective-permute-start(bf16[64,512]{1,0:T(8,128)(2,1)S(1)} %get-tuple-element.38), channel_id=1, source_target_pairs={{0,12},{4,8},{8,4},{12,0},{1,13},{5,9},{9,5},{13,1},{2,14},{6,10},... | collective-permute-start | bytes 196616 | tf_op jit(solution)/shard_map/ppermute | solution.py:261
  3.8 4.6 %collective-permute-start.3 = (bf16[64,512]{1,0:T(8,128)(2,1)S(1)}, bf16[64,512]{1,0:T(8,128)(2,1)S(1)}, u32[]{:S(2)}, u32[]{:S(2)}) collective-permute-start(bf16[64,512]{1,0:T(8,128)(2,1)S(1)} %get-tuple-element.37), channel_id=1, source_target_pairs={{0,8},{4,12},{8,0},{12,4},{1,9},{5,13},{9,1},{13,5},{2,10},{6,14},... | collective-permute-start | bytes 196616 | tf_op jit(solution)/shard_map/ppermute | solution.py:261
  8.5 26.9 %collective-permute-start.5 = (bf16[256,512]{1,0:T(8,128)(2,1)S(1)}, bf16[256,512]{1,0:T(8,128)(2,1)S(1)}, u32[]{:S(2)}, u32[]{:S(2)}) collective-permute-start(bf16[256,512]{1,0:T(8,128)(2,1)S(1)} %maximum_select_fusion.1), channel_id=1, source_target_pairs={{16,0},{32,16},{48,32},{0,48},{17,1},{33,17},{49,33},{1,49},{18,2}... | collective-permute-start | bytes 786440 | tf_op jit(solution)/shard_map/ppermute | solution.py:246
  15.3 43.2 %all-to-all-start = ((bf16[64,8,640]{2,1,0:T(8,128)(2,1)}), bf16[64,8,640]{2,1,0:T(8,128)(2,1)}, u32[]{:S(2)}, u32[]{:S(2)}) async-start(bf16[64,8,640]{2,1,0:T(8,128)(2,1)} %bitcast.8), calls=%async_computation | async-start | bytes 1310720 | tf_op jit(solution)/shard_map/all_to_all | solution.py:285
  31.7 17.1 %collective-permute-start.6 = (bf16[256,512]{1,0:T(8,128)(2,1)S(1)}, bf16[256,512]{1,0:T(8,128)(2,1)S(1)}, u32[]{:S(2)}, u32[]{:S(2)}) collective-permute-start(bf16[256,512]{1,0:T(8,128)(2,1)S(1)} %maximum_select_fusion.1), channel_id=1, source_target_pairs={{32,0},{48,16},{0,32},{16,48},{33,1},{49,17},{1,33},{17,49},{34,2}... | collective-permute-start | bytes 786440 | tf_op jit(solution)/shard_map/ppermute | solution.py:246
  34.8 19.1 %collective-permute-start.7 = (bf16[256,512]{1,0:T(8,128)(2,1)S(1)}, bf16[256,512]{1,0:T(8,128)(2,1)S(1)}, u32[]{:S(2)}, u32[]{:S(2)}) collective-permute-start(bf16[256,512]{1,0:T(8,128)(2,1)S(1)} %maximum_select_fusion.1), channel_id=1, source_target_pairs={{48,0},{0,16},{16,32},{32,48},{49,1},{1,17},{17,33},{33,49},{50,2}... | collective-permute-start | bytes 786440 | tf_op jit(solution)/shard_map/ppermute | solution.py:246
  54.1 53.4 %collective-permute-start.8 = (bf16[1024,512]{1,0:T(8,128)(2,1)S(1)}, bf16[1024,512]{1,0:T(8,128)(2,1)S(1)}, u32[]{:S(2)}, u32[]{:S(2)}) collective-permute-start(bf16[1024,512]{1,0:T(8,128)(2,1)S(1)} %bitcast.24), channel_id=1, source_target_pairs={{64,0},{128,64},{192,128},{0,192},{65,1},{129,65},{193,129},{1,193... | collective-permute-start | bytes 3145736 | tf_op jit(solution)/shard_map/ppermute | solution.py:246
  56.7 50.8 %collective-permute-start.9 = (bf16[1024,512]{1,0:T(8,128)(2,1)S(1)}, bf16[1024,512]{1,0:T(8,128)(2,1)S(1)}, u32[]{:S(2)}, u32[]{:S(2)}) collective-permute-start(bf16[1024,512]{1,0:T(8,128)(2,1)S(1)} %bitcast.25), channel_id=1, source_target_pairs={{128,0},{192,64},{0,128},{64,192},{129,1},{193,65},{1,129},{65,193... | collective-permute-start | bytes 3145736 | tf_op jit(solution)/shard_map/ppermute | solution.py:246
  57.8 51.8 %collective-permute-start.10 = (bf16[1024,512]{1,0:T(8,128)(2,1)S(1)}, bf16[1024,512]{1,0:T(8,128)(2,1)}, u32[]{:S(2)}, u32[]{:S(2)}) collective-permute-start(bf16[1024,512]{1,0:T(8,128)(2,1)S(1)} %bitcast.26), channel_id=1, source_target_pairs={{192,0},{0,64},{64,128},{128,192},{193,1},{1,65},{65,129},{129,193... | collective-permute-start | bytes 3145736 | tf_op jit(solution)/shard_map/ppermute | solution.py:246
  63.0 54.9 %all-to-all-start.1 = ((bf16[64,8,640]{2,1,0:T(8,128)(2,1)}), bf16[64,8,640]{2,1,0:T(8,128)(2,1)}, u32[]{:S(2)}, u32[]{:S(2)}) async-start(bf16[64,8,640]{2,1,0:T(8,128)(2,1)} %bitcast.32), calls=%async_computation.1 | async-start | bytes 1310720 | tf_op jit(solution)/shard_map/all_to_all | solution.py:287
  68.9 59.3 %collective-permute-start.11 = (bf16[1024,512]{1,0:T(8,128)(2,1)S(1)}, bf16[1024,512]{1,0:T(8,128)(2,1)}, u32[]{:S(2)}, u32[]{:S(2)}) collective-permute-start(bf16[1024,512]{1,0:T(8,128)(2,1)S(1)} %bitcast.27), channel_id=1, source_target_pairs={{0,4},{4,0},{1,5},{5,1},{2,6},{6,2},{3,7},{7,3},{8,12},{12,8},{9,1... | collective-permute-start | bytes 3145736 | tf_op jit(solution)/shard_map/ppermute | solution.py:275
  107.5 25.5 %collective-permute-start.12 = (bf16[1024,512]{1,0:T(8,128)(2,1)S(1)}, bf16[1024,512]{1,0:T(8,128)(2,1)}, u32[]{:S(2)}, u32[]{:S(2)}) collective-permute-start(bf16[1024,512]{1,0:T(8,128)(2,1)S(1)} %collective-permute-done.8.refs_1_), channel_id=1, source_target_pairs={{0,4},{4,0},{1,5},{5,1},{2,6},{6,2},{3,7},{7,3},{8,12},{12,8},{9,1... | collective-permute-start | bytes 3145736 | tf_op jit(solution)/shard_map/ppermute | solution.py:275
  107.5 31.1 %collective-permute-start.13 = (bf16[1024,512]{1,0:T(8,128)(2,1)S(1)}, bf16[1024,512]{1,0:T(8,128)(2,1)}, u32[]{:S(2)}, u32[]{:S(2)}) collective-permute-start(bf16[1024,512]{1,0:T(8,128)(2,1)S(1)} %collective-permute-done.9.refs_2_), channel_id=1, source_target_pairs={{0,4},{4,0},{1,5},{5,1},{2,6},{6,2},{3,7},{7,3},{8,12},{12,8},{9,1... | collective-permute-start | bytes 3145736 | tf_op jit(solution)/shard_map/ppermute | solution.py:275
  109.6 29.1 %collective-permute-start.14 = (bf16[1024,512]{1,0:T(8,128)(2,1)}, bf16[1024,512]{1,0:T(8,128)(2,1)}, u32[]{:S(2)}, u32[]{:S(2)}) collective-permute-start(bf16[1024,512]{1,0:T(8,128)(2,1)} %collective-permute-done.10.refs_3_), channel_id=1, source_target_pairs={{0,4},{4,0},{1,5},{5,1},{2,6},{6,2},{3,7},{7,3},{8,12},{12,8},{9,1... | collective-permute-start | bytes 3145736 | tf_op jit(solution)/shard_map/ppermute | solution.py:275
  121.5 32.2 %collective-permute-start.20 = (bf16[128,1024]{1,0:T(8,128)(2,1)}, bf16[128,1024]{1,0:T(8,128)(2,1)}, u32[]{:S(2)}, u32[]{:S(2)}) collective-permute-start(bf16[128,1024]{1,0:T(8,128)(2,1)} %shard_map.73.own_ref), channel_id=1, source_target_pairs={{0,1},{1,0},{2,3},{3,2},{4,5},{5,4},{6,7},{7,6},{8,9},{9,8},{10,11... | collective-permute-start | bytes 786440 | tf_op jit(solution)/shard_map/ppermute | solution.py:315
  128.2 38.4 %collective-permute-start.18 = (bf16[128,1024]{1,0:T(8,128)(2,1)S(1)}, bf16[128,1024]{1,0:T(8,128)(2,1)}, u32[]{:S(2)}, u32[]{:S(2)}) collective-permute-start(bf16[128,1024]{1,0:T(8,128)(2,1)S(1)} %shard_map.71.own_ref), channel_id=1, source_target_pairs={{0,1},{1,0},{2,3},{3,2},{4,5},{5,4},{6,7},{7,6},{8,9},{9,8},{10,11... | collective-permute-start | bytes 786440 | tf_op jit(solution)/shard_map/ppermute | solution.py:315
  133.0 40.3 %collective-permute-start.16 = (bf16[128,1024]{1,0:T(8,128)(2,1)S(1)}, bf16[128,1024]{1,0:T(8,128)(2,1)S(1)}, u32[]{:S(2)}, u32[]{:S(2)}) collective-permute-start(bf16[128,1024]{1,0:T(8,128)(2,1)S(1)} %shard_map.69.own_ref), channel_id=1, source_target_pairs={{0,1},{1,0},{2,3},{3,2},{4,5},{5,4},{6,7},{7,6},{8,9},{9,8},{10,11... | collective-permute-start | bytes 786440 | tf_op jit(solution)/shard_map/ppermute | solution.py:315
  138.5 45.3 %collective-permute-start = (bf16[128,1024]{1,0:T(8,128)(2,1)S(1)}, bf16[128,1024]{1,0:T(8,128)(2,1)S(1)}, u32[]{:S(2)}, u32[]{:S(2)}) collective-permute-start(bf16[128,1024]{1,0:T(8,128)(2,1)S(1)} %shard_map.67.own_ref), channel_id=1, source_target_pairs={{0,1},{1,0},{2,3},{3,2},{4,5},{5,4},{6,7},{7,6},{8,9},{9,8},{10,11... | collective-permute-start | bytes 786440 | tf_op jit(solution)/shard_map/ppermute | solution.py:315
  160.3 29.8 %collective-permute-start.21 = (bf16[128,1024]{1,0:T(8,128)(2,1)S(1)}, bf16[128,1024]{1,0:T(8,128)(2,1)S(1)}, u32[]{:S(2)}, u32[]{:S(2)}) collective-permute-start(bf16[128,1024]{1,0:T(8,128)(2,1)S(1)} %get-tuple-element.24), channel_id=1, source_target_pairs={{0,3},{1,2},{2,1},{3,0},{4,7},{5,6},{6,5},{7,4},{8,11},{9,10},{10,... | collective-permute-start | bytes 786440 | tf_op jit(solution)/shard_map/ppermute | solution.py:327
  173.2 31.1 %collective-permute-start.19 = (bf16[128,1024]{1,0:T(8,128)(2,1)S(1)}, bf16[128,1024]{1,0:T(8,128)(2,1)S(1)}, u32[]{:S(2)}, u32[]{:S(2)}) collective-permute-start(bf16[128,1024]{1,0:T(8,128)(2,1)S(1)} %get-tuple-element.22), channel_id=1, source_target_pairs={{0,3},{1,2},{2,1},{3,0},{4,7},{5,6},{6,5},{7,4},{8,11},{9,10},{10,... | collective-permute-start | bytes 786440 | tf_op jit(solution)/shard_map/ppermute | solution.py:327
  179.4 30.5 %collective-permute-start.17 = (bf16[128,1024]{1,0:T(8,128)(2,1)S(1)}, bf16[128,1024]{1,0:T(8,128)(2,1)S(1)}, u32[]{:S(2)}, u32[]{:S(2)}) collective-permute-start(bf16[128,1024]{1,0:T(8,128)(2,1)S(1)} %get-tuple-element.20), channel_id=1, source_target_pairs={{0,3},{1,2},{2,1},{3,0},{4,7},{5,6},{6,5},{7,4},{8,11},{9,10},{10,... | collective-permute-start | bytes 786440 | tf_op jit(solution)/shard_map/ppermute | solution.py:327
  190.0 25.4 %collective-permute-start.15 = (bf16[128,1024]{1,0:T(8,128)(2,1)S(1)}, bf16[128,1024]{1,0:T(8,128)(2,1)S(1)}, u32[]{:S(2)}, u32[]{:S(2)}) collective-permute-start(bf16[128,1024]{1,0:T(8,128)(2,1)S(1)} %get-tuple-element.18), channel_id=1, source_target_pairs={{0,3},{1,2},{2,1},{3,0},{4,7},{5,6},{6,5},{7,4},{8,11},{9,10},{10,... | collective-permute-start | bytes 786440 | tf_op jit(solution)/shard_map/ppermute | solution.py:327
  (19 other events, 149.3 us)

commit v2 on v1

v2 whole, which is shorter than its diff:
```python
import functools

import jax
import jax.numpy as jnp
import numpy as np
from jax import lax
from jax.experimental import pallas as pl
from jax.experimental.pallas import tpu as pltpu
from jax.sharding import Mesh, PartitionSpec as P

DH = 512
DK = 256
T = 512
BLOCKS = 64
SLICE = 8
EXT = DH + 128
SEQ = ("x", "y", "z", "c")
CHUNKS = 4
F32 = jnp.float32
BF16 = jnp.bfloat16
SCALE = DK ** (-0.5)
LOWEST = -1e30


def split3(a):
    hi = a.astype(BF16).astype(F32)
    rest = a - hi
    mid = rest.astype(BF16).astype(F32)
    return hi, mid, rest - mid


def lanes(shape):
    return lax.broadcasted_iota(jnp.int32, shape, len(shape) - 1)


def rows(shape):
    return lax.broadcasted_iota(jnp.int32, shape, 0)


def place(columns, shape):
    lane = lanes(shape)
    out = jnp.zeros(shape, F32)
    for i, column in enumerate(columns):
        out = jnp.where(lane == i, column, out)
    return out


def pick(tile, first, count):
    lane = lanes(tile.shape)
    keep = (lane >= first) & (lane < first + count)
    return jnp.sum(jnp.where(keep, tile, 0.0), axis=1, keepdims=True)


def running_sum(a):
    width = a.shape[1]
    lane = lanes(a.shape)
    step = 1
    while step < width:
        a = a + jnp.where(lane >= step, pltpu.roll(a, step, 1), 0.0)
        step *= 2
    return a


def suffix_sum(a):
    width = a.shape[1]
    lane = lanes(a.shape)
    step = 1
    while step < width:
        a = a + jnp.where(lane < width - step, pltpu.roll(a, width - step, 1), 0.0)
        step *= 2
    return a


def decay_rows(forget):
    return running_sum(jnp.minimum(forget, 0.0) - jnp.log1p(jnp.exp(-jnp.abs(forget))))


def to_columns(tile):
    full = jnp.concatenate([tile, jnp.zeros((120, tile.shape[1]), F32)], axis=0)
    return full.T


def load(pairs, sems):
    copies = [pltpu.make_async_copy(a, b, sems.at[i]) for i, (a, b) in enumerate(pairs)]
    for copy in copies:
        copy.start()
    return copies


def summary_kernel(k_hbm, v_hbm, ig_hbm, fg_hbm, *refs):
    out_ref, k_ref, v_ref, ig_ref, fg_ref, sems = refs[-6:]
    copies = load(
        ((fg_hbm, fg_ref), (ig_hbm, ig_ref), (k_hbm, k_ref), (v_hbm, v_ref)), sems
    )
    for copy in copies[:2]:
        copy.wait()
    decay = decay_rows(fg_ref[...])
    total = decay[:, T - 1 : T]
    source = total - decay + ig_ref[...]
    peak = jnp.max(source, axis=1, keepdims=True)
    scale = jnp.exp(source - peak)
    for copy in copies[2:]:
        copy.wait()
    for h in range(2):
        keys = k_ref[:, h * DK : (h + 1) * DK].astype(F32).T
        scaled = keys * scale[h : h + 1]
        normal = jnp.sum(scaled, axis=1, keepdims=True)
        memory = jnp.dot(
            scaled.astype(BF16), v_ref[:, h * DH : (h + 1) * DH], preferred_element_type=F32
        )
        held = slice(h * DK, (h + 1) * DK)
        out_ref[held, :DH] = memory.astype(BF16)
        ones = jnp.ones((DK, 1), F32)
        parts = split3(normal)
        parts += split3(ones * jnp.maximum(total[h : h + 1], LOWEST))
        parts += split3(ones * peak[h : h + 1])
        out_ref[held, DH:] = place(parts, (DK, 128)).astype(BF16)


def combine_kernel(in_ref, *refs):
    out_ref = refs[-1]
    size = BLOCKS * SLICE
    tile = in_ref[:, DH:].astype(F32)
    across = tile.T
    decay = (across[3:4] + across[4:5]) + across[5:6]
    peak = (across[6:7] + across[7:8]) + across[8:9]
    shape = (BLOCKS, size)
    block, lane = rows(shape), lanes(shape)
    source = lax.shift_right_logical(lane, 3)
    earlier = source < block
    head_lane = (lane & (SLICE - 1)) == 0
    held = jnp.where(earlier & head_lane, decay, 0.0)
    total = jnp.sum(held, axis=1, keepdims=True)
    after = suffix_sum(jnp.where(lane < size - 1, pltpu.roll(held, size - 1, 1), 0.0))
    weight = peak + after
    running = jnp.maximum(
        total, jnp.max(jnp.where(earlier, weight, LOWEST), axis=1, keepdims=True)
    )
    factor = jnp.where(earlier, jnp.exp(jnp.minimum(weight - running, 0.0)), 0.0)
    spread = (
        lax.shift_right_logical(rows((size, BLOCKS)), 3) == lanes((size, BLOCKS))
    ).astype(BF16)
    same = (rows((size, size)) & (SLICE - 1)) == (lanes((size, size)) & (SLICE - 1))
    memory = jnp.zeros((size, DH), F32)
    scalars = jnp.zeros((size, 128), F32)
    for i, part in enumerate(split3(factor)):
        wide = jnp.dot(spread, part.astype(BF16), preferred_element_type=F32)
        wide = jnp.where(same, wide, 0.0).astype(BF16)
        scalars += jnp.dot(wide, in_ref[:, DH:], preferred_element_type=F32)
        if i < 2:
            memory += jnp.dot(wide, in_ref[:, :DH], preferred_element_type=F32)
    out_ref[:, :DH] = memory.astype(BF16)
    peaks = place(split3(running), (BLOCKS, 128)).astype(BF16)
    peaks = jnp.dot(spread, peaks, preferred_element_type=F32)
    normal = pick(scalars, 0, 3)
    entries = split3(normal) + split3(pick(peaks, 0, 3))
    out_ref[:, DH:] = place(entries, (size, 128)).astype(BF16)


def intra_kernel(q_hbm, k_hbm, v_hbm, ig_hbm, fg_hbm, _, numer_hbm, terms_hbm, *scratch):
    q_ref, k_ref, v_ref, ig_ref, fg_ref, numer_ref, terms_ref, sems = scratch
    copies = load(
        (
            (fg_hbm, fg_ref), (ig_hbm, ig_ref), (q_hbm, q_ref), (k_hbm, k_ref), (v_hbm, v_ref),
        ),
        sems,
    )
    for copy in copies[:2]:
        copy.wait()
    decay = decay_rows(fg_ref[...])
    offset = ig_ref[...]
    columns = to_columns(jnp.concatenate([decay, jnp.zeros((6, T), F32)], axis=0))
    causal = rows((T, T)) >= lanes((T, T))
    for copy in copies[2:]:
        copy.wait()
    terms = []
    stores = []
    for h in range(2):
        scores = (
            lax.dot_general(
                q_ref[:, h * DK : (h + 1) * DK],
                k_ref[:, h * DK : (h + 1) * DK],
                (((1,), (1,)), ((), ())),
                preferred_element_type=F32,
            )
            * SCALE
        )
        own = columns[:, h : h + 1]
        logits = own - decay[h : h + 1] + offset[h : h + 1]
        logits = jnp.where(causal, logits, -jnp.inf)
        row_peak = jnp.max(logits, axis=1, keepdims=True)
        weights = (jnp.exp(logits - row_peak) * scores).astype(BF16)
        held = numer_ref.at[:, h * DH : (h + 1) * DH]
        held[...] = jnp.dot(weights, v_ref[:, h * DH : (h + 1) * DH], preferred_element_type=F32)
        store = pltpu.make_async_copy(
            held, numer_hbm.at[:, h * DH : (h + 1) * DH], sems.at[5 + h]
        )
        store.start()
        stores.append(store)
        terms += [own, row_peak, jnp.sum(weights.astype(F32), axis=1, keepdims=True)]
    terms_ref[...] = place(terms, (T, 128))
    store = pltpu.make_async_copy(terms_ref, terms_hbm, sems.at[7])
    store.start()
    for store in stores + [store]:
        store.wait()


def readout_kernel(start, q_hbm, m_hbm, numer_hbm, terms_hbm, out_ref, *scratch):
    q_ref, m_ref, numer_ref, terms_ref, sems = scratch
    mine = pl.ds(start, out_ref.shape[0])
    copies = load(
        (
            (m_hbm, m_ref), (q_hbm.at[mine], q_ref),
            (terms_hbm.at[mine], terms_ref), (numer_hbm.at[mine], numer_ref),
        ),
        sems,
    )
    for copy in copies:
        copy.wait()
    terms = terms_ref[...]
    for h in range(2):
        own, row_peak, denom = (terms[:, 3 * h + i : 3 * h + i + 1] for i in range(3))
        held = slice(h * DK, (h + 1) * DK)
        peak = pick(m_ref[h * DK : h * DK + 8, DH:].astype(F32), 3, 3)[:1]
        read = jnp.dot(q_ref[:, held], m_ref[held], preferred_element_type=F32) * SCALE
        prior = own + peak
        ceiling = jnp.maximum(prior, row_peak)
        prior_scale = jnp.exp(prior - ceiling)
        local_scale = jnp.exp(row_peak - ceiling)
        columns = slice(h * DH, (h + 1) * DH)
        numerator = prior_scale * read[:, :DH] + local_scale * numer_ref[:, columns]
        denominator = prior_scale * pick(read[:, DH:], 0, 3) + local_scale * denom
        floor_value = jnp.maximum(jnp.abs(denominator), 1.0)
        out_ref[:, columns] = (numerator / floor_value).astype(BF16)


def order_kernel(*refs):
    pass


def group_kernel(where_ref, *refs):
    pieces, out_ref = refs[:4], refs[-1]
    for i, piece in enumerate(pieces):
        slot = where_ref[2] ^ i
        out_ref[pl.ds(pl.multiple_of(slot * 64, 64), 64)] = piece[...]


def ring_kernel(where_ref, *refs):
    pieces, out_ref = refs[:4], refs[-1]
    start = jnp.where((where_ref[2] & 1) == 0, where_ref[1], where_ref[0])
    for r, piece in enumerate(pieces):
        out_ref[(start + r) & 3] = piece[...]


def product(first, where_ref, own_ref, other_ref, pieces, held, sems):
    x, y, c = where_ref[0], where_ref[1], where_ref[2] & 1
    blocks = (where_ref[first], where_ref[first + 1])

    def fetch(along_x, along_y):
        for s in range(2):
            for r in range(4):
                @pl.when(((x + r) & 3) == blocks[s])
                def _():
                    pltpu.make_async_copy(along_x[r], held.at[0, s], sems.at[s]).start()
        for s in range(2):
            for r in range(4):
                pltpu.make_async_copy(
                    along_y[r].at[blocks[s]], held.at[1, s, (y + r) & 3], sems.at[2 + s]
                ).start()

    @pl.when(c == 0)
    def _():
        fetch(pieces[:4], pieces[4:])

    @pl.when(c == 1)
    def _():
        fetch(pieces[4:], pieces[:4])

    total = jnp.zeros((own_ref.shape[0], 1024), F32)
    for half in range(2):
        for s, rows_ref in enumerate((own_ref, other_ref)):
            block = held.at[half, s]
            pltpu.make_async_copy(block, block, sems.at[2 * half + s]).wait()
            total += lax.dot_general(
                rows_ref[:, half * 512 : (half + 1) * 512],
                block[...].reshape(1024, 512),
                (((1,), (1,)), ((), ())),
                preferred_element_type=F32,
            )
    return total


def project_kernel(first, where_ref, own_ref, other_ref, *refs):
    out_ref, held, sems = refs[-3:]
    total = product(first, where_ref, own_ref, other_ref, refs[:8], held, sems)
    out_ref[...] = total.astype(out_ref.dtype)


def finish_kernel(start, where_ref, own_ref, other_ref, arrived_ref, *refs):
    out_hbm, held, sems, staged = refs[-4:]
    total = product(5, where_ref, own_ref, other_ref, refs[:8], held, sems)
    staged[...] = (total + arrived_ref[...].astype(F32)).astype(BF16)
    rows_out = out_hbm.at[pl.ds(start, staged.shape[0])]
    pltpu.async_copy(staged, rows_out, sems.at[0]).wait()


def add_kernel(start, kept_ref, arrived_ref, _, out_hbm, staged, sem):
    staged[...] = (kept_ref[...] + arrived_ref[...].astype(F32)).astype(BF16)
    pltpu.async_copy(staged, out_hbm.at[pl.ds(start, staged.shape[0])], sem).wait()


def call(kernel, out_shape, *operands, cost_us=None, **kwargs):
    if cost_us is not None:
        kwargs["cost_estimate"] = pl.CostEstimate(
            flops=0, bytes_accessed=int(cost_us * 3.7e6), transcendentals=0
        )
    return pl.pallas_call(
        kernel,
        out_shape=out_shape,
        compiler_params=pltpu.CompilerParams(vmem_limit_bytes=16 * 1024 * 1024),
        **kwargs,
    )(*operands)


def shape(rows_, columns, dtype):
    return jax.ShapeDtypeStruct((rows_, columns), dtype)


SIZES = (4, 4, 2, 2, 4)
NAMES = SEQ + ("h",)
ANY = pl.BlockSpec(memory_space=pl.ANY)
VMEM = pl.BlockSpec(memory_space=pltpu.VMEM)
SMEM = pl.BlockSpec(memory_space=pltpu.SMEM)
HBM = pl.BlockSpec(memory_space=pltpu.MemorySpace.HBM)
SEM = pltpu.SemaphoreType.DMA


def fetch(a, source_of):
    places = [tuple(int(i) for i in p) for p in np.ndindex(*SIZES)]
    index = {p: i for i, p in enumerate(places)}
    return lax.ppermute(a, NAMES, [(index[source_of(*p)], index[p]) for p in places])


def paired(x, h):
    outer = h in (0, 3)
    moves = {1: 0, 2: 3} if outer else {0: 1, 3: 2}
    return (moves[x], h ^ 1) if x in moves else (x, h)


def along(turned, r):
    def source_of(x, y, z, c, h):
        if (c == 1) ^ turned:
            return ((x + r) % 4, y, z, c, h)
        return (x, (y + r) % 4, z, c, h)

    return source_of


def pinned(*arrays):
    return [pltpu.with_memory_space_constraint(a, pltpu.MemorySpace.HBM) for a in arrays]


def order(a, *after):
    return call(
        order_kernel, jax.ShapeDtypeStruct(a.shape, a.dtype), a, *after,
        in_specs=[ANY] * (1 + len(after)), out_specs=ANY, input_output_aliases={0: 0},
    )


def weight_near(out_weight):
    c = lax.axis_index("c")
    columns = out_weight.T
    low, high = columns[:, :512], columns[:, 512:]
    halves = (jnp.where(c == 0, low, high), jnp.where(c == 0, high, low))

    def source_of(dz, dc):
        def of(x, y, z, c, h):
            sx, sh = paired(x, h)
            return (sx, y, z ^ dz, c ^ dc, sh)

        return of

    return [fetch(halves[dc], source_of(dz, dc)) for dz in range(2) for dc in range(2)]


def per_device(queries, key_rows, value_rows, input_gate, forget_gate, out_weight):
    x, y, z, c, h = (lax.axis_index(n) for n in NAMES)
    outer = (h == 0) | (h == 3)
    keep = (h >= 2).astype(jnp.int32)

    def block(half, is_outer):
        return jnp.where(is_outer, 3 * half, 1 + half)

    where = jnp.stack(
        [
            x, y, 2 * z + c,
            block(1 - keep, outer), block(1 - keep, ~outer),
            block(keep, outer), block(keep, ~outer),
        ]
    ).astype(jnp.int32)

    near = weight_near(out_weight)
    gates = (input_gate.T, forget_gate.T)
    gate_space = [pltpu.VMEM((2, T), F32)] * 2
    summary = call(
        summary_kernel, shape(T, EXT, BF16), *pinned(key_rows, value_rows, *gates),
        in_specs=[HBM] * 4, out_specs=VMEM,
        scratch_shapes=[
            pltpu.VMEM((T, 2 * DK), BF16), pltpu.VMEM((T, 2 * DH), BF16), *gate_space, SEM((4,)),
        ],
    )
    grouped = lax.all_to_all(summary.reshape(BLOCKS, SLICE, EXT), SEQ, 0, 0, tiled=True)
    group = call(
        group_kernel, shape(256, 512, BF16), where, *near, summary,
        in_specs=[SMEM] + [VMEM] * 4 + [ANY], out_specs=VMEM,
    )
    ring = [group] + [fetch(group, along(False, r)) for r in (1, 2, 3)]
    entering = call(
        combine_kernel, shape(T, EXT, BF16), grouped.reshape(T, EXT), group,
        in_specs=[VMEM, ANY], out_specs=VMEM, cost_us=0.1,
    )
    carried = lax.all_to_all(entering.reshape(BLOCKS, SLICE, EXT), SEQ, 0, 0, tiled=True)
    carried = carried.reshape(T, EXT)
    plane = call(
        ring_kernel, jax.ShapeDtypeStruct((4, 256, 512), BF16), where, *ring, entering,
        in_specs=[SMEM] + [VMEM] * 4 + [ANY], out_specs=VMEM, cost_us=20,
    )
    pieces = [plane] + [fetch(plane, along(True, r)) for r in (1, 2, 3)]
    numer, terms = call(
        intra_kernel,
        (pltpu.MemorySpace.HBM((T, 2 * DH), F32), pltpu.MemorySpace.HBM((T, 128), F32)),
        *pinned(queries, key_rows, value_rows, *gates), plane,
        in_specs=[HBM] * 5 + [ANY], out_specs=(HBM, HBM), cost_us=0.1,
        scratch_shapes=[
            pltpu.VMEM((T, 2 * DK), BF16), pltpu.VMEM((T, 2 * DK), BF16),
            pltpu.VMEM((T, 2 * DH), BF16), *gate_space,
            pltpu.VMEM((T, 2 * DH), F32), pltpu.VMEM((T, 128), F32), SEM((8,)),
        ],
    )

    size = T // CHUNKS
    hiddens = []
    for i in range(CHUNKS):
        hiddens.append(call(
            functools.partial(readout_kernel, i * size), shape(size, 2 * DH, BF16),
            *pinned(queries, carried, numer, terms),
            in_specs=[HBM] * 4, out_specs=VMEM,
            scratch_shapes=[
                pltpu.VMEM((size, 2 * DK), BF16), pltpu.VMEM((T, EXT), BF16),
                pltpu.VMEM((size, 2 * DH), F32), pltpu.VMEM((size, 128), F32), SEM((4,)),
            ],
        ))
    first = lax.ppermute(hiddens[0], "h", [(j, j ^ 1) for j in range(4)])
    pieces = pieces[:1] + [order(a, first) for a in pieces[1:]]
    pieces += [lax.ppermute(a, "c", [(0, 1), (1, 0)]) for a in pieces]
    held = [pltpu.VMEM((2, 2, 4, 256, 512), BF16), SEM((4,))]
    staged = pltpu.VMEM((size, 1024), BF16)

    def project(first, dtype, hidden, other, *after):
        return call(
            functools.partial(project_kernel, first), shape(size, 1024, dtype),
            where, hidden, other, *pieces, *after,
            in_specs=[SMEM, VMEM, VMEM] + [ANY] * (8 + len(after)), out_specs=VMEM,
            scratch_shapes=held,
        )

    out = None
    others, sends, arrivals = [], [], []
    for i, hidden in enumerate(hiddens):
        if i > 0:
            hidden = order(hidden, others[i - 1], *sends[max(i - 2, 0) : i - 1])
            other = lax.ppermute(hidden, "h", [(j, j ^ 1) for j in range(4)])
        else:
            other = first
        send = project(3, BF16, hidden, other)
        if i > 0:
            send = order(send, arrivals[i - 1])
        arrived = lax.ppermute(send, "h", [(j, 3 - j) for j in range(4)])
        others.append(other)
        sends.append(send)
        arrivals.append(arrived)
        before = [] if out is None else [out]
        if i < CHUNKS - 1:
            out = call(
                functools.partial(finish_kernel, i * size), shape(T, 1024, BF16),
                where, hidden, other, arrived, *pieces, *before,
                in_specs=[SMEM, VMEM, VMEM, VMEM] + [ANY] * 8 + [HBM] * len(before),
                out_specs=HBM, scratch_shapes=held + [staged],
                input_output_aliases={12: 0} if before else {},
            )
        else:
            out = call(
                functools.partial(add_kernel, i * size), shape(T, 1024, BF16),
                project(5, F32, hidden, other), arrived, out,
                in_specs=[VMEM, VMEM, HBM], out_specs=HBM,
                scratch_shapes=[staged, SEM], input_output_aliases={2: 0},
            )
    return out


def solution(mesh):
    fine = Mesh(mesh.devices.reshape(4, 4, 2, 2, 4), SEQ + ("h",))
    both = P(SEQ, "h")
    return jax.shard_map(
        per_device,
        mesh=fine,
        in_specs=(both,) * 5 + (P("h", SEQ),),
        out_specs=both,
        check_vma=False,
    )
```

time: 218 us -> 163 us (0.75)
  waiting for transfers between devices: 103 us -> 51.7 us
  local copies, waits for them, and re-layouts: 16.2 us -> 0.09 us
  starting transfers between devices: 54.8 us -> 63.7 us
  Pallas kernels: 40.7 us -> 46.4 us
    ppermute x14 -> x15, waiting for transfers between devices: 62.8 us -> 40.1 us  [the longest x10 40.1 us: fetch(): lax.ppermute(a, NAMES, [(index[source_of(*p)], index[p]) for p in places])]
    ppermute x4, waiting for transfers between devices: 25.1 us -> 3.77 us  [per_device(): arrived = lax.ppermute(send, 'h', [(j, 3 - j) for j in range(4)])]
    unnamed x42 -> x2, local copies, waits for them, and re-layouts: 13.2 us -> 0.01 us
    all_to_all x1, starting transfers between devices: 5.9 us -> 14.3 us  [per_device(): lax.all_to_all(entering.reshape(BLOCKS, SLICE, EXT), SEQ, 0, 0, tiled=True)]
    all_to_all x1, starting transfers between devices: 16.3 us -> 8.96 us  [per_device(): lax.all_to_all(summary.reshape(BLOCKS, SLICE, EXT), SEQ, 0, 0, tiled=True)]
    ppermute x4 -> x3, waiting for transfers between devices: 15 us -> 7.82 us  [per_device(): other = lax.ppermute(hidden, 'h', [(j, j ^ 1) for j in range(4)])]
    ppermute x4, starting transfers between devices: 11 us -> 18.1 us  [per_device(): arrived = lax.ppermute(send, 'h', [(j, 3 - j) for j in range(4)])]
    pallas_call x11 -> x27, Pallas kernels: 40.7 us -> 46.4 us  [call(): pl.pallas_call(kernel, out_shape=out_shape, compiler_params=pltpu.Compile...]
  transfers between devices with their start and end apart: 24 -> 24, of which waited for: 10 -> 11; matrix products, arithmetic and copies ran while one was open for 2% -> 0% of each run, Pallas kernels for 19% -> 24%
where the time goes in v2:
time: 163 us; the launch traced here: 162 us
  starting transfers between devices  63.7 us (39%)
  waiting for transfers between devices  51.7 us (32%)
  Pallas kernels  46.4 us (28%)
    pallas_call x27, Pallas kernels, call(): pl.pallas_call(kernel, out_shape=out_shape, compiler_params=pltpu.Compile...  46.4 us
    ppermute x10, waiting for transfers between devices, fetch(): lax.ppermute(a, NAMES, [(index[source_of(*p)], index[p]) for p in places])  40.1 us
    ppermute x4, starting transfers between devices, per_device(): arrived = lax.ppermute(send, 'h', [(j, 3 - j) for j in range(4)])  18.1 us
    all_to_all x1, starting transfers between devices, per_device(): lax.all_to_all(entering.reshape(BLOCKS, SLICE, EXT), SEQ, 0, 0, tiled=True)  14.3 us
    ppermute x10, starting transfers between devices, fetch(): lax.ppermute(a, NAMES, [(index[source_of(*p)], index[p]) for p in places])  12.3 us
    all_to_all x1, starting transfers between devices, per_device(): lax.all_to_all(summary.reshape(BLOCKS, SLICE, EXT), SEQ, 0, 0, tiled=True)  8.96 us
    ppermute x3, starting transfers between devices, per_device(): other = lax.ppermute(hidden, 'h', [(j, j ^ 1) for j in range(4)])  8.17 us
    ppermute x3, waiting for transfers between devices, per_device(): other = lax.ppermute(hidden, 'h', [(j, j ^ 1) for j in range(4)])  7.82 us
  transfers between devices with their start and end apart: 24, of which 11 were waited for; matrix products, arithmetic and copies ran while one was open for 0% of the time, Pallas kernels for 24%

profile of v2, /device:TPU:32, one launch (start us, length us, event | category | flops | bytes accessed | tf_op | source)
XLA Modules:
  0.0 162.3 jit_solution(7324280215718618257)
XLA Ops:
  0.0 2.9 %shard_map.64.refs_4_ = bf16[512,640]{1,0:T(8,128)(2,1)} custom-call(bf16[512,512]{1,0:T(8,128)(2,1)} %k_hbm.3, bf16[512,1024]{1,0:T(8,128)(2,1)} %v_hbm.3, f32[2,512]{1,0:T(2,128)} %bitcast.16, f32[2,512]{1,0:T(2,128)} %bitcast.18), custom_call_target="tpu_custom_call" | custom-call | tf_op jit(solution)/shard_map/pallas_call | solution.py:317
  2.9 9.0 %all-to-all-start = ((bf16[64,8,640]{2,1,0:T(8,128)(2,1)}), bf16[64,8,640]{2,1,0:T(8,128)(2,1)S(1)}, u32[]{:S(2)}, u32[]{:S(2)}) async-start(bf16[64,8,640]{2,1,0:T(8,128)(2,1)} %bitcast.9), calls=%async_computation | async-start | bytes 1310720 | tf_op jit(solution)/shard_map/all_to_all | solution.py:412
  14.9 8.7 %collective-permute-done.3.refs_3_ = bf16[64,512]{1,0:T(8,128)(2,1)S(1)} collective-permute-done((bf16[64,512]{1,0:T(8,128)(2,1)S(1)}, bf16[64,512]{1,0:T(8,128)(2,1)S(1)}, u32[]{:S(2)}, u32[]{:S(2)}) %collective-permute-start.3) | collective-permute-done | bytes 65568 | tf_op jit(solution)/shard_map/ppermute | solution.py:341
  26.0 3.3 %shard_map.66.refs_4_ = bf16[512,640]{1,0:T(8,128)(2,1)} custom-call(bf16[512,640]{1,0:T(8,128)(2,1)S(1)} %bitcast.14, bf16[256,512]{1,0:T(8,128)(2,1)S(1)} %shard_map.65.refs_0_), custom_call_target="tpu_custom_call" | custom-call | bytes 370000 | tf_op jit(solution)/shard_map/pallas_call | solution.py:317
  29.3 14.3 %all-to-all-start.1 = ((bf16[64,8,640]{2,1,0:T(8,128)(2,1)}), bf16[64,8,640]{2,1,0:T(8,128)(2,1)}, u32[]{:S(2)}, u32[]{:S(2)}) async-start(bf16[64,8,640]{2,1,0:T(8,128)(2,1)} %bitcast.12), calls=%async_computation.1 | async-start | bytes 1310720 | tf_op jit(solution)/shard_map/all_to_all | solution.py:422
  45.2 2.7 %collective-permute-start.5 = (bf16[256,512]{1,0:T(8,128)(2,1)S(1)}, bf16[256,512]{1,0:T(8,128)(2,1)S(1)}, u32[]{:S(2)}, u32[]{:S(2)}) collective-permute-start(bf16[256,512]{1,0:T(8,128)(2,1)S(1)} %shard_map.65.refs_0_), channel_id=1, source_target_pairs={{32,0},{33,1},{34,2},{35,3},{132,4},{133,5},{134,6},{135,7},{40,8}... | collective-permute-start | bytes 786440 | tf_op jit(solution)/shard_map/ppermute | solution.py:341
  49.3 8.1 %collective-permute-done.6.refs_3_ = bf16[256,512]{1,0:T(8,128)(2,1)S(1)} collective-permute-done((bf16[256,512]{1,0:T(8,128)(2,1)S(1)}, bf16[256,512]{1,0:T(8,128)(2,1)S(1)}, u32[]{:S(2)}, u32[]{:S(2)}) %collective-permute-start.6) | collective-permute-done | bytes 262176 | tf_op jit(solution)/shard_map/ppermute | solution.py:341
  57.4 3.3 %collective-permute-done.5.refs_2_ = bf16[256,512]{1,0:T(8,128)(2,1)S(1)} collective-permute-done((bf16[256,512]{1,0:T(8,128)(2,1)S(1)}, bf16[256,512]{1,0:T(8,128)(2,1)S(1)}, u32[]{:S(2)}, u32[]{:S(2)}) %collective-permute-start.5) | collective-permute-done | bytes 262176 | tf_op jit(solution)/shard_map/ppermute | solution.py:341
  65.1 4.1 %shard_map.68 = (f32[512,1024]{1,0:T(8,128)}, f32[512,128]{1,0:T(8,128)}) custom-call(bf16[512,512]{1,0:T(8,128)(2,1)} %q_hbm.9, bf16[512,512]{1,0:T(8,128)(2,1)} %k_hbm.3, bf16[512,1024]{1,0:T(8,128)(2,1)} %v_hbm.3, f32[2,512]{1,0:T(2,128)} %bitcast.17, f32[2,512]{1,0:T(2,128)} %bitcast.19, bf16[4,256,512]{2,1,0:T(8,128)(2,1)S(1)} %shard_map.67._.refs_0_), custom_call_target="tpu_custom_call" | custom-call | bytes 370000 | tf_op jit(solution)/shard_map/pallas_call | solution.py:317
  72.5 14.7 %collective-permute-done.9.refs_0_ = bf16[4,256,512]{2,1,0:T(8,128)(2,1)} collective-permute-done((bf16[4,256,512]{2,1,0:T(8,128)(2,1)S(1)}, bf16[4,256,512]{2,1,0:T(8,128)(2,1)}, u32[]{:S(2)}, u32[]{:S(2)}) %collective-permute-start.9) | collective-permute-done | bytes 1048608 | tf_op jit(solution)/shard_map/ppermute | solution.py:341
  87.8 3.4 %collective-permute-done.11.refs_0_ = bf16[4,256,512]{2,1,0:T(8,128)(2,1)S(1)} collective-permute-done((bf16[4,256,512]{2,1,0:T(8,128)(2,1)S(1)}, bf16[4,256,512]{2,1,0:T(8,128)(2,1)S(1)}, u32[]{:S(2)}, u32[]{:S(2)}) %collective-permute-start.11) | collective-permute-done | bytes 1048608 | tf_op jit(solution)/shard_map/ppermute | solution.py:341
  97.1 4.6 %collective-permute-start.17 = (bf16[128,1024]{1,0:T(8,128)(2,1)S(1)}, bf16[128,1024]{1,0:T(8,128)(2,1)S(1)}, u32[]{:S(2)}, u32[]{:S(2)}) collective-permute-start(bf16[128,1024]{1,0:T(8,128)(2,1)S(1)} %shard_map.77.refs_2_), channel_id=1, source_target_pairs={{0,3},{1,2},{2,1},{3,0},{4,7},{5,6},{6,5},{7,4},{8,11},{9,10},{10,... | collective-permute-start | bytes 786440 | tf_op jit(solution)/shard_map/ppermute | solution.py:478
  106.3 3.4 %collective-permute-start.16 = (bf16[128,1024]{1,0:T(8,128)(2,1)S(1)}, bf16[128,1024]{1,0:T(8,128)(2,1)S(1)}, u32[]{:S(2)}, u32[]{:S(2)}) collective-permute-start(bf16[128,1024]{1,0:T(8,128)(2,1)S(1)} %shard_map.78.own_ref), channel_id=1, source_target_pairs={{0,1},{1,0},{2,3},{3,2},{4,5},{5,4},{6,7},{7,6},{8,9},{9,8},{10,11... | collective-permute-start | bytes 786440 | tf_op jit(solution)/shard_map/ppermute | solution.py:472
  112.3 4.2 %collective-permute-start.19 = (bf16[128,1024]{1,0:T(8,128)(2,1)S(1)}, bf16[128,1024]{1,0:T(8,128)(2,1)S(1)}, u32[]{:S(2)}, u32[]{:S(2)}) collective-permute-start(bf16[128,1024]{1,0:T(8,128)(2,1)S(1)} %shard_map.80.refs_2_), channel_id=1, source_target_pairs={{0,3},{1,2},{2,1},{3,0},{4,7},{5,6},{6,5},{7,4},{8,11},{9,10},{10,... | collective-permute-start | bytes 786440 | tf_op jit(solution)/shard_map/ppermute | solution.py:478
  121.0 3.4 %collective-permute-start.18 = (bf16[128,1024]{1,0:T(8,128)(2,1)S(1)}, bf16[128,1024]{1,0:T(8,128)(2,1)S(1)}, u32[]{:S(2)}, u32[]{:S(2)}) collective-permute-start(bf16[128,1024]{1,0:T(8,128)(2,1)S(1)} %shard_map.81.own_ref), channel_id=1, source_target_pairs={{0,1},{1,0},{2,3},{3,2},{4,5},{5,4},{6,7},{7,6},{8,9},{9,8},{10,11... | collective-permute-start | bytes 786440 | tf_op jit(solution)/shard_map/ppermute | solution.py:472
  124.5 2.8 %shard_map.84.refs_0_ = bf16[128,1024]{1,0:T(8,128)(2,1)S(1)} custom-call(s32[7]{0:T(128)S(1)} %stack.31.where_ref, bf16[128,1024]{1,0:T(8,128)(2,1)S(1)} %shard_map.78.own_ref, bf16[128,1024]{1,0:T(8,128)(2,1)S(1)} %collective-permute-done.16.refs_1_.other_ref, bf16[4,256,512]{2,1,0:T(8,128)(2,1)S(1)} %shard_map.67._.refs_0_, ...), custom_call_target="tpu_custom_call" | custom-call | tf_op jit(solution)/shard_map/pallas_call | solution.py:317
  127.7 4.6 %collective-permute-start.20 = (bf16[128,1024]{1,0:T(8,128)(2,1)S(1)}, bf16[128,1024]{1,0:T(8,128)(2,1)S(1)}, u32[]{:S(2)}, u32[]{:S(2)}) collective-permute-start(bf16[128,1024]{1,0:T(8,128)(2,1)S(1)} %shard_map.85), channel_id=1, source_target_pairs={{0,3},{1,2},{2,1},{3,0},{4,7},{5,6},{6,5},{7,4},{8,11},{9,10},{10,... | collective-permute-start | bytes 786440 | tf_op jit(solution)/shard_map/ppermute | solution.py:478
  132.2 2.7 %collective-permute-done.18.other_ref = bf16[128,1024]{1,0:T(8,128)(2,1)S(1)} collective-permute-done((bf16[128,1024]{1,0:T(8,128)(2,1)S(1)}, bf16[128,1024]{1,0:T(8,128)(2,1)S(1)}, u32[]{:S(2)}, u32[]{:S(2)}) %collective-permute-start.18) | collective-permute-done | bytes 262176 | tf_op jit(solution)/shard_map/ppermute | solution.py:472
  137.5 3.3 %collective-permute-done.20.refs_1_.arrived_ref = bf16[128,1024]{1,0:T(8,128)(2,1)S(1)} collective-permute-done((bf16[128,1024]{1,0:T(8,128)(2,1)S(1)}, bf16[128,1024]{1,0:T(8,128)(2,1)S(1)}, u32[]{:S(2)}, u32[]{:S(2)}) %collective-permute-start.20) | collective-permute-done | bytes 262176 | tf_op jit(solution)/shard_map/ppermute | solution.py:478
  140.8 4.7 %collective-permute-start.21 = (bf16[128,1024]{1,0:T(8,128)(2,1)S(1)}, bf16[128,1024]{1,0:T(8,128)(2,1)S(1)}, u32[]{:S(2)}, u32[]{:S(2)}) collective-permute-start(bf16[128,1024]{1,0:T(8,128)(2,1)S(1)} %shard_map.86), channel_id=1, source_target_pairs={{0,3},{1,2},{2,1},{3,0},{4,7},{5,6},{6,5},{7,4},{8,11},{9,10},{10,... | collective-permute-start | bytes 786440 | tf_op jit(solution)/shard_map/ppermute | solution.py:478
  145.5 4.1 %shard_map.87.refs_8_ = bf16[512,1024]{1,0:T(8,128)(2,1)} custom-call(s32[7]{0:T(128)S(1)} %stack.31.where_ref, bf16[128,1024]{1,0:T(8,128)(2,1)S(1)} %shard_map.72.own_ref, bf16[128,1024]{1,0:T(8,128)(2,1)S(1)} %collective-permute-done.7.refs_1_.other_ref, bf16[128,1024]{1,0:T(8,128)(2,1)S(1)} %collective-permute-done.17.refs_1_.arrived_ref, ...), custom_call_target="tpu_custom_call" | custom-call | tf_op jit(solution)/shard_map/pallas_call | solution.py:317
  149.6 3.5 %shard_map.82.kept_ref = f32[128,1024]{1,0:T(8,128)S(1)} custom-call(s32[7]{0:T(128)S(1)} %stack.31.where_ref, bf16[128,1024]{1,0:T(8,128)(2,1)S(1)} %shard_map.81.own_ref, bf16[128,1024]{1,0:T(8,128)(2,1)S(1)} %collective-permute-done.18.other_ref, bf16[4,256,512]{2,1,0:T(8,128)(2,1)S(1)} %shard_map.67._.refs_0_, bf16[4,256,512]{2,1,0:T(8,128)(2,1)} %shard_map.74.refs_1_, ...), custom_call_target="tpu_custom_call" | custom-call | tf_op jit(solution)/shard_map/pallas_call | solution.py:317
  153.1 4.1 %shard_map.88.refs_8_ = bf16[512,1024]{1,0:T(8,128)(2,1)} custom-call(s32[7]{0:T(128)S(1)} %stack.31.where_ref, bf16[128,1024]{1,0:T(8,128)(2,1)S(1)} %shard_map.73.own_ref, bf16[128,1024]{1,0:T(8,128)(2,1)S(1)} %collective-permute-done.8.refs_1_.other_ref, ...), custom_call_target="tpu_custom_call", output_to_operand_aliasing={{}: (12, {})} | custom-call | tf_op jit(solution)/shard_map/pallas_call | solution.py:317
  157.2 4.1 %shard_map.89._ = bf16[512,1024]{1,0:T(8,128)(2,1)} custom-call(s32[7]{0:T(128)S(1)} %stack.31.where_ref, bf16[128,1024]{1,0:T(8,128)(2,1)S(1)} %shard_map.78.own_ref, bf16[128,1024]{1,0:T(8,128)(2,1)S(1)} %collective-permute-done.16.refs_1_.other_ref, ...), custom_call_target="tpu_custom_call", output_to_operand_aliasing={{}: (12, {})} | custom-call | tf_op jit(solution)/shard_map/pallas_call | solution.py:317
  (55 shorter events, 37.8 us)
Async XLA Ops:
  2.9 23.1 %all-to-all-start = ((bf16[64,8,640]{2,1,0:T(8,128)(2,1)}), bf16[64,8,640]{2,1,0:T(8,128)(2,1)S(1)}, u32[]{:S(2)}, u32[]{:S(2)}) async-start(bf16[64,8,640]{2,1,0:T(8,128)(2,1)} %bitcast.9), calls=%async_computation | async-start | bytes 1310720 | tf_op jit(solution)/shard_map/all_to_all | solution.py:412
  11.9 11.7 %collective-permute-start.3 = (bf16[64,512]{1,0:T(8,128)(2,1)S(1)}, bf16[64,512]{1,0:T(8,128)(2,1)S(1)}, u32[]{:S(2)}, u32[]{:S(2)}) collective-permute-start(bf16[64,512]{1,0:T(8,128)(2,1)S(1)} %get-tuple-element.9), channel_id=1, source_target_pairs={{12,0},{76,1},{79,2},{15,3},{8,4},{72,5},{75,6},{11,7},{4,8},{68,9... | collective-permute-start | bytes 196616 | tf_op jit(solution)/shard_map/ppermute | solution.py:341
  12.1 11.5 %collective-permute-start.1 = (bf16[64,512]{1,0:T(8,128)(2,1)S(1)}, bf16[64,512]{1,0:T(8,128)(2,1)S(1)}, u32[]{:S(2)}, u32[]{:S(2)}) collective-permute-start(bf16[64,512]{1,0:T(8,128)(2,1)S(1)} %get-tuple-element.9), channel_id=1, source_target_pairs={{4,0},{68,1},{71,2},{7,3},{0,4},{64,5},{67,6},{3,7},{12,8},{76,9},... | collective-permute-start | bytes 196616 | tf_op jit(solution)/shard_map/ppermute | solution.py:341
  12.6 12.9 %collective-permute-start.2 = (bf16[64,512]{1,0:T(8,128)(2,1)S(1)}, bf16[64,512]{1,0:T(8,128)(2,1)S(1)}, u32[]{:S(2)}, u32[]{:S(2)}) collective-permute-start(bf16[64,512]{1,0:T(8,128)(2,1)S(1)} %get-tuple-element.10), channel_id=1, source_target_pairs={{8,0},{72,1},{75,2},{11,3},{12,4},{76,5},{79,6},{15,7},{0,8},{64,9... | collective-permute-start | bytes 196616 | tf_op jit(solution)/shard_map/ppermute | solution.py:341
  14.2 11.3 %collective-permute-start = (bf16[64,512]{1,0:T(8,128)(2,1)S(1)}, bf16[64,512]{1,0:T(8,128)(2,1)S(1)}, u32[]{:S(2)}, u32[]{:S(2)}) collective-permute-start(bf16[64,512]{1,0:T(8,128)(2,1)S(1)} %get-tuple-element.10), channel_id=1, source_target_pairs={{0,0},{64,1},{67,2},{3,3},{4,4},{68,5},{71,6},{7,7},{8,8},{72,9},{... | collective-permute-start | bytes 196616 | tf_op jit(solution)/shard_map/ppermute | solution.py:341
  29.3 39.9 %all-to-all-start.1 = ((bf16[64,8,640]{2,1,0:T(8,128)(2,1)}), bf16[64,8,640]{2,1,0:T(8,128)(2,1)}, u32[]{:S(2)}, u32[]{:S(2)}) async-start(bf16[64,8,640]{2,1,0:T(8,128)(2,1)} %bitcast.12), calls=%async_computation.1 | async-start | bytes 1310720 | tf_op jit(solution)/shard_map/all_to_all | solution.py:422
  43.6 13.8 %collective-permute-start.6 = (bf16[256,512]{1,0:T(8,128)(2,1)S(1)}, bf16[256,512]{1,0:T(8,128)(2,1)S(1)}, u32[]{:S(2)}, u32[]{:S(2)}) collective-permute-start(bf16[256,512]{1,0:T(8,128)(2,1)S(1)} %shard_map.65.refs_0_), channel_id=1, source_target_pairs={{48,0},{49,1},{50,2},{51,3},{196,4},{197,5},{198,6},{199,7},{56,8}... | collective-permute-start | bytes 786440 | tf_op jit(solution)/shard_map/ppermute | solution.py:341
  45.2 15.5 %collective-permute-start.5 = (bf16[256,512]{1,0:T(8,128)(2,1)S(1)}, bf16[256,512]{1,0:T(8,128)(2,1)S(1)}, u32[]{:S(2)}, u32[]{:S(2)}) collective-permute-start(bf16[256,512]{1,0:T(8,128)(2,1)S(1)} %shard_map.65.refs_0_), channel_id=1, source_target_pairs={{32,0},{33,1},{34,2},{35,3},{132,4},{133,5},{134,6},{135,7},{40,8}... | collective-permute-start | bytes 786440 | tf_op jit(solution)/shard_map/ppermute | solution.py:341
  47.9 12.9 %collective-permute-start.4 = (bf16[256,512]{1,0:T(8,128)(2,1)S(1)}, bf16[256,512]{1,0:T(8,128)(2,1)S(1)}, u32[]{:S(2)}, u32[]{:S(2)}) collective-permute-start(bf16[256,512]{1,0:T(8,128)(2,1)S(1)} %shard_map.65.refs_0_), channel_id=1, source_target_pairs={{16,0},{17,1},{18,2},{19,3},{68,4},{69,5},{70,6},{71,7},{24,8},{25... | collective-permute-start | bytes 786440 | tf_op jit(solution)/shard_map/ppermute | solution.py:341
  61.3 25.9 %collective-permute-start.9 = (bf16[4,256,512]{2,1,0:T(8,128)(2,1)S(1)}, bf16[4,256,512]{2,1,0:T(8,128)(2,1)}, u32[]{:S(2)}, u32[]{:S(2)}) collective-permute-start(bf16[4,256,512]{2,1,0:T(8,128)(2,1)S(1)} %shard_map.67._.refs_0_), channel_id=1, source_target_pairs={{64,0},{65,1},{66,2},{67,3},{20,4},{21,5},{22,6},{23,7},{72,8},{73... | collective-permute-start | bytes 3145736 | tf_op jit(solution)/shard_map/ppermute | solution.py:341
  63.7 23.6 %collective-permute-start.10 = (bf16[4,256,512]{2,1,0:T(8,128)(2,1)S(1)}, bf16[4,256,512]{2,1,0:T(8,128)(2,1)S(1)}, u32[]{:S(2)}, u32[]{:S(2)}) collective-permute-start(bf16[4,256,512]{2,1,0:T(8,128)(2,1)S(1)} %shard_map.67._.refs_0_), channel_id=1, source_target_pairs={{128,0},{129,1},{130,2},{131,3},{36,4},{37,5},{38,6},{39,7},{136,8... | collective-permute-start | bytes 3145736 | tf_op jit(solution)/shard_map/ppermute | solution.py:341
  64.2 27.1 %collective-permute-start.11 = (bf16[4,256,512]{2,1,0:T(8,128)(2,1)S(1)}, bf16[4,256,512]{2,1,0:T(8,128)(2,1)S(1)}, u32[]{:S(2)}, u32[]{:S(2)}) collective-permute-start(bf16[4,256,512]{2,1,0:T(8,128)(2,1)S(1)} %shard_map.67._.refs_0_), channel_id=1, source_target_pairs={{192,0},{193,1},{194,2},{195,3},{52,4},{53,5},{54,6},{55,7},{200,8... | collective-permute-start | bytes 3145736 | tf_op jit(solution)/shard_map/ppermute | solution.py:341
  71.2 16.1 %collective-permute-start.7 = (bf16[128,1024]{1,0:T(8,128)(2,1)S(1)}, bf16[128,1024]{1,0:T(8,128)(2,1)S(1)}, u32[]{:S(2)}, u32[]{:S(2)}) collective-permute-start(bf16[128,1024]{1,0:T(8,128)(2,1)S(1)} %shard_map.72.own_ref), channel_id=1, source_target_pairs={{0,1},{1,0},{2,3},{3,2},{4,5},{5,4},{6,7},{7,6},{8,9},{9,8},{10,11... | collective-permute-start | bytes 786440 | tf_op jit(solution)/shard_map/ppermute | solution.py:453
  72.5 22.0 %collective-permute-start.12 = (bf16[4,256,512]{2,1,0:T(8,128)(2,1)S(1)}, bf16[4,256,512]{2,1,0:T(8,128)(2,1)S(1)}, u32[]{:S(2)}, u32[]{:S(2)}) collective-permute-start(bf16[4,256,512]{2,1,0:T(8,128)(2,1)S(1)} %shard_map.67._.refs_0_), channel_id=1, source_target_pairs={{0,4},{4,0},{1,5},{5,1},{2,6},{6,2},{3,7},{7,3},{8,12},{12,8},{9,1... | collective-permute-start | bytes 3145736 | tf_op jit(solution)/shard_map/ppermute | solution.py:455
  87.3 7.3 %collective-permute-start.13 = (bf16[4,256,512]{2,1,0:T(8,128)(2,1)}, bf16[4,256,512]{2,1,0:T(8,128)(2,1)S(1)}, u32[]{:S(2)}, u32[]{:S(2)}) collective-permute-start(bf16[4,256,512]{2,1,0:T(8,128)(2,1)} %shard_map.74.refs_1_), channel_id=1, source_target_pairs={{0,4},{4,0},{1,5},{5,1},{2,6},{6,2},{3,7},{7,3},{8,12},{12,8},{9,1... | collective-permute-start | bytes 3145736 | tf_op jit(solution)/shard_map/ppermute | solution.py:455
  87.3 7.3 %collective-permute-start.14 = (bf16[4,256,512]{2,1,0:T(8,128)(2,1)S(1)}, bf16[4,256,512]{2,1,0:T(8,128)(2,1)S(1)}, u32[]{:S(2)}, u32[]{:S(2)}) collective-permute-start(bf16[4,256,512]{2,1,0:T(8,128)(2,1)S(1)} %shard_map.75.refs_2_), channel_id=1, source_target_pairs={{0,4},{4,0},{1,5},{5,1},{2,6},{6,2},{3,7},{7,3},{8,12},{12,8},{9,1... | collective-permute-start | bytes 3145736 | tf_op jit(solution)/shard_map/ppermute | solution.py:455
  91.2 3.3 %collective-permute-start.15 = (bf16[4,256,512]{2,1,0:T(8,128)(2,1)S(1)}, bf16[4,256,512]{2,1,0:T(8,128)(2,1)S(1)}, u32[]{:S(2)}, u32[]{:S(2)}) collective-permute-start(bf16[4,256,512]{2,1,0:T(8,128)(2,1)S(1)} %shard_map.76.refs_3_), channel_id=1, source_target_pairs={{0,4},{4,0},{1,5},{5,1},{2,6},{6,2},{3,7},{7,3},{8,12},{12,8},{9,1... | collective-permute-start | bytes 3145736 | tf_op jit(solution)/shard_map/ppermute | solution.py:455
  93.2 13.1 %collective-permute-start.8 = (bf16[128,1024]{1,0:T(8,128)(2,1)S(1)}, bf16[128,1024]{1,0:T(8,128)(2,1)S(1)}, u32[]{:S(2)}, u32[]{:S(2)}) collective-permute-start(bf16[128,1024]{1,0:T(8,128)(2,1)S(1)} %shard_map.73.own_ref), channel_id=1, source_target_pairs={{0,1},{1,0},{2,3},{3,2},{4,5},{5,4},{6,7},{7,6},{8,9},{9,8},{10,11... | collective-permute-start | bytes 786440 | tf_op jit(solution)/shard_map/ppermute | solution.py:472
  97.1 15.2 %collective-permute-start.17 = (bf16[128,1024]{1,0:T(8,128)(2,1)S(1)}, bf16[128,1024]{1,0:T(8,128)(2,1)S(1)}, u32[]{:S(2)}, u32[]{:S(2)}) collective-permute-start(bf16[128,1024]{1,0:T(8,128)(2,1)S(1)} %shard_map.77.refs_2_), channel_id=1, source_target_pairs={{0,3},{1,2},{2,1},{3,0},{4,7},{5,6},{6,5},{7,4},{8,11},{9,10},{10,... | collective-permute-start | bytes 786440 | tf_op jit(solution)/shard_map/ppermute | solution.py:478
  106.3 14.7 %collective-permute-start.16 = (bf16[128,1024]{1,0:T(8,128)(2,1)S(1)}, bf16[128,1024]{1,0:T(8,128)(2,1)S(1)}, u32[]{:S(2)}, u32[]{:S(2)}) collective-permute-start(bf16[128,1024]{1,0:T(8,128)(2,1)S(1)} %shard_map.78.own_ref), channel_id=1, source_target_pairs={{0,1},{1,0},{2,3},{3,2},{4,5},{5,4},{6,7},{7,6},{8,9},{9,8},{10,11... | collective-permute-start | bytes 786440 | tf_op jit(solution)/shard_map/ppermute | solution.py:472
  112.3 15.4 %collective-permute-start.19 = (bf16[128,1024]{1,0:T(8,128)(2,1)S(1)}, bf16[128,1024]{1,0:T(8,128)(2,1)S(1)}, u32[]{:S(2)}, u32[]{:S(2)}) collective-permute-start(bf16[128,1024]{1,0:T(8,128)(2,1)S(1)} %shard_map.80.refs_2_), channel_id=1, source_target_pairs={{0,3},{1,2},{2,1},{3,0},{4,7},{5,6},{6,5},{7,4},{8,11},{9,10},{10,... | collective-permute-start | bytes 786440 | tf_op jit(solution)/shard_map/ppermute | solution.py:478
  121.0 13.9 %collective-permute-start.18 = (bf16[128,1024]{1,0:T(8,128)(2,1)S(1)}, bf16[128,1024]{1,0:T(8,128)(2,1)S(1)}, u32[]{:S(2)}, u32[]{:S(2)}) collective-permute-start(bf16[128,1024]{1,0:T(8,128)(2,1)S(1)} %shard_map.81.own_ref), channel_id=1, source_target_pairs={{0,1},{1,0},{2,3},{3,2},{4,5},{5,4},{6,7},{7,6},{8,9},{9,8},{10,11... | collective-permute-start | bytes 786440 | tf_op jit(solution)/shard_map/ppermute | solution.py:472
  127.7 13.1 %collective-permute-start.20 = (bf16[128,1024]{1,0:T(8,128)(2,1)S(1)}, bf16[128,1024]{1,0:T(8,128)(2,1)S(1)}, u32[]{:S(2)}, u32[]{:S(2)}) collective-permute-start(bf16[128,1024]{1,0:T(8,128)(2,1)S(1)} %shard_map.85), channel_id=1, source_target_pairs={{0,3},{1,2},{2,1},{3,0},{4,7},{5,6},{6,5},{7,4},{8,11},{9,10},{10,... | collective-permute-start | bytes 786440 | tf_op jit(solution)/shard_map/ppermute | solution.py:478
  140.8 20.6 %collective-permute-start.21 = (bf16[128,1024]{1,0:T(8,128)(2,1)S(1)}, bf16[128,1024]{1,0:T(8,128)(2,1)S(1)}, u32[]{:S(2)}, u32[]{:S(2)}) collective-permute-start(bf16[128,1024]{1,0:T(8,128)(2,1)S(1)} %shard_map.86), channel_id=1, source_target_pairs={{0,3},{1,2},{2,1},{3,0},{4,7},{5,6},{6,5},{7,4},{8,11},{9,10},{10,... | collective-permute-start | bytes 786440 | tf_op jit(solution)/shard_map/ppermute | solution.py:478
  (1 other events, 11.9 us)

commit v3 on v2

--- a/solution.py
+++ b/solution.py
@@ -15,7 +15,7 @@
 SLICE = 8
 EXT = DH + 128
 SEQ = ("x", "y", "z", "c")
-CHUNKS = 4
+SIZES_OUT = (128, 192, 192)
 F32 = jnp.float32
 BF16 = jnp.bfloat16
 SCALE = DK ** (-0.5)
@@ -205,8 +205,8 @@
         store.wait()
 
 
-def readout_kernel(start, q_hbm, m_hbm, numer_hbm, terms_hbm, out_ref, *scratch):
-    q_ref, m_ref, numer_ref, terms_ref, sems = scratch
+def readout_kernel(start, q_hbm, m_hbm, numer_hbm, terms_hbm, *refs):
+    out_ref, q_ref, m_ref, numer_ref, terms_ref, sems = refs[-6:]
     mine = pl.ds(start, out_ref.shape[0])
     copies = load(
         (
@@ -309,11 +309,7 @@
     pltpu.async_copy(staged, out_hbm.at[pl.ds(start, staged.shape[0])], sem).wait()
 
 
-def call(kernel, out_shape, *operands, cost_us=None, **kwargs):
-    if cost_us is not None:
-        kwargs["cost_estimate"] = pl.CostEstimate(
-            flops=0, bytes_accessed=int(cost_us * 3.7e6), transcendentals=0
-        )
+def call(kernel, out_shape, *operands, **kwargs):
     return pl.pallas_call(
         kernel,
         out_shape=out_shape,
@@ -415,50 +411,49 @@
         in_specs=[SMEM] + [VMEM] * 4 + [ANY], out_specs=VMEM,
     )
     ring = [group] + [fetch(group, along(False, r)) for r in (1, 2, 3)]
-    entering = call(
-        combine_kernel, shape(T, EXT, BF16), grouped.reshape(T, EXT), group,
-        in_specs=[VMEM, ANY], out_specs=VMEM, cost_us=0.1,
-    )
-    carried = lax.all_to_all(entering.reshape(BLOCKS, SLICE, EXT), SEQ, 0, 0, tiled=True)
-    carried = carried.reshape(T, EXT)
     plane = call(
-        ring_kernel, jax.ShapeDtypeStruct((4, 256, 512), BF16), where, *ring, entering,
-        in_specs=[SMEM] + [VMEM] * 4 + [ANY], out_specs=VMEM, cost_us=20,
+        ring_kernel, jax.ShapeDtypeStruct((4, 256, 512), BF16), where, *ring,
+        in_specs=[SMEM] + [VMEM] * 4, out_specs=VMEM,
     )
     pieces = [plane] + [fetch(plane, along(True, r)) for r in (1, 2, 3)]
     numer, terms = call(
         intra_kernel,
         (pltpu.MemorySpace.HBM((T, 2 * DH), F32), pltpu.MemorySpace.HBM((T, 128), F32)),
-        *pinned(queries, key_rows, value_rows, *gates), plane,
-        in_specs=[HBM] * 5 + [ANY], out_specs=(HBM, HBM), cost_us=0.1,
+        *pinned(queries, key_rows, value_rows, *gates), near[3],
+        in_specs=[HBM] * 5 + [ANY], out_specs=(HBM, HBM),
         scratch_shapes=[
             pltpu.VMEM((T, 2 * DK), BF16), pltpu.VMEM((T, 2 * DK), BF16),
             pltpu.VMEM((T, 2 * DH), BF16), *gate_space,
             pltpu.VMEM((T, 2 * DH), F32), pltpu.VMEM((T, 128), F32), SEM((8,)),
         ],
     )
-
-    size = T // CHUNKS
+    entering = call(
+        combine_kernel, shape(T, EXT, BF16), grouped.reshape(T, EXT), plane, terms,
+        in_specs=[VMEM, ANY, ANY], out_specs=VMEM,
+    )
+    carried = lax.all_to_all(entering.reshape(BLOCKS, SLICE, EXT), SEQ, 0, 0, tiled=True)
+    carried = carried.reshape(T, EXT)
+
+    starts = [sum(SIZES_OUT[:i]) for i in range(len(SIZES_OUT))]
     hiddens = []
-    for i in range(CHUNKS):
+    for start, size in zip(starts, SIZES_OUT):
         hiddens.append(call(
-            functools.partial(readout_kernel, i * size), shape(size, 2 * DH, BF16),
-            *pinned(queries, carried, numer, terms),
-            in_specs=[HBM] * 4, out_specs=VMEM,
+            functools.partial(readout_kernel, start), shape(size, 2 * DH, BF16),
+            *pinned(queries, carried, numer, terms), *hiddens[-1:],
+            in_specs=[HBM] * 4 + [ANY] * min(len(hiddens), 1), out_specs=VMEM,
             scratch_shapes=[
                 pltpu.VMEM((size, 2 * DK), BF16), pltpu.VMEM((T, EXT), BF16),
                 pltpu.VMEM((size, 2 * DH), F32), pltpu.VMEM((size, 128), F32), SEM((4,)),
             ],
         ))
     first = lax.ppermute(hiddens[0], "h", [(j, j ^ 1) for j in range(4)])
-    pieces = pieces[:1] + [order(a, first) for a in pieces[1:]]
+    pieces = pieces[:1] + [order(a, first, hiddens[-1]) for a in pieces[1:]]
     pieces += [lax.ppermute(a, "c", [(0, 1), (1, 0)]) for a in pieces]
     held = [pltpu.VMEM((2, 2, 4, 256, 512), BF16), SEM((4,))]
-    staged = pltpu.VMEM((size, 1024), BF16)
 
     def project(first, dtype, hidden, other, *after):
         return call(
-            functools.partial(project_kernel, first), shape(size, 1024, dtype),
+            functools.partial(project_kernel, first), shape(hidden.shape[0], 1024, dtype),
             where, hidden, other, *pieces, *after,
             in_specs=[SMEM, VMEM, VMEM] + [ANY] * (8 + len(after)), out_specs=VMEM,
             scratch_shapes=held,
@@ -466,23 +461,26 @@
 
     out = None
     others, sends, arrivals = [], [], []
-    for i, hidden in enumerate(hiddens):
-        if i > 0:
-            hidden = order(hidden, others[i - 1], *sends[max(i - 2, 0) : i - 1])
-            other = lax.ppermute(hidden, "h", [(j, j ^ 1) for j in range(4)])
-        else:
-            other = first
-        send = project(3, BF16, hidden, other)
+    for i, start in enumerate(starts):
+        hidden = hiddens[i]
+        other = first if i == 0 else lax.ppermute(hidden, "h", [(j, j ^ 1) for j in range(4)])
+        others.append(other)
+        after = []
+        if i + 1 < len(hiddens):
+            after = [other, *sends[max(i - 1, 0) : i]]
+            hiddens[i + 1] = order(hiddens[i + 1], *after)
+            after = hiddens[i + 1 : i + 2] if i == 0 else []
+        send = project(3, BF16, hidden, other, *after)
         if i > 0:
             send = order(send, arrivals[i - 1])
         arrived = lax.ppermute(send, "h", [(j, 3 - j) for j in range(4)])
-        others.append(other)
         sends.append(send)
         arrivals.append(arrived)
         before = [] if out is None else [out]
-        if i < CHUNKS - 1:
+        staged = pltpu.VMEM((hidden.shape[0], 1024), BF16)
+        if i < len(SIZES_OUT) - 1:
             out = call(
-                functools.partial(finish_kernel, i * size), shape(T, 1024, BF16),
+                functools.partial(finish_kernel, start), shape(T, 1024, BF16),
                 where, hidden, other, arrived, *pieces, *before,
                 in_specs=[SMEM, VMEM, VMEM, VMEM] + [ANY] * 8 + [HBM] * len(before),
                 out_specs=HBM, scratch_shapes=held + [staged],
@@ -490,7 +488,7 @@
             )
         else:
             out = call(
-                functools.partial(add_kernel, i * size), shape(T, 1024, BF16),
+                functools.partial(add_kernel, start), shape(T, 1024, BF16),
                 project(5, F32, hidden, other), arrived, out,
                 in_specs=[VMEM, VMEM, HBM], out_specs=HBM,
                 scratch_shapes=[staged, SEM], input_output_aliases={2: 0},

time: 163 us -> 156 us (0.957)
  Pallas kernels: 46.4 us -> 38.6 us
  starting transfers between devices: 63.7 us -> 56.7 us
  waiting for transfers between devices: 51.7 us -> 58.6 us
    ppermute x10, waiting for transfers between devices: 40.1 us -> 17.6 us  [fetch(): lax.ppermute(a, NAMES, [(index[source_of(*p)], index[p]) for p in places])]
    ppermute x3 -> x2, waiting for transfers between devices: 7.82 us -> 17.8 us  [per_device(): lax.ppermute(hidden, 'h', [(j, j ^ 1) for j in range(4)])]
    all_to_all x1, waiting for transfers between devices: 0.01 us -> 8.55 us  [per_device(): lax.all_to_all(entering.reshape(BLOCKS, SLICE, EXT), SEQ, 0, 0, tiled=True)]
    pallas_call x27 -> x22, Pallas kernels: 46.4 us -> 38.6 us  [call(): pl.pallas_call(kernel, out_shape=out_shape, compiler_params=pltpu.Compile...]
    ppermute x1, waiting for transfers between devices: 0.01 us -> 5.8 us  [per_device(): first = lax.ppermute(hiddens[0], 'h', [(j, j ^ 1) for j in range(4)])]
    ppermute x4 -> x3, starting transfers between devices: 18.1 us -> 12.8 us  [per_device(): arrived = lax.ppermute(send, 'h', [(j, 3 - j) for j in range(4)])]
    ppermute x4 -> x3, waiting for transfers between devices: 3.77 us -> 7.77 us  [per_device(): arrived = lax.ppermute(send, 'h', [(j, 3 - j) for j in range(4)])]
    ppermute x3 -> x2, starting transfers between devices: 8.17 us -> 4.67 us  [per_device(): lax.ppermute(hidden, 'h', [(j, j ^ 1) for j in range(4)])]
  transfers between devices with their start and end apart: 24 -> 22, of which waited for: 11 -> 11; matrix products, arithmetic and copies ran while one was open for 0% -> 0% of each run, Pallas kernels for 24% -> 20%
where the time goes in v3:
time: 156 us; the launch traced here: 154 us
  waiting for transfers between devices  58.6 us (38%)
  starting transfers between devices  56.7 us (36%)
  Pallas kernels  38.6 us (25%)
    pallas_call x22, Pallas kernels, call(): pl.pallas_call(kernel, out_shape=out_shape, compiler_params=pltpu.Compile...  38.6 us
    ppermute x2, waiting for transfers between devices, per_device(): lax.ppermute(hidden, 'h', [(j, j ^ 1) for j in range(4)])  17.8 us
    ppermute x10, waiting for transfers between devices, fetch(): lax.ppermute(a, NAMES, [(index[source_of(*p)], index[p]) for p in places])  17.6 us
    all_to_all x1, starting transfers between devices, per_device(): lax.all_to_all(entering.reshape(BLOCKS, SLICE, EXT), SEQ, 0, 0, tiled=True)  14.3 us
    ppermute x10, starting transfers between devices, fetch(): lax.ppermute(a, NAMES, [(index[source_of(*p)], index[p]) for p in places])  13.1 us
    ppermute x3, starting transfers between devices, per_device(): arrived = lax.ppermute(send, 'h', [(j, 3 - j) for j in range(4)])  12.8 us
    all_to_all x1, starting transfers between devices, per_device(): lax.all_to_all(summary.reshape(BLOCKS, SLICE, EXT), SEQ, 0, 0, tiled=True)  8.96 us
    all_to_all x1, waiting for transfers between devices, per_device(): lax.all_to_all(entering.reshape(BLOCKS, SLICE, EXT), SEQ, 0, 0, tiled=True)  8.55 us
  transfers between devices with their start and end apart: 22, of which 11 were waited for; matrix products, arithmetic and copies ran while one was open for 0% of the time, Pallas kernels for 20%

profile of v3, /device:TPU:32, one launch (start us, length us, event | category | flops | bytes accessed | tf_op | source)
XLA Modules:
  0.0 154.5 jit_solution(15629911262997104567)
XLA Ops:
  0.0 2.9 %shard_map.64.refs_4_ = bf16[512,640]{1,0:T(8,128)(2,1)} custom-call(bf16[512,512]{1,0:T(8,128)(2,1)} %k_hbm.3, bf16[512,1024]{1,0:T(8,128)(2,1)} %v_hbm.3, f32[2,512]{1,0:T(2,128)} %bitcast.16, f32[2,512]{1,0:T(2,128)} %bitcast.18), custom_call_target="tpu_custom_call" | custom-call | tf_op jit(solution)/shard_map/pallas_call | solution.py:313
  2.9 9.0 %all-to-all-start = ((bf16[64,8,640]{2,1,0:T(8,128)(2,1)}), bf16[64,8,640]{2,1,0:T(8,128)(2,1)S(1)}, u32[]{:S(2)}, u32[]{:S(2)}) async-start(bf16[64,8,640]{2,1,0:T(8,128)(2,1)} %bitcast.9), calls=%async_computation | async-start | bytes 1310720 | tf_op jit(solution)/shard_map/all_to_all | solution.py:408
  14.9 8.7 %collective-permute-done.3.refs_3_._ = bf16[64,512]{1,0:T(8,128)(2,1)S(1)} collective-permute-done((bf16[64,512]{1,0:T(8,128)(2,1)S(1)}, bf16[64,512]{1,0:T(8,128)(2,1)S(1)}, u32[]{:S(2)}, u32[]{:S(2)}) %collective-permute-start.3) | collective-permute-done | bytes 65568 | tf_op jit(solution)/shard_map/ppermute | solution.py:337
  27.6 2.7 %collective-permute-start.5 = (bf16[256,512]{1,0:T(8,128)(2,1)S(1)}, bf16[256,512]{1,0:T(8,128)(2,1)S(1)}, u32[]{:S(2)}, u32[]{:S(2)}) collective-permute-start(bf16[256,512]{1,0:T(8,128)(2,1)S(1)} %shard_map.65.refs_0_), channel_id=1, source_target_pairs={{32,0},{33,1},{34,2},{35,3},{132,4},{133,5},{134,6},{135,7},{40,8}... | collective-permute-start | bytes 786440 | tf_op jit(solution)/shard_map/ppermute | solution.py:337
  31.7 4.1 %shard_map.67 = (f32[512,1024]{1,0:T(8,128)}, f32[512,128]{1,0:T(8,128)}) custom-call(bf16[512,512]{1,0:T(8,128)(2,1)} %q_hbm.7, bf16[512,512]{1,0:T(8,128)(2,1)} %k_hbm.3, bf16[512,1024]{1,0:T(8,128)(2,1)} %v_hbm.3, f32[2,512]{1,0:T(2,128)} %bitcast.17, f32[2,512]{1,0:T(2,128)} %bitcast.19, bf16[64,512]{1,0:T(8,128)(2,1)S(1)} %collective-permute-done.3.refs_3_._), custom_call_target="tpu_custom_call" | custom-call | tf_op jit(solution)/shard_map/pallas_call | solution.py:313
  38.0 3.3 %shard_map.68 = bf16[512,640]{1,0:T(8,128)(2,1)} custom-call(bf16[512,640]{1,0:T(8,128)(2,1)S(1)} %bitcast.14, bf16[4,256,512]{2,1,0:T(8,128)(2,1)S(1)} %shard_map.66.refs_0_, f32[512,128]{1,0:T(8,128)S(1)} %copy-done), custom_call_target="tpu_custom_call" | custom-call | tf_op jit(solution)/shard_map/pallas_call | solution.py:313
  41.3 14.3 %all-to-all-start.1 = ((bf16[64,8,640]{2,1,0:T(8,128)(2,1)}), bf16[64,8,640]{2,1,0:T(8,128)(2,1)}, u32[]{:S(2)}, u32[]{:S(2)}) async-start(bf16[64,8,640]{2,1,0:T(8,128)(2,1)} %bitcast.12), calls=%async_computation.1 | async-start | bytes 1310720 | tf_op jit(solution)/shard_map/all_to_all | solution.py:434
  55.6 3.0 %collective-permute-start.9 = (bf16[4,256,512]{2,1,0:T(8,128)(2,1)S(1)}, bf16[4,256,512]{2,1,0:T(8,128)(2,1)}, u32[]{:S(2)}, u32[]{:S(2)}) collective-permute-start(bf16[4,256,512]{2,1,0:T(8,128)(2,1)S(1)} %shard_map.66.refs_0_), channel_id=1, source_target_pairs={{64,0},{65,1},{66,2},{67,3},{20,4},{21,5},{22,6},{23,7},{72,8},{73... | collective-permute-start | bytes 3145736 | tf_op jit(solution)/shard_map/ppermute | solution.py:337
  60.2 8.5 %all-to-all-done.1 = bf16[64,8,640]{2,1,0:T(8,128)(2,1)} async-done(((bf16[64,8,640]{2,1,0:T(8,128)(2,1)}), bf16[64,8,640]{2,1,0:T(8,128)(2,1)}, u32[]{:S(2)}, u32[]{:S(2)}) %all-to-all-start.1) | async-done | bytes 655392 | tf_op jit(solution)/shard_map/all_to_all | solution.py:434
  76.9 5.8 %collective-permute-done.7.refs_1_.other_ref = bf16[128,1024]{1,0:T(8,128)(2,1)S(1)} collective-permute-done((bf16[128,1024]{1,0:T(8,128)(2,1)S(1)}, bf16[128,1024]{1,0:T(8,128)(2,1)S(1)}, u32[]{:S(2)}, u32[]{:S(2)}) %collective-permute-start.7) | collective-permute-done | bytes 262176 | tf_op jit(solution)/shard_map/ppermute | solution.py:449
  83.2 5.5 %collective-permute-done.11.refs_0_ = bf16[4,256,512]{2,1,0:T(8,128)(2,1)S(1)} collective-permute-done((bf16[4,256,512]{2,1,0:T(8,128)(2,1)S(1)}, bf16[4,256,512]{2,1,0:T(8,128)(2,1)S(1)}, u32[]{:S(2)}, u32[]{:S(2)}) %collective-permute-start.11) | collective-permute-done | bytes 1048608 | tf_op jit(solution)/shard_map/ppermute | solution.py:337
  94.6 4.7 %collective-permute-start.17 = (bf16[128,1024]{1,0:T(8,128)(2,1)S(1)}, bf16[128,1024]{1,0:T(8,128)(2,1)S(1)}, u32[]{:S(2)}, u32[]{:S(2)}) collective-permute-start(bf16[128,1024]{1,0:T(8,128)(2,1)S(1)} %shard_map.76.refs_2_), channel_id=1, source_target_pairs={{0,3},{1,2},{2,1},{3,0},{4,7},{5,6},{6,5},{7,4},{8,11},{9,10},{10,... | collective-permute-start | bytes 786440 | tf_op jit(solution)/shard_map/ppermute | solution.py:476
  99.2 8.7 %collective-permute-done.8.refs_1_.other_ref = bf16[192,1024]{1,0:T(8,128)(2,1)S(1)} collective-permute-done((bf16[192,1024]{1,0:T(8,128)(2,1)S(1)}, bf16[192,1024]{1,0:T(8,128)(2,1)S(1)}, u32[]{:S(2)}, u32[]{:S(2)}) %collective-permute-start.8) | collective-permute-done | bytes 393248 | tf_op jit(solution)/shard_map/ppermute | solution.py:466
  107.9 3.4 %collective-permute-start.16 = (bf16[192,1024]{1,0:T(8,128)(2,1)S(1)}, bf16[192,1024]{1,0:T(8,128)(2,1)S(1)}, u32[]{:S(2)}, u32[]{:S(2)}) collective-permute-start(bf16[192,1024]{1,0:T(8,128)(2,1)S(1)} %shard_map.77.own_ref), channel_id=1, source_target_pairs={{0,1},{1,0},{2,3},{3,2},{4,5},{5,4},{6,7},{7,6},{8,9},{9,8},{10,11... | collective-permute-start | bytes 1179656 | tf_op jit(solution)/shard_map/ppermute | solution.py:466
  111.4 2.6 %shard_map.80.refs_0_ = bf16[192,1024]{1,0:T(8,128)(2,1)S(1)} custom-call(s32[7]{0:T(128)S(1)} %stack.31.where_ref, bf16[192,1024]{1,0:T(8,128)(2,1)S(1)} %shard_map.72.refs_8_.own_ref, bf16[192,1024]{1,0:T(8,128)(2,1)S(1)} %collective-permute-done.8.refs_1_.other_ref, bf16[4,256,512]{2,1,0:T(8,128)(2,1)S(1)} %shard_map.66.refs_0_, ...), custom_call_target="tpu_custom_call" | custom-call | tf_op jit(solution)/shard_map/pallas_call | solution.py:313
  114.0 3.4 %collective-permute-start.18 = (bf16[192,1024]{1,0:T(8,128)(2,1)S(1)}, bf16[192,1024]{1,0:T(8,128)(2,1)S(1)}, u32[]{:S(2)}, u32[]{:S(2)}) collective-permute-start(bf16[192,1024]{1,0:T(8,128)(2,1)S(1)} %shard_map.81), channel_id=1, source_target_pairs={{0,3},{1,2},{2,1},{3,0},{4,7},{5,6},{6,5},{7,4},{8,11},{9,10},{10,... | collective-permute-start | bytes 1179656 | tf_op jit(solution)/shard_map/ppermute | solution.py:476
  117.4 9.1 %collective-permute-done.16.other_ref = bf16[192,1024]{1,0:T(8,128)(2,1)S(1)} collective-permute-done((bf16[192,1024]{1,0:T(8,128)(2,1)S(1)}, bf16[192,1024]{1,0:T(8,128)(2,1)S(1)}, u32[]{:S(2)}, u32[]{:S(2)}) %collective-permute-start.16) | collective-permute-done | bytes 393248 | tf_op jit(solution)/shard_map/ppermute | solution.py:466
  126.5 2.6 %shard_map.79.refs_0_ = bf16[192,1024]{1,0:T(8,128)(2,1)S(1)} custom-call(s32[7]{0:T(128)S(1)} %stack.31.where_ref, bf16[192,1024]{1,0:T(8,128)(2,1)S(1)} %shard_map.77.own_ref, bf16[192,1024]{1,0:T(8,128)(2,1)S(1)} %collective-permute-done.16.other_ref, bf16[4,256,512]{2,1,0:T(8,128)(2,1)S(1)} %shard_map.66.refs_0_, ...), custom_call_target="tpu_custom_call" | custom-call | tf_op jit(solution)/shard_map/pallas_call | solution.py:313
  129.1 3.9 %collective-permute-done.18.refs_1_.arrived_ref = bf16[192,1024]{1,0:T(8,128)(2,1)S(1)} collective-permute-done((bf16[192,1024]{1,0:T(8,128)(2,1)S(1)}, bf16[192,1024]{1,0:T(8,128)(2,1)S(1)}, u32[]{:S(2)}, u32[]{:S(2)}) %collective-permute-start.18) | collective-permute-done | bytes 393248 | tf_op jit(solution)/shard_map/ppermute | solution.py:476
  133.0 4.7 %collective-permute-start.19 = (bf16[192,1024]{1,0:T(8,128)(2,1)S(1)}, bf16[192,1024]{1,0:T(8,128)(2,1)S(1)}, u32[]{:S(2)}, u32[]{:S(2)}) collective-permute-start(bf16[192,1024]{1,0:T(8,128)(2,1)S(1)} %shard_map.82), channel_id=1, source_target_pairs={{0,3},{1,2},{2,1},{3,0},{4,7},{5,6},{6,5},{7,4},{8,11},{9,10},{10,... | collective-permute-start | bytes 1179656 | tf_op jit(solution)/shard_map/ppermute | solution.py:476
  137.7 4.1 %shard_map.83.refs_8_ = bf16[512,1024]{1,0:T(8,128)(2,1)} custom-call(s32[7]{0:T(128)S(1)} %stack.31.where_ref, bf16[128,1024]{1,0:T(8,128)(2,1)S(1)} %shard_map.69.refs_0_.own_ref, bf16[128,1024]{1,0:T(8,128)(2,1)S(1)} %collective-permute-done.7.refs_1_.other_ref, bf16[128,1024]{1,0:T(8,128)(2,1)S(1)} %collective-permute-done.17.refs_1_.arrived_ref, ...), custom_call_target="tpu_custom_call" | custom-call | tf_op jit(solution)/shard_map/pallas_call | solution.py:313
  141.9 3.5 %shard_map.78.kept_ref = f32[192,1024]{1,0:T(8,128)S(1)} custom-call(s32[7]{0:T(128)S(1)} %stack.31.where_ref, bf16[192,1024]{1,0:T(8,128)(2,1)S(1)} %shard_map.77.own_ref, bf16[192,1024]{1,0:T(8,128)(2,1)S(1)} %collective-permute-done.16.other_ref, bf16[4,256,512]{2,1,0:T(8,128)(2,1)S(1)} %shard_map.66.refs_0_, bf16[4,256,512]{2,1,0:T(8,128)(2,1)} %shard_map.73.refs_1_, ...), custom_call_target="tpu_custom_call" | custom-call | tf_op jit(solution)/shard_map/pallas_call | solution.py:313
  145.4 4.2 %shard_map.84._ = bf16[512,1024]{1,0:T(8,128)(2,1)} custom-call(s32[7]{0:T(128)S(1)} %stack.31.where_ref, bf16[192,1024]{1,0:T(8,128)(2,1)S(1)} %shard_map.72.refs_8_.own_ref, bf16[192,1024]{1,0:T(8,128)(2,1)S(1)} %collective-permute-done.8.refs_1_.other_ref, ...), custom_call_target="tpu_custom_call", output_to_operand_aliasing={{}: (12, {})} | custom-call | tf_op jit(solution)/shard_map/pallas_call | solution.py:313
  149.6 3.8 %collective-permute-done.19.arrived_ref = bf16[192,1024]{1,0:T(8,128)(2,1)S(1)} collective-permute-done((bf16[192,1024]{1,0:T(8,128)(2,1)S(1)}, bf16[192,1024]{1,0:T(8,128)(2,1)S(1)}, u32[]{:S(2)}, u32[]{:S(2)}) %collective-permute-start.19) | collective-permute-done | bytes 393248 | tf_op jit(solution)/shard_map/ppermute | solution.py:476
  (48 shorter events, 27.4 us)
Async XLA Ops:
  0.0 11.9 %copy-start.1 = (bf16[1024,64]{0,1:T(8,128)(2,1)S(1)}, bf16[1024,64]{0,1:T(8,128)(2,1)}, u32[]{:S(2)}) copy-start(bf16[1024,64]{0,1:T(8,128)(2,1)} %param.11) | copy-start | bytes 393220
  2.9 35.1 %all-to-all-start = ((bf16[64,8,640]{2,1,0:T(8,128)(2,1)}), bf16[64,8,640]{2,1,0:T(8,128)(2,1)S(1)}, u32[]{:S(2)}, u32[]{:S(2)}) async-start(bf16[64,8,640]{2,1,0:T(8,128)(2,1)} %bitcast.9), calls=%async_computation | async-start | bytes 1310720 | tf_op jit(solution)/shard_map/all_to_all | solution.py:408
  11.9 11.7 %collective-permute-start.3 = (bf16[64,512]{1,0:T(8,128)(2,1)S(1)}, bf16[64,512]{1,0:T(8,128)(2,1)S(1)}, u32[]{:S(2)}, u32[]{:S(2)}) collective-permute-start(bf16[64,512]{1,0:T(8,128)(2,1)S(1)} %get-tuple-element.9), channel_id=1, source_target_pairs={{12,0},{76,1},{79,2},{15,3},{8,4},{72,5},{75,6},{11,7},{4,8},{68,9... | collective-permute-start | bytes 196616 | tf_op jit(solution)/shard_map/ppermute | solution.py:337
  12.1 11.5 %collective-permute-start.1 = (bf16[64,512]{1,0:T(8,128)(2,1)S(1)}, bf16[64,512]{1,0:T(8,128)(2,1)S(1)}, u32[]{:S(2)}, u32[]{:S(2)}) collective-permute-start(bf16[64,512]{1,0:T(8,128)(2,1)S(1)} %get-tuple-element.9), channel_id=1, source_target_pairs={{4,0},{68,1},{71,2},{7,3},{0,4},{64,5},{67,6},{3,7},{12,8},{76,9},... | collective-permute-start | bytes 196616 | tf_op jit(solution)/shard_map/ppermute | solution.py:337
  12.6 12.9 %collective-permute-start.2 = (bf16[64,512]{1,0:T(8,128)(2,1)S(1)}, bf16[64,512]{1,0:T(8,128)(2,1)S(1)}, u32[]{:S(2)}, u32[]{:S(2)}) collective-permute-start(bf16[64,512]{1,0:T(8,128)(2,1)S(1)} %get-tuple-element.10), channel_id=1, source_target_pairs={{8,0},{72,1},{75,2},{11,3},{12,4},{76,5},{79,6},{15,7},{0,8},{64,9... | collective-permute-start | bytes 196616 | tf_op jit(solution)/shard_map/ppermute | solution.py:337
  14.2 11.3 %collective-permute-start = (bf16[64,512]{1,0:T(8,128)(2,1)S(1)}, bf16[64,512]{1,0:T(8,128)(2,1)S(1)}, u32[]{:S(2)}, u32[]{:S(2)}) collective-permute-start(bf16[64,512]{1,0:T(8,128)(2,1)S(1)} %get-tuple-element.10), channel_id=1, source_target_pairs={{0,0},{64,1},{67,2},{3,3},{4,4},{68,5},{71,6},{7,7},{8,8},{72,9},{... | collective-permute-start | bytes 196616 | tf_op jit(solution)/shard_map/ppermute | solution.py:337
  26.0 9.8 %collective-permute-start.6 = (bf16[256,512]{1,0:T(8,128)(2,1)S(1)}, bf16[256,512]{1,0:T(8,128)(2,1)S(1)}, u32[]{:S(2)}, u32[]{:S(2)}) collective-permute-start(bf16[256,512]{1,0:T(8,128)(2,1)S(1)} %shard_map.65.refs_0_), channel_id=1, source_target_pairs={{48,0},{49,1},{50,2},{51,3},{196,4},{197,5},{198,6},{199,7},{56,8}... | collective-permute-start | bytes 786440 | tf_op jit(solution)/shard_map/ppermute | solution.py:337
  27.6 9.8 %collective-permute-start.5 = (bf16[256,512]{1,0:T(8,128)(2,1)S(1)}, bf16[256,512]{1,0:T(8,128)(2,1)S(1)}, u32[]{:S(2)}, u32[]{:S(2)}) collective-permute-start(bf16[256,512]{1,0:T(8,128)(2,1)S(1)} %shard_map.65.refs_0_), channel_id=1, source_target_pairs={{32,0},{33,1},{34,2},{35,3},{132,4},{133,5},{134,6},{135,7},{40,8}... | collective-permute-start | bytes 786440 | tf_op jit(solution)/shard_map/ppermute | solution.py:337
  30.2 7.2 %collective-permute-start.4 = (bf16[256,512]{1,0:T(8,128)(2,1)S(1)}, bf16[256,512]{1,0:T(8,128)(2,1)S(1)}, u32[]{:S(2)}, u32[]{:S(2)}) collective-permute-start(bf16[256,512]{1,0:T(8,128)(2,1)S(1)} %shard_map.65.refs_0_), channel_id=1, source_target_pairs={{16,0},{17,1},{18,2},{19,3},{68,4},{69,5},{70,6},{71,7},{24,8},{25... | collective-permute-start | bytes 786440 | tf_op jit(solution)/shard_map/ppermute | solution.py:337
  35.8 2.2 %copy-start = (f32[512,128]{1,0:T(8,128)S(1)}, f32[512,128]{1,0:T(8,128)}, u32[]{:S(2)}) copy-start(f32[512,128]{1,0:T(8,128)} %get-tuple-element.7.refs_1_.terms_hbm) | copy-start | bytes 786436
  41.3 27.4 %all-to-all-start.1 = ((bf16[64,8,640]{2,1,0:T(8,128)(2,1)}), bf16[64,8,640]{2,1,0:T(8,128)(2,1)}, u32[]{:S(2)}, u32[]{:S(2)}) async-start(bf16[64,8,640]{2,1,0:T(8,128)(2,1)} %bitcast.12), calls=%async_computation.1 | async-start | bytes 1310720 | tf_op jit(solution)/shard_map/all_to_all | solution.py:434
  55.6 21.2 %collective-permute-start.9 = (bf16[4,256,512]{2,1,0:T(8,128)(2,1)S(1)}, bf16[4,256,512]{2,1,0:T(8,128)(2,1)}, u32[]{:S(2)}, u32[]{:S(2)}) collective-permute-start(bf16[4,256,512]{2,1,0:T(8,128)(2,1)S(1)} %shard_map.66.refs_0_), channel_id=1, source_target_pairs={{64,0},{65,1},{66,2},{67,3},{20,4},{21,5},{22,6},{23,7},{72,8},{73... | collective-permute-start | bytes 3145736 | tf_op jit(solution)/shard_map/ppermute | solution.py:337
  58.6 24.1 %collective-permute-start.10 = (bf16[4,256,512]{2,1,0:T(8,128)(2,1)S(1)}, bf16[4,256,512]{2,1,0:T(8,128)(2,1)S(1)}, u32[]{:S(2)}, u32[]{:S(2)}) collective-permute-start(bf16[4,256,512]{2,1,0:T(8,128)(2,1)S(1)} %shard_map.66.refs_0_), channel_id=1, source_target_pairs={{128,0},{129,1},{130,2},{131,3},{36,4},{37,5},{38,6},{39,7},{136,8... | collective-permute-start | bytes 3145736 | tf_op jit(solution)/shard_map/ppermute | solution.py:337
  59.3 29.4 %collective-permute-start.11 = (bf16[4,256,512]{2,1,0:T(8,128)(2,1)S(1)}, bf16[4,256,512]{2,1,0:T(8,128)(2,1)S(1)}, u32[]{:S(2)}, u32[]{:S(2)}) collective-permute-start(bf16[4,256,512]{2,1,0:T(8,128)(2,1)S(1)} %shard_map.66.refs_0_), channel_id=1, source_target_pairs={{192,0},{193,1},{194,2},{195,3},{52,4},{53,5},{54,6},{55,7},{200,8... | collective-permute-start | bytes 3145736 | tf_op jit(solution)/shard_map/ppermute | solution.py:337
  70.8 11.9 %collective-permute-start.7 = (bf16[128,1024]{1,0:T(8,128)(2,1)S(1)}, bf16[128,1024]{1,0:T(8,128)(2,1)S(1)}, u32[]{:S(2)}, u32[]{:S(2)}) collective-permute-start(bf16[128,1024]{1,0:T(8,128)(2,1)S(1)} %shard_map.69.refs_0_.own_ref), channel_id=1, source_target_pairs={{0,1},{1,0},{2,3},{3,2},{4,5},{5,4},{6,7},{7,6},{8,9},{9,8},{10,11... | collective-permute-start | bytes 786440 | tf_op jit(solution)/shard_map/ppermute | solution.py:449
  72.1 18.9 %collective-permute-start.12 = (bf16[4,256,512]{2,1,0:T(8,128)(2,1)S(1)}, bf16[4,256,512]{2,1,0:T(8,128)(2,1)S(1)}, u32[]{:S(2)}, u32[]{:S(2)}) collective-permute-start(bf16[4,256,512]{2,1,0:T(8,128)(2,1)S(1)} %shard_map.66.refs_0_), channel_id=1, source_target_pairs={{0,4},{4,0},{1,5},{5,1},{2,6},{6,2},{3,7},{7,3},{8,12},{12,8},{9,1... | collective-permute-start | bytes 3145736 | tf_op jit(solution)/shard_map/ppermute | solution.py:451
  82.7 8.3 %collective-permute-start.13 = (bf16[4,256,512]{2,1,0:T(8,128)(2,1)}, bf16[4,256,512]{2,1,0:T(8,128)(2,1)S(1)}, u32[]{:S(2)}, u32[]{:S(2)}) collective-permute-start(bf16[4,256,512]{2,1,0:T(8,128)(2,1)} %shard_map.73.refs_1_), channel_id=1, source_target_pairs={{0,4},{4,0},{1,5},{5,1},{2,6},{6,2},{3,7},{7,3},{8,12},{12,8},{9,1... | collective-permute-start | bytes 3145736 | tf_op jit(solution)/shard_map/ppermute | solution.py:451
  82.7 8.3 %collective-permute-start.14 = (bf16[4,256,512]{2,1,0:T(8,128)(2,1)S(1)}, bf16[4,256,512]{2,1,0:T(8,128)(2,1)S(1)}, u32[]{:S(2)}, u32[]{:S(2)}) collective-permute-start(bf16[4,256,512]{2,1,0:T(8,128)(2,1)S(1)} %shard_map.74.refs_2_), channel_id=1, source_target_pairs={{0,4},{4,0},{1,5},{5,1},{2,6},{6,2},{3,7},{7,3},{8,12},{12,8},{9,1... | collective-permute-start | bytes 3145736 | tf_op jit(solution)/shard_map/ppermute | solution.py:451
  88.7 3.3 %collective-permute-start.15 = (bf16[4,256,512]{2,1,0:T(8,128)(2,1)S(1)}, bf16[4,256,512]{2,1,0:T(8,128)(2,1)S(1)}, u32[]{:S(2)}, u32[]{:S(2)}) collective-permute-start(bf16[4,256,512]{2,1,0:T(8,128)(2,1)S(1)} %shard_map.75.refs_3_), channel_id=1, source_target_pairs={{0,4},{4,0},{1,5},{5,1},{2,6},{6,2},{3,7},{7,3},{8,12},{12,8},{9,1... | collective-permute-start | bytes 3145736 | tf_op jit(solution)/shard_map/ppermute | solution.py:451
  89.7 18.2 %collective-permute-start.8 = (bf16[192,1024]{1,0:T(8,128)(2,1)S(1)}, bf16[192,1024]{1,0:T(8,128)(2,1)S(1)}, u32[]{:S(2)}, u32[]{:S(2)}) collective-permute-start(bf16[192,1024]{1,0:T(8,128)(2,1)S(1)} %shard_map.72.refs_8_.own_ref), channel_id=1, source_target_pairs={{0,1},{1,0},{2,3},{3,2},{4,5},{5,4},{6,7},{7,6},{8,9},{9,8},{10,11... | collective-permute-start | bytes 1179656 | tf_op jit(solution)/shard_map/ppermute | solution.py:466
  94.6 19.4 %collective-permute-start.17 = (bf16[128,1024]{1,0:T(8,128)(2,1)S(1)}, bf16[128,1024]{1,0:T(8,128)(2,1)S(1)}, u32[]{:S(2)}, u32[]{:S(2)}) collective-permute-start(bf16[128,1024]{1,0:T(8,128)(2,1)S(1)} %shard_map.76.refs_2_), channel_id=1, source_target_pairs={{0,3},{1,2},{2,1},{3,0},{4,7},{5,6},{6,5},{7,4},{8,11},{9,10},{10,... | collective-permute-start | bytes 786440 | tf_op jit(solution)/shard_map/ppermute | solution.py:476
  107.9 18.6 %collective-permute-start.16 = (bf16[192,1024]{1,0:T(8,128)(2,1)S(1)}, bf16[192,1024]{1,0:T(8,128)(2,1)S(1)}, u32[]{:S(2)}, u32[]{:S(2)}) collective-permute-start(bf16[192,1024]{1,0:T(8,128)(2,1)S(1)} %shard_map.77.own_ref), channel_id=1, source_target_pairs={{0,1},{1,0},{2,3},{3,2},{4,5},{5,4},{6,7},{7,6},{8,9},{9,8},{10,11... | collective-permute-start | bytes 1179656 | tf_op jit(solution)/shard_map/ppermute | solution.py:466
  114.0 19.1 %collective-permute-start.18 = (bf16[192,1024]{1,0:T(8,128)(2,1)S(1)}, bf16[192,1024]{1,0:T(8,128)(2,1)S(1)}, u32[]{:S(2)}, u32[]{:S(2)}) collective-permute-start(bf16[192,1024]{1,0:T(8,128)(2,1)S(1)} %shard_map.81), channel_id=1, source_target_pairs={{0,3},{1,2},{2,1},{3,0},{4,7},{5,6},{6,5},{7,4},{8,11},{9,10},{10,... | collective-permute-start | bytes 1179656 | tf_op jit(solution)/shard_map/ppermute | solution.py:476
  133.0 20.5 %collective-permute-start.19 = (bf16[192,1024]{1,0:T(8,128)(2,1)S(1)}, bf16[192,1024]{1,0:T(8,128)(2,1)S(1)}, u32[]{:S(2)}, u32[]{:S(2)}) collective-permute-start(bf16[192,1024]{1,0:T(8,128)(2,1)S(1)} %shard_map.82), channel_id=1, source_target_pairs={{0,3},{1,2},{2,1},{3,0},{4,7},{5,6},{6,5},{7,4},{8,11},{9,10},{10,... | collective-permute-start | bytes 1179656 | tf_op jit(solution)/shard_map/ppermute | solution.py:476

commit v4 on v3

--- a/solution.py
+++ b/solution.py
@@ -15,7 +15,7 @@
 SLICE = 8
 EXT = DH + 128
 SEQ = ("x", "y", "z", "c")
-SIZES_OUT = (128, 192, 192)
+SIZES_OUT = (176, 176, 160)
 F32 = jnp.float32
 BF16 = jnp.bfloat16
 SCALE = DK ** (-0.5)
@@ -405,6 +405,7 @@
             pltpu.VMEM((T, 2 * DK), BF16), pltpu.VMEM((T, 2 * DH), BF16), *gate_space, SEM((4,)),
         ],
     )
+    summary = order(summary, *near)
     grouped = lax.all_to_all(summary.reshape(BLOCKS, SLICE, EXT), SEQ, 0, 0, tiled=True)
     group = call(
         group_kernel, shape(256, 512, BF16), where, *near, summary,
@@ -419,7 +420,7 @@
     numer, terms = call(
         intra_kernel,
         (pltpu.MemorySpace.HBM((T, 2 * DH), F32), pltpu.MemorySpace.HBM((T, 128), F32)),
-        *pinned(queries, key_rows, value_rows, *gates), near[3],
+        *pinned(queries, key_rows, value_rows, *gates), group,
         in_specs=[HBM] * 5 + [ANY], out_specs=(HBM, HBM),
         scratch_shapes=[
             pltpu.VMEM((T, 2 * DK), BF16), pltpu.VMEM((T, 2 * DK), BF16),

time: 156 us -> 158 us (1.013)
  waiting for transfers between devices: 58.6 us -> 62.1 us
  starting transfers between devices: 56.7 us -> 54.1 us
    all_to_all x1, starting transfers between devices: 8.96 us -> 19 us  [per_device(): lax.all_to_all(summary.reshape(BLOCKS, SLICE, EXT), SEQ, 0, 0, tiled=True)]
    all_to_all x1, starting transfers between devices: 14.3 us -> 5.95 us  [per_device(): lax.all_to_all(entering.reshape(BLOCKS, SLICE, EXT), SEQ, 0, 0, tiled=True)]
    ppermute x10, waiting for transfers between devices: 17.6 us -> 12.7 us  [fetch(): lax.ppermute(a, NAMES, [(index[source_of(*p)], index[p]) for p in places])]
    ppermute x1, waiting for transfers between devices: 5.8 us -> 9.75 us  [per_device(): first = lax.ppermute(hiddens[0], 'h', [(j, j ^ 1) for j in range(4)])]
    ppermute x3, waiting for transfers between devices: 7.77 us -> 10.6 us  [per_device(): arrived = lax.ppermute(send, 'h', [(j, 3 - j) for j in range(4)])]
    ppermute x3, starting transfers between devices: 12.8 us -> 10.2 us  [per_device(): arrived = lax.ppermute(send, 'h', [(j, 3 - j) for j in range(4)])]
    ppermute x2, waiting for transfers between devices: 17.8 us -> 20.3 us  [per_device(): lax.ppermute(hidden, 'h', [(j, j ^ 1) for j in range(4)])]
    pallas_call x22 -> x23, Pallas kernels: 38.6 us -> 38.8 us  [call(): pl.pallas_call(kernel, out_shape=out_shape, compiler_params=pltpu.Compile...]
  transfers between devices with their start and end apart: 22 -> 22, of which waited for: 11 -> 15; matrix products, arithmetic and copies ran while one was open for 0% -> 0% of each run, Pallas kernels for 20% -> 22%
where the time goes in v4:
time: 158 us; the launch traced here: 156 us
  waiting for transfers between devices  62.1 us (39%)
  starting transfers between devices  54.1 us (34%)
  Pallas kernels  38.8 us (25%)
    pallas_call x23, Pallas kernels, call(): pl.pallas_call(kernel, out_shape=out_shape, compiler_params=pltpu.Compile...  38.8 us
    ppermute x2, waiting for transfers between devices, per_device(): lax.ppermute(hidden, 'h', [(j, j ^ 1) for j in range(4)])  20.3 us
    all_to_all x1, starting transfers between devices, per_device(): lax.all_to_all(summary.reshape(BLOCKS, SLICE, EXT), SEQ, 0, 0, tiled=True)  19 us
    ppermute x10, starting transfers between devices, fetch(): lax.ppermute(a, NAMES, [(index[source_of(*p)], index[p]) for p in places])  13 us
    ppermute x10, waiting for transfers between devices, fetch(): lax.ppermute(a, NAMES, [(index[source_of(*p)], index[p]) for p in places])  12.7 us
    ppermute x3, waiting for transfers between devices, per_device(): arrived = lax.ppermute(send, 'h', [(j, 3 - j) for j in range(4)])  10.6 us
    ppermute x3, starting transfers between devices, per_device(): arrived = lax.ppermute(send, 'h', [(j, 3 - j) for j in range(4)])  10.2 us
    ppermute x1, waiting for transfers between devices, per_device(): first = lax.ppermute(hiddens[0], 'h', [(j, j ^ 1) for j in range(4)])  9.75 us
  transfers between devices with their start and end apart: 22, of which 15 were waited for; matrix products, arithmetic and copies ran while one was open for 0% of the time, Pallas kernels for 22%

profile of v4, /device:TPU:32, one launch (start us, length us, event | category | flops | bytes accessed | tf_op | source)
XLA Modules:
  0.0 156.4 jit_solution(5887175653861906010)
XLA Ops:
  3.6 2.9 %shard_map.64.refs_0_ = bf16[512,640]{1,0:T(8,128)(2,1)} custom-call(bf16[512,512]{1,0:T(8,128)(2,1)} %k_hbm.3, bf16[512,1024]{1,0:T(8,128)(2,1)} %v_hbm.3, f32[2,512]{1,0:T(2,128)} %bitcast.16, f32[2,512]{1,0:T(2,128)} %bitcast.18), custom_call_target="tpu_custom_call" | custom-call | tf_op jit(solution)/shard_map/pallas_call | solution.py:313
  8.4 19.0 %all-to-all-start = ((bf16[64,8,640]{2,1,0:T(8,128)(2,1)}), bf16[64,8,640]{2,1,0:T(8,128)(2,1)S(1)}, u32[]{:S(2)}, u32[]{:S(2)}) async-start(bf16[64,8,640]{2,1,0:T(8,128)(2,1)} %bitcast.10), calls=%async_computation | async-start | bytes 1310720 | tf_op jit(solution)/shard_map/all_to_all | solution.py:409
  28.0 2.8 %collective-permute-start.4 = (bf16[256,512]{1,0:T(8,128)(2,1)S(1)}, bf16[256,512]{1,0:T(8,128)(2,1)S(1)}, u32[]{:S(2)}, u32[]{:S(2)}) collective-permute-start(bf16[256,512]{1,0:T(8,128)(2,1)S(1)} %shard_map.66.refs_0_._), channel_id=1, source_target_pairs={{16,0},{17,1},{18,2},{19,3},{68,4},{69,5},{70,6},{71,7},{24,8},{25... | collective-permute-start | bytes 786440 | tf_op jit(solution)/shard_map/ppermute | solution.py:337
  32.5 4.1 %shard_map.68 = (f32[512,1024]{1,0:T(8,128)}, f32[512,128]{1,0:T(8,128)}) custom-call(bf16[512,512]{1,0:T(8,128)(2,1)} %q_hbm.7, bf16[512,512]{1,0:T(8,128)(2,1)} %k_hbm.3, bf16[512,1024]{1,0:T(8,128)(2,1)} %v_hbm.3, f32[2,512]{1,0:T(2,128)} %bitcast.17, f32[2,512]{1,0:T(2,128)} %bitcast.19, bf16[256,512]{1,0:T(8,128)(2,1)S(1)} %shard_map.66.refs_0_._), custom_call_target="tpu_custom_call" | custom-call | tf_op jit(solution)/shard_map/pallas_call | solution.py:313
  36.6 3.0 %collective-permute-done.4.refs_1_ = bf16[256,512]{1,0:T(8,128)(2,1)S(1)} collective-permute-done((bf16[256,512]{1,0:T(8,128)(2,1)S(1)}, bf16[256,512]{1,0:T(8,128)(2,1)S(1)}, u32[]{:S(2)}, u32[]{:S(2)}) %collective-permute-start.4) | collective-permute-done | bytes 262176 | tf_op jit(solution)/shard_map/ppermute | solution.py:337
  39.6 3.1 %collective-permute-done.5.refs_2_ = bf16[256,512]{1,0:T(8,128)(2,1)S(1)} collective-permute-done((bf16[256,512]{1,0:T(8,128)(2,1)S(1)}, bf16[256,512]{1,0:T(8,128)(2,1)S(1)}, u32[]{:S(2)}, u32[]{:S(2)}) %collective-permute-start.5) | collective-permute-done | bytes 262176 | tf_op jit(solution)/shard_map/ppermute | solution.py:337
  42.8 2.2 %collective-permute-done.6.refs_3_ = bf16[256,512]{1,0:T(8,128)(2,1)S(1)} collective-permute-done((bf16[256,512]{1,0:T(8,128)(2,1)S(1)}, bf16[256,512]{1,0:T(8,128)(2,1)S(1)}, u32[]{:S(2)}, u32[]{:S(2)}) %collective-permute-start.6) | collective-permute-done | bytes 262176 | tf_op jit(solution)/shard_map/ppermute | solution.py:337
  45.7 3.3 %shard_map.69 = bf16[512,640]{1,0:T(8,128)(2,1)} custom-call(bf16[512,640]{1,0:T(8,128)(2,1)S(1)} %bitcast.14, bf16[4,256,512]{2,1,0:T(8,128)(2,1)S(1)} %shard_map.67.refs_0_, f32[512,128]{1,0:T(8,128)S(1)} %copy-done), custom_call_target="tpu_custom_call" | custom-call | tf_op jit(solution)/shard_map/pallas_call | solution.py:313
  48.9 6.0 %all-to-all-start.1 = ((bf16[64,8,640]{2,1,0:T(8,128)(2,1)}), bf16[64,8,640]{2,1,0:T(8,128)(2,1)}, u32[]{:S(2)}, u32[]{:S(2)}) async-start(bf16[64,8,640]{2,1,0:T(8,128)(2,1)} %bitcast.12), calls=%async_computation.1 | async-start | bytes 1310720 | tf_op jit(solution)/shard_map/all_to_all | solution.py:435
  56.5 2.9 %collective-permute-start.10 = (bf16[4,256,512]{2,1,0:T(8,128)(2,1)S(1)}, bf16[4,256,512]{2,1,0:T(8,128)(2,1)S(1)}, u32[]{:S(2)}, u32[]{:S(2)}) collective-permute-start(bf16[4,256,512]{2,1,0:T(8,128)(2,1)S(1)} %shard_map.67.refs_0_), channel_id=1, source_target_pairs={{128,0},{129,1},{130,2},{131,3},{36,4},{37,5},{38,6},{39,7},{136,8... | collective-permute-start | bytes 3145736 | tf_op jit(solution)/shard_map/ppermute | solution.py:337
  60.7 7.0 %all-to-all-done.1 = bf16[64,8,640]{2,1,0:T(8,128)(2,1)} async-done(((bf16[64,8,640]{2,1,0:T(8,128)(2,1)}), bf16[64,8,640]{2,1,0:T(8,128)(2,1)}, u32[]{:S(2)}, u32[]{:S(2)}) %all-to-all-start.1) | async-done | bytes 655392 | tf_op jit(solution)/shard_map/all_to_all | solution.py:435
  76.8 9.8 %collective-permute-done.7.refs_1_.other_ref = bf16[176,1024]{1,0:T(8,128)(2,1)S(1)} collective-permute-done((bf16[176,1024]{1,0:T(8,128)(2,1)S(1)}, bf16[176,1024]{1,0:T(8,128)(2,1)S(1)}, u32[]{:S(2)}, u32[]{:S(2)}) %collective-permute-start.7) | collective-permute-done | bytes 360480 | tf_op jit(solution)/shard_map/ppermute | solution.py:450
  92.3 3.5 %shard_map.77.refs_2_ = bf16[176,1024]{1,0:T(8,128)(2,1)S(1)} custom-call(s32[7]{0:T(128)S(1)} %stack.31.where_ref, bf16[176,1024]{1,0:T(8,128)(2,1)S(1)} %shard_map.70.refs_0_.own_ref, bf16[176,1024]{1,0:T(8,128)(2,1)S(1)} %collective-permute-done.7.refs_1_.other_ref, bf16[4,256,512]{2,1,0:T(8,128)(2,1)S(1)} %shard_map.67.refs_0_, ...), custom_call_target="tpu_custom_call" | custom-call | tf_op jit(solution)/shard_map/pallas_call | solution.py:313
  95.8 5.5 %collective-permute-start.17 = (bf16[176,1024]{1,0:T(8,128)(2,1)S(1)}, bf16[176,1024]{1,0:T(8,128)(2,1)S(1)}, u32[]{:S(2)}, u32[]{:S(2)}) collective-permute-start(bf16[176,1024]{1,0:T(8,128)(2,1)S(1)} %shard_map.77.refs_2_), channel_id=1, source_target_pairs={{0,3},{1,2},{2,1},{3,0},{4,7},{5,6},{6,5},{7,4},{8,11},{9,10},{10,... | collective-permute-start | bytes 1081352 | tf_op jit(solution)/shard_map/ppermute | solution.py:477
  101.3 5.1 %collective-permute-done.8.refs_1_.other_ref = bf16[176,1024]{1,0:T(8,128)(2,1)S(1)} collective-permute-done((bf16[176,1024]{1,0:T(8,128)(2,1)S(1)}, bf16[176,1024]{1,0:T(8,128)(2,1)S(1)}, u32[]{:S(2)}, u32[]{:S(2)}) %collective-permute-start.8) | collective-permute-done | bytes 360480 | tf_op jit(solution)/shard_map/ppermute | solution.py:467
  106.4 3.5 %shard_map.81.refs_0_ = bf16[176,1024]{1,0:T(8,128)(2,1)S(1)} custom-call(s32[7]{0:T(128)S(1)} %stack.31.where_ref, bf16[176,1024]{1,0:T(8,128)(2,1)S(1)} %shard_map.73.refs_8_.own_ref, bf16[176,1024]{1,0:T(8,128)(2,1)S(1)} %collective-permute-done.8.refs_1_.other_ref, bf16[4,256,512]{2,1,0:T(8,128)(2,1)S(1)} %shard_map.67.refs_0_, ...), custom_call_target="tpu_custom_call" | custom-call | tf_op jit(solution)/shard_map/pallas_call | solution.py:313
  109.9 4.6 %collective-permute-done.17.refs_1_.arrived_ref = bf16[176,1024]{1,0:T(8,128)(2,1)S(1)} collective-permute-done((bf16[176,1024]{1,0:T(8,128)(2,1)S(1)}, bf16[176,1024]{1,0:T(8,128)(2,1)S(1)}, u32[]{:S(2)}, u32[]{:S(2)}) %collective-permute-start.17) | collective-permute-done | bytes 360480 | tf_op jit(solution)/shard_map/ppermute | solution.py:477
  114.5 4.6 %collective-permute-start.18 = (bf16[176,1024]{1,0:T(8,128)(2,1)S(1)}, bf16[176,1024]{1,0:T(8,128)(2,1)S(1)}, u32[]{:S(2)}, u32[]{:S(2)}) collective-permute-start(bf16[176,1024]{1,0:T(8,128)(2,1)S(1)} %shard_map.82), channel_id=1, source_target_pairs={{0,3},{1,2},{2,1},{3,0},{4,7},{5,6},{6,5},{7,4},{8,11},{9,10},{10,... | collective-permute-start | bytes 1081352 | tf_op jit(solution)/shard_map/ppermute | solution.py:477
  121.2 15.2 %collective-permute-done.16.other_ref = bf16[160,1024]{1,0:T(8,128)(2,1)S(1)} collective-permute-done((bf16[160,1024]{1,0:T(8,128)(2,1)S(1)}, bf16[160,1024]{1,0:T(8,128)(2,1)S(1)}, u32[]{:S(2)}, u32[]{:S(2)}) %collective-permute-start.16) | collective-permute-done | bytes 327712 | tf_op jit(solution)/shard_map/ppermute | solution.py:467
  136.3 3.5 %shard_map.80.refs_0_ = bf16[160,1024]{1,0:T(8,128)(2,1)S(1)} custom-call(s32[7]{0:T(128)S(1)} %stack.31.where_ref, bf16[160,1024]{1,0:T(8,128)(2,1)S(1)} %shard_map.78.own_ref, bf16[160,1024]{1,0:T(8,128)(2,1)S(1)} %collective-permute-done.16.other_ref, bf16[4,256,512]{2,1,0:T(8,128)(2,1)S(1)} %shard_map.67.refs_0_, ...), custom_call_target="tpu_custom_call" | custom-call | tf_op jit(solution)/shard_map/pallas_call | solution.py:313
  140.0 2.8 %shard_map.79.kept_ref = f32[160,1024]{1,0:T(8,128)S(1)} custom-call(s32[7]{0:T(128)S(1)} %stack.31.where_ref, bf16[160,1024]{1,0:T(8,128)(2,1)S(1)} %shard_map.78.own_ref, bf16[160,1024]{1,0:T(8,128)(2,1)S(1)} %collective-permute-done.16.other_ref, bf16[4,256,512]{2,1,0:T(8,128)(2,1)S(1)} %shard_map.67.refs_0_, bf16[4,256,512]{2,1,0:T(8,128)(2,1)S(1)} %shard_map.74.refs_1_, ...), custom_call_target="tpu_custom_call" | custom-call | tf_op jit(solution)/shard_map/pallas_call | solution.py:313
  142.8 3.3 %shard_map.84.refs_8_ = bf16[512,1024]{1,0:T(8,128)(2,1)} custom-call(s32[7]{0:T(128)S(1)} %stack.31.where_ref, bf16[176,1024]{1,0:T(8,128)(2,1)S(1)} %shard_map.70.refs_0_.own_ref, bf16[176,1024]{1,0:T(8,128)(2,1)S(1)} %collective-permute-done.7.refs_1_.other_ref, bf16[176,1024]{1,0:T(8,128)(2,1)S(1)} %collective-permute-done.17.refs_1_.arrived_ref, ...), custom_call_target="tpu_custom_call" | custom-call | tf_op jit(solution)/shard_map/pallas_call | solution.py:313
  146.1 3.3 %shard_map.85._ = bf16[512,1024]{1,0:T(8,128)(2,1)} custom-call(s32[7]{0:T(128)S(1)} %stack.31.where_ref, bf16[176,1024]{1,0:T(8,128)(2,1)S(1)} %shard_map.73.refs_8_.own_ref, bf16[176,1024]{1,0:T(8,128)(2,1)S(1)} %collective-permute-done.8.refs_1_.other_ref, ...), custom_call_target="tpu_custom_call", output_to_operand_aliasing={{}: (12, {})} | custom-call | tf_op jit(solution)/shard_map/pallas_call | solution.py:313
  149.5 6.0 %collective-permute-done.19.arrived_ref = bf16[160,1024]{1,0:T(8,128)(2,1)S(1)} collective-permute-done((bf16[160,1024]{1,0:T(8,128)(2,1)S(1)}, bf16[160,1024]{1,0:T(8,128)(2,1)S(1)}, u32[]{:S(2)}, u32[]{:S(2)}) %collective-permute-start.19) | collective-permute-done | bytes 327712 | tf_op jit(solution)/shard_map/ppermute | solution.py:477
  (47 shorter events, 29.1 us)
Async XLA Ops:
  0.9 5.6 %collective-permute-start = (bf16[64,512]{1,0:T(8,128)(2,1)S(1)}, bf16[64,512]{1,0:T(8,128)(2,1)S(1)}, u32[]{:S(2)}, u32[]{:S(2)}) collective-permute-start(bf16[64,512]{1,0:T(8,128)(2,1)S(1)} %get-tuple-element.10), channel_id=1, source_target_pairs={{0,0},{64,1},{67,2},{3,3},{4,4},{68,5},{71,6},{7,7},{8,8},{72,9},{... | collective-permute-start | bytes 196616 | tf_op jit(solution)/shard_map/ppermute | solution.py:337
  1.6 5.0 %collective-permute-start.1 = (bf16[64,512]{1,0:T(8,128)(2,1)S(1)}, bf16[64,512]{1,0:T(8,128)(2,1)S(1)}, u32[]{:S(2)}, u32[]{:S(2)}) collective-permute-start(bf16[64,512]{1,0:T(8,128)(2,1)S(1)} %get-tuple-element.9), channel_id=1, source_target_pairs={{4,0},{68,1},{71,2},{7,3},{0,4},{64,5},{67,6},{3,7},{12,8},{76,9},... | collective-permute-start | bytes 196616 | tf_op jit(solution)/shard_map/ppermute | solution.py:337
  1.7 5.4 %collective-permute-start.2 = (bf16[64,512]{1,0:T(8,128)(2,1)S(1)}, bf16[64,512]{1,0:T(8,128)(2,1)S(1)}, u32[]{:S(2)}, u32[]{:S(2)}) collective-permute-start(bf16[64,512]{1,0:T(8,128)(2,1)S(1)} %get-tuple-element.10), channel_id=1, source_target_pairs={{8,0},{72,1},{75,2},{11,3},{12,4},{76,5},{79,6},{15,7},{0,8},{64,9... | collective-permute-start | bytes 196616 | tf_op jit(solution)/shard_map/ppermute | solution.py:337
  3.6 4.8 %collective-permute-start.3 = (bf16[64,512]{1,0:T(8,128)(2,1)S(1)}, bf16[64,512]{1,0:T(8,128)(2,1)S(1)}, u32[]{:S(2)}, u32[]{:S(2)}) collective-permute-start(bf16[64,512]{1,0:T(8,128)(2,1)S(1)} %get-tuple-element.9), channel_id=1, source_target_pairs={{12,0},{76,1},{79,2},{15,3},{8,4},{72,5},{75,6},{11,7},{4,8},{68,9... | collective-permute-start | bytes 196616 | tf_op jit(solution)/shard_map/ppermute | solution.py:337
  8.4 37.3 %all-to-all-start = ((bf16[64,8,640]{2,1,0:T(8,128)(2,1)}), bf16[64,8,640]{2,1,0:T(8,128)(2,1)S(1)}, u32[]{:S(2)}, u32[]{:S(2)}) async-start(bf16[64,8,640]{2,1,0:T(8,128)(2,1)} %bitcast.10), calls=%async_computation | async-start | bytes 1310720 | tf_op jit(solution)/shard_map/all_to_all | solution.py:409
  28.0 11.6 %collective-permute-start.4 = (bf16[256,512]{1,0:T(8,128)(2,1)S(1)}, bf16[256,512]{1,0:T(8,128)(2,1)S(1)}, u32[]{:S(2)}, u32[]{:S(2)}) collective-permute-start(bf16[256,512]{1,0:T(8,128)(2,1)S(1)} %shard_map.66.refs_0_._), channel_id=1, source_target_pairs={{16,0},{17,1},{18,2},{19,3},{68,4},{69,5},{70,6},{71,7},{24,8},{25... | collective-permute-start | bytes 786440 | tf_op jit(solution)/shard_map/ppermute | solution.py:337
  30.8 12.0 %collective-permute-start.5 = (bf16[256,512]{1,0:T(8,128)(2,1)S(1)}, bf16[256,512]{1,0:T(8,128)(2,1)S(1)}, u32[]{:S(2)}, u32[]{:S(2)}) collective-permute-start(bf16[256,512]{1,0:T(8,128)(2,1)S(1)} %shard_map.66.refs_0_._), channel_id=1, source_target_pairs={{32,0},{33,1},{34,2},{35,3},{132,4},{133,5},{134,6},{135,7},{40,8}... | collective-permute-start | bytes 786440 | tf_op jit(solution)/shard_map/ppermute | solution.py:337
  31.6 13.4 %collective-permute-start.6 = (bf16[256,512]{1,0:T(8,128)(2,1)S(1)}, bf16[256,512]{1,0:T(8,128)(2,1)S(1)}, u32[]{:S(2)}, u32[]{:S(2)}) collective-permute-start(bf16[256,512]{1,0:T(8,128)(2,1)S(1)} %shard_map.66.refs_0_._), channel_id=1, source_target_pairs={{48,0},{49,1},{50,2},{51,3},{196,4},{197,5},{198,6},{199,7},{56,8}... | collective-permute-start | bytes 786440 | tf_op jit(solution)/shard_map/ppermute | solution.py:337
  36.6 9.1 %copy-start = (f32[512,128]{1,0:T(8,128)S(1)}, f32[512,128]{1,0:T(8,128)}, u32[]{:S(2)}) copy-start(f32[512,128]{1,0:T(8,128)} %get-tuple-element.7.refs_1_.terms_hbm) | copy-start | bytes 786436
  48.9 18.8 %all-to-all-start.1 = ((bf16[64,8,640]{2,1,0:T(8,128)(2,1)}), bf16[64,8,640]{2,1,0:T(8,128)(2,1)}, u32[]{:S(2)}, u32[]{:S(2)}) async-start(bf16[64,8,640]{2,1,0:T(8,128)(2,1)} %bitcast.12), calls=%async_computation.1 | async-start | bytes 1310720 | tf_op jit(solution)/shard_map/all_to_all | solution.py:435
  54.9 21.9 %collective-permute-start.11 = (bf16[4,256,512]{2,1,0:T(8,128)(2,1)S(1)}, bf16[4,256,512]{2,1,0:T(8,128)(2,1)}, u32[]{:S(2)}, u32[]{:S(2)}) collective-permute-start(bf16[4,256,512]{2,1,0:T(8,128)(2,1)S(1)} %shard_map.67.refs_0_), channel_id=1, source_target_pairs={{192,0},{193,1},{194,2},{195,3},{52,4},{53,5},{54,6},{55,7},{200,8... | collective-permute-start | bytes 3145736 | tf_op jit(solution)/shard_map/ppermute | solution.py:337
  56.5 31.7 %collective-permute-start.10 = (bf16[4,256,512]{2,1,0:T(8,128)(2,1)S(1)}, bf16[4,256,512]{2,1,0:T(8,128)(2,1)S(1)}, u32[]{:S(2)}, u32[]{:S(2)}) collective-permute-start(bf16[4,256,512]{2,1,0:T(8,128)(2,1)S(1)} %shard_map.67.refs_0_), channel_id=1, source_target_pairs={{128,0},{129,1},{130,2},{131,3},{36,4},{37,5},{38,6},{39,7},{136,8... | collective-permute-start | bytes 3145736 | tf_op jit(solution)/shard_map/ppermute | solution.py:337
  59.3 28.9 %collective-permute-start.9 = (bf16[4,256,512]{2,1,0:T(8,128)(2,1)S(1)}, bf16[4,256,512]{2,1,0:T(8,128)(2,1)S(1)}, u32[]{:S(2)}, u32[]{:S(2)}) collective-permute-start(bf16[4,256,512]{2,1,0:T(8,128)(2,1)S(1)} %shard_map.67.refs_0_), channel_id=1, source_target_pairs={{64,0},{65,1},{66,2},{67,3},{20,4},{21,5},{22,6},{23,7},{72,8},{73... | collective-permute-start | bytes 3145736 | tf_op jit(solution)/shard_map/ppermute | solution.py:337
  70.0 16.6 %collective-permute-start.7 = (bf16[176,1024]{1,0:T(8,128)(2,1)S(1)}, bf16[176,1024]{1,0:T(8,128)(2,1)S(1)}, u32[]{:S(2)}, u32[]{:S(2)}) collective-permute-start(bf16[176,1024]{1,0:T(8,128)(2,1)S(1)} %shard_map.70.refs_0_.own_ref), channel_id=1, source_target_pairs={{0,1},{1,0},{2,3},{3,2},{4,5},{5,4},{6,7},{7,6},{8,9},{9,8},{10,11... | collective-permute-start | bytes 1081352 | tf_op jit(solution)/shard_map/ppermute | solution.py:450
  71.5 19.1 %collective-permute-start.12 = (bf16[4,256,512]{2,1,0:T(8,128)(2,1)S(1)}, bf16[4,256,512]{2,1,0:T(8,128)(2,1)S(1)}, u32[]{:S(2)}, u32[]{:S(2)}) collective-permute-start(bf16[4,256,512]{2,1,0:T(8,128)(2,1)S(1)} %shard_map.67.refs_0_), channel_id=1, source_target_pairs={{0,4},{4,0},{1,5},{5,1},{2,6},{6,2},{3,7},{7,3},{8,12},{12,8},{9,1... | collective-permute-start | bytes 3145736 | tf_op jit(solution)/shard_map/ppermute | solution.py:452
  86.6 4.0 %collective-permute-start.15 = (bf16[4,256,512]{2,1,0:T(8,128)(2,1)}, bf16[4,256,512]{2,1,0:T(8,128)(2,1)S(1)}, u32[]{:S(2)}, u32[]{:S(2)}) collective-permute-start(bf16[4,256,512]{2,1,0:T(8,128)(2,1)} %shard_map.76.refs_3_), channel_id=1, source_target_pairs={{0,4},{4,0},{1,5},{5,1},{2,6},{6,2},{3,7},{7,3},{8,12},{12,8},{9,1... | collective-permute-start | bytes 3145736 | tf_op jit(solution)/shard_map/ppermute | solution.py:452
  88.1 2.7 %collective-permute-start.14 = (bf16[4,256,512]{2,1,0:T(8,128)(2,1)S(1)}, bf16[4,256,512]{2,1,0:T(8,128)(2,1)S(1)}, u32[]{:S(2)}, u32[]{:S(2)}) collective-permute-start(bf16[4,256,512]{2,1,0:T(8,128)(2,1)S(1)} %shard_map.75.refs_2_), channel_id=1, source_target_pairs={{0,4},{4,0},{1,5},{5,1},{2,6},{6,2},{3,7},{7,3},{8,12},{12,8},{9,1... | collective-permute-start | bytes 3145736 | tf_op jit(solution)/shard_map/ppermute | solution.py:452
  88.3 4.0 %collective-permute-start.13 = (bf16[4,256,512]{2,1,0:T(8,128)(2,1)S(1)}, bf16[4,256,512]{2,1,0:T(8,128)(2,1)S(1)}, u32[]{:S(2)}, u32[]{:S(2)}) collective-permute-start(bf16[4,256,512]{2,1,0:T(8,128)(2,1)S(1)} %shard_map.74.refs_1_), channel_id=1, source_target_pairs={{0,4},{4,0},{1,5},{5,1},{2,6},{6,2},{3,7},{7,3},{8,12},{12,8},{9,1... | collective-permute-start | bytes 3145736 | tf_op jit(solution)/shard_map/ppermute | solution.py:452
  88.7 17.7 %collective-permute-start.8 = (bf16[176,1024]{1,0:T(8,128)(2,1)S(1)}, bf16[176,1024]{1,0:T(8,128)(2,1)S(1)}, u32[]{:S(2)}, u32[]{:S(2)}) collective-permute-start(bf16[176,1024]{1,0:T(8,128)(2,1)S(1)} %shard_map.73.refs_8_.own_ref), channel_id=1, source_target_pairs={{0,1},{1,0},{2,3},{3,2},{4,5},{5,4},{6,7},{7,6},{8,9},{9,8},{10,11... | collective-permute-start | bytes 1081352 | tf_op jit(solution)/shard_map/ppermute | solution.py:467
  95.8 18.7 %collective-permute-start.17 = (bf16[176,1024]{1,0:T(8,128)(2,1)S(1)}, bf16[176,1024]{1,0:T(8,128)(2,1)S(1)}, u32[]{:S(2)}, u32[]{:S(2)}) collective-permute-start(bf16[176,1024]{1,0:T(8,128)(2,1)S(1)} %shard_map.77.refs_2_), channel_id=1, source_target_pairs={{0,3},{1,2},{2,1},{3,0},{4,7},{5,6},{6,5},{7,4},{8,11},{9,10},{10,... | collective-permute-start | bytes 1081352 | tf_op jit(solution)/shard_map/ppermute | solution.py:477
  114.5 25.4 %collective-permute-start.18 = (bf16[176,1024]{1,0:T(8,128)(2,1)S(1)}, bf16[176,1024]{1,0:T(8,128)(2,1)S(1)}, u32[]{:S(2)}, u32[]{:S(2)}) collective-permute-start(bf16[176,1024]{1,0:T(8,128)(2,1)S(1)} %shard_map.82), channel_id=1, source_target_pairs={{0,3},{1,2},{2,1},{3,0},{4,7},{5,6},{6,5},{7,4},{8,11},{9,10},{10,... | collective-permute-start | bytes 1081352 | tf_op jit(solution)/shard_map/ppermute | solution.py:477
  119.1 17.2 %collective-permute-start.16 = (bf16[160,1024]{1,0:T(8,128)(2,1)S(1)}, bf16[160,1024]{1,0:T(8,128)(2,1)S(1)}, u32[]{:S(2)}, u32[]{:S(2)}) collective-permute-start(bf16[160,1024]{1,0:T(8,128)(2,1)S(1)} %shard_map.78.own_ref), channel_id=1, source_target_pairs={{0,1},{1,0},{2,3},{3,2},{4,5},{5,4},{6,7},{7,6},{8,9},{9,8},{10,11... | collective-permute-start | bytes 983048 | tf_op jit(solution)/shard_map/ppermute | solution.py:467
  139.9 15.6 %collective-permute-start.19 = (bf16[160,1024]{1,0:T(8,128)(2,1)S(1)}, bf16[160,1024]{1,0:T(8,128)(2,1)S(1)}, u32[]{:S(2)}, u32[]{:S(2)}) collective-permute-start(bf16[160,1024]{1,0:T(8,128)(2,1)S(1)} %shard_map.83), channel_id=1, source_target_pairs={{0,3},{1,2},{2,1},{3,0},{4,7},{5,6},{6,5},{7,4},{8,11},{9,10},{10,... | collective-permute-start | bytes 983048 | tf_op jit(solution)/shard_map/ppermute | solution.py:477

commit v5 on v3

--- a/solution.py
+++ b/solution.py
@@ -15,7 +15,7 @@
 SLICE = 8
 EXT = DH + 128
 SEQ = ("x", "y", "z", "c")
-SIZES_OUT = (128, 192, 192)
+SIZES_OUT = (144, 192, 176)
 F32 = jnp.float32
 BF16 = jnp.bfloat16
 SCALE = DK ** (-0.5)
@@ -447,7 +447,10 @@
             ],
         ))
     first = lax.ppermute(hiddens[0], "h", [(j, j ^ 1) for j in range(4)])
-    pieces = pieces[:1] + [order(a, first, hiddens[-1]) for a in pieces[1:]]
+    pieces = [
+        pieces[0], order(pieces[1], hiddens[-1]), order(pieces[2], first, hiddens[-1]),
+        order(pieces[3], hiddens[-1]),
+    ]
     pieces += [lax.ppermute(a, "c", [(0, 1), (1, 0)]) for a in pieces]
     held = [pltpu.VMEM((2, 2, 4, 256, 512), BF16), SEM((4,))]
 

time: 156 us -> 159 us (1.019)
  waiting for transfers between devices: 58.6 us -> 75.6 us
  starting transfers between devices: 56.7 us -> 43.3 us
    ppermute x2, waiting for transfers between devices: 17.8 us -> 28.9 us  [per_device(): lax.ppermute(hidden, 'h', [(j, j ^ 1) for j in range(4)])]
    ppermute x10, waiting for transfers between devices: 17.6 us -> 27.7 us  [fetch(): lax.ppermute(a, NAMES, [(index[source_of(*p)], index[p]) for p in places])]
    ppermute x3, starting transfers between devices: 12.8 us -> 6.58 us  [per_device(): arrived = lax.ppermute(send, 'h', [(j, 3 - j) for j in range(4)])]
    ppermute x1, waiting for transfers between devices: 5.8 us -> 0.01 us  [per_device(): first = lax.ppermute(hiddens[0], 'h', [(j, j ^ 1) for j in range(4)])]
    ppermute x2, starting transfers between devices: 4.67 us -> 0.01 us  [per_device(): lax.ppermute(hidden, 'h', [(j, j ^ 1) for j in range(4)])]
  transfers between devices with their start and end apart: 22 -> 22, of which waited for: 11 -> 13; matrix products, arithmetic and copies ran while one was open for 0% -> 0% of each run, Pallas kernels for 20% -> 20%
where the time goes in v5:
time: 159 us; the launch traced here: 158 us
  waiting for transfers between devices  75.6 us (48%)
  starting transfers between devices  43.3 us (27%)
  Pallas kernels  38.8 us (24%)
    pallas_call x22, Pallas kernels, call(): pl.pallas_call(kernel, out_shape=out_shape, compiler_params=pltpu.Compile...  38.8 us
    ppermute x2, waiting for transfers between devices, per_device(): lax.ppermute(hidden, 'h', [(j, j ^ 1) for j in range(4)])  28.9 us
    ppermute x10, waiting for transfers between devices, fetch(): lax.ppermute(a, NAMES, [(index[source_of(*p)], index[p]) for p in places])  27.7 us
    all_to_all x1, starting transfers between devices, per_device(): lax.all_to_all(entering.reshape(BLOCKS, SLICE, EXT), SEQ, 0, 0, tiled=True)  14.3 us
    ppermute x10, starting transfers between devices, fetch(): lax.ppermute(a, NAMES, [(index[source_of(*p)], index[p]) for p in places])  12.6 us
    all_to_all x1, starting transfers between devices, per_device(): lax.all_to_all(summary.reshape(BLOCKS, SLICE, EXT), SEQ, 0, 0, tiled=True)  8.96 us
    ppermute x3, waiting for transfers between devices, per_device(): arrived = lax.ppermute(send, 'h', [(j, 3 - j) for j in range(4)])  8.77 us
    all_to_all x1, waiting for transfers between devices, per_device(): lax.all_to_all(entering.reshape(BLOCKS, SLICE, EXT), SEQ, 0, 0, tiled=True)  7.64 us
  transfers between devices with their start and end apart: 22, of which 13 were waited for; matrix products, arithmetic and copies ran while one was open for 0% of the time, Pallas kernels for 20%

profile of v5, /device:TPU:32, one launch (start us, length us, event | category | flops | bytes accessed | tf_op | source)
XLA Modules:
  0.0 158.2 jit_solution(18388391243279069002)
XLA Ops:
  0.0 2.9 %shard_map.64.refs_4_ = bf16[512,640]{1,0:T(8,128)(2,1)} custom-call(bf16[512,512]{1,0:T(8,128)(2,1)} %k_hbm.3, bf16[512,1024]{1,0:T(8,128)(2,1)} %v_hbm.3, f32[2,512]{1,0:T(2,128)} %bitcast.16, f32[2,512]{1,0:T(2,128)} %bitcast.18), custom_call_target="tpu_custom_call" | custom-call | tf_op jit(solution)/shard_map/pallas_call | solution.py:313
  2.9 9.0 %all-to-all-start = ((bf16[64,8,640]{2,1,0:T(8,128)(2,1)}), bf16[64,8,640]{2,1,0:T(8,128)(2,1)S(1)}, u32[]{:S(2)}, u32[]{:S(2)}) async-start(bf16[64,8,640]{2,1,0:T(8,128)(2,1)} %bitcast.9), calls=%async_computation | async-start | bytes 1310720 | tf_op jit(solution)/shard_map/all_to_all | solution.py:408
  15.0 8.4 %collective-permute-done.3.refs_3_._ = bf16[64,512]{1,0:T(8,128)(2,1)S(1)} collective-permute-done((bf16[64,512]{1,0:T(8,128)(2,1)S(1)}, bf16[64,512]{1,0:T(8,128)(2,1)S(1)}, u32[]{:S(2)}, u32[]{:S(2)}) %collective-permute-start.3) | collective-permute-done | bytes 65568 | tf_op jit(solution)/shard_map/ppermute | solution.py:337
  25.4 2.8 %collective-permute-start.4 = (bf16[256,512]{1,0:T(8,128)(2,1)S(1)}, bf16[256,512]{1,0:T(8,128)(2,1)S(1)}, u32[]{:S(2)}, u32[]{:S(2)}) collective-permute-start(bf16[256,512]{1,0:T(8,128)(2,1)S(1)} %shard_map.65.refs_0_), channel_id=1, source_target_pairs={{16,0},{17,1},{18,2},{19,3},{68,4},{69,5},{70,6},{71,7},{24,8},{25... | collective-permute-start | bytes 786440 | tf_op jit(solution)/shard_map/ppermute | solution.py:337
  29.8 4.1 %shard_map.67 = (f32[512,1024]{1,0:T(8,128)}, f32[512,128]{1,0:T(8,128)}) custom-call(bf16[512,512]{1,0:T(8,128)(2,1)} %q_hbm.7, bf16[512,512]{1,0:T(8,128)(2,1)} %k_hbm.3, bf16[512,1024]{1,0:T(8,128)(2,1)} %v_hbm.3, f32[2,512]{1,0:T(2,128)} %bitcast.17, f32[2,512]{1,0:T(2,128)} %bitcast.19, bf16[64,512]{1,0:T(8,128)(2,1)S(1)} %collective-permute-done.3.refs_3_._), custom_call_target="tpu_custom_call" | custom-call | tf_op jit(solution)/shard_map/pallas_call | solution.py:313
  36.1 2.7 %collective-permute-done.6.refs_3_ = bf16[256,512]{1,0:T(8,128)(2,1)S(1)} collective-permute-done((bf16[256,512]{1,0:T(8,128)(2,1)S(1)}, bf16[256,512]{1,0:T(8,128)(2,1)S(1)}, u32[]{:S(2)}, u32[]{:S(2)}) %collective-permute-start.6) | collective-permute-done | bytes 262176 | tf_op jit(solution)/shard_map/ppermute | solution.py:337
  39.5 3.3 %shard_map.68 = bf16[512,640]{1,0:T(8,128)(2,1)} custom-call(bf16[512,640]{1,0:T(8,128)(2,1)S(1)} %bitcast.14, bf16[4,256,512]{2,1,0:T(8,128)(2,1)S(1)} %shard_map.66.refs_0_, f32[512,128]{1,0:T(8,128)S(1)} %copy-done), custom_call_target="tpu_custom_call" | custom-call | tf_op jit(solution)/shard_map/pallas_call | solution.py:313
  42.8 14.3 %all-to-all-start.1 = ((bf16[64,8,640]{2,1,0:T(8,128)(2,1)}), bf16[64,8,640]{2,1,0:T(8,128)(2,1)}, u32[]{:S(2)}, u32[]{:S(2)}) async-start(bf16[64,8,640]{2,1,0:T(8,128)(2,1)} %bitcast.12), calls=%async_computation.1 | async-start | bytes 1310720 | tf_op jit(solution)/shard_map/all_to_all | solution.py:434
  62.3 7.6 %all-to-all-done.1 = bf16[64,8,640]{2,1,0:T(8,128)(2,1)} async-done(((bf16[64,8,640]{2,1,0:T(8,128)(2,1)}), bf16[64,8,640]{2,1,0:T(8,128)(2,1)}, u32[]{:S(2)}, u32[]{:S(2)}) %all-to-all-start.1) | async-done | bytes 655392 | tf_op jit(solution)/shard_map/all_to_all | solution.py:434
  72.1 2.4 %shard_map.70.refs_0_ = bf16[192,1024]{1,0:T(8,128)(2,1)S(1)} custom-call(bf16[512,512]{1,0:T(8,128)(2,1)} %q_hbm.7, bf16[512,640]{1,0:T(8,128)(2,1)} %bitcast.13.m_hbm, f32[512,1024]{1,0:T(8,128)} %get-tuple-element.8.numer_hbm, f32[512,128]{1,0:T(8,128)} %get-tuple-element.7.refs_1_.terms_hbm, bf16[144,1024]{1,0:T(8,128)(2,1)S(1)} %shard_map.69.refs_0_.own_ref), custom_call_target="tpu_custom_call" | custom-call | tf_op jit(solution)/shard_map/pallas_call | solution.py:313
  74.5 2.2 %shard_map.71.refs_1_.refs_2_.refs_0_ = bf16[176,1024]{1,0:T(8,128)(2,1)S(1)} custom-call(bf16[512,512]{1,0:T(8,128)(2,1)} %q_hbm.7, bf16[512,640]{1,0:T(8,128)(2,1)} %bitcast.13.m_hbm, f32[512,1024]{1,0:T(8,128)} %get-tuple-element.8.numer_hbm, f32[512,128]{1,0:T(8,128)} %get-tuple-element.7.refs_1_.terms_hbm, bf16[192,1024]{1,0:T(8,128)(2,1)S(1)} %shard_map.70.refs_0_), custom_call_target="tpu_custom_call" | custom-call | tf_op jit(solution)/shard_map/pallas_call | solution.py:313
  76.7 2.3 %collective-permute-done.11.refs_0_ = bf16[4,256,512]{2,1,0:T(8,128)(2,1)} collective-permute-done((bf16[4,256,512]{2,1,0:T(8,128)(2,1)S(1)}, bf16[4,256,512]{2,1,0:T(8,128)(2,1)}, u32[]{:S(2)}, u32[]{:S(2)}) %collective-permute-start.11) | collective-permute-done | bytes 1048608 | tf_op jit(solution)/shard_map/ppermute | solution.py:337
  79.5 10.8 %collective-permute-done.10.refs_0_ = bf16[4,256,512]{2,1,0:T(8,128)(2,1)S(1)} collective-permute-done((bf16[4,256,512]{2,1,0:T(8,128)(2,1)S(1)}, bf16[4,256,512]{2,1,0:T(8,128)(2,1)S(1)}, u32[]{:S(2)}, u32[]{:S(2)}) %collective-permute-start.10) | collective-permute-done | bytes 1048608 | tf_op jit(solution)/shard_map/ppermute | solution.py:337
  90.4 2.5 %collective-permute-done.14.refs_6_ = bf16[4,256,512]{2,1,0:T(8,128)(2,1)S(1)} collective-permute-done((bf16[4,256,512]{2,1,0:T(8,128)(2,1)S(1)}, bf16[4,256,512]{2,1,0:T(8,128)(2,1)S(1)}, u32[]{:S(2)}, u32[]{:S(2)}) %collective-permute-start.14) | collective-permute-done | bytes 1048608 | tf_op jit(solution)/shard_map/ppermute | solution.py:454
  93.0 3.5 %shard_map.76.refs_2_ = bf16[144,1024]{1,0:T(8,128)(2,1)S(1)} custom-call(s32[7]{0:T(128)S(1)} %stack.31.where_ref, bf16[144,1024]{1,0:T(8,128)(2,1)S(1)} %shard_map.69.refs_0_.own_ref, bf16[144,1024]{1,0:T(8,128)(2,1)S(1)} %collective-permute-done.7.refs_1_.other_ref, bf16[4,256,512]{2,1,0:T(8,128)(2,1)S(1)} %shard_map.66.refs_0_, ...), custom_call_target="tpu_custom_call" | custom-call | tf_op jit(solution)/shard_map/pallas_call | solution.py:313
  98.3 9.7 %collective-permute-done.8.refs_1_.other_ref = bf16[192,1024]{1,0:T(8,128)(2,1)S(1)} collective-permute-done((bf16[192,1024]{1,0:T(8,128)(2,1)S(1)}, bf16[192,1024]{1,0:T(8,128)(2,1)S(1)}, u32[]{:S(2)}, u32[]{:S(2)}) %collective-permute-start.8) | collective-permute-done | bytes 393248 | tf_op jit(solution)/shard_map/ppermute | solution.py:469
  108.1 3.5 %shard_map.80.refs_0_ = bf16[192,1024]{1,0:T(8,128)(2,1)S(1)} custom-call(s32[7]{0:T(128)S(1)} %stack.31.where_ref, bf16[192,1024]{1,0:T(8,128)(2,1)S(1)} %shard_map.72.refs_8_.own_ref, bf16[192,1024]{1,0:T(8,128)(2,1)S(1)} %collective-permute-done.8.refs_1_.other_ref, bf16[4,256,512]{2,1,0:T(8,128)(2,1)S(1)} %shard_map.66.refs_0_, ...), custom_call_target="tpu_custom_call" | custom-call | tf_op jit(solution)/shard_map/pallas_call | solution.py:313
  112.4 4.6 %collective-permute-start.18 = (bf16[192,1024]{1,0:T(8,128)(2,1)S(1)}, bf16[192,1024]{1,0:T(8,128)(2,1)S(1)}, u32[]{:S(2)}, u32[]{:S(2)}) collective-permute-start(bf16[192,1024]{1,0:T(8,128)(2,1)S(1)} %shard_map.81), channel_id=1, source_target_pairs={{0,3},{1,2},{2,1},{3,0},{4,7},{5,6},{6,5},{7,4},{8,11},{9,10},{10,... | collective-permute-start | bytes 1179656 | tf_op jit(solution)/shard_map/ppermute | solution.py:479
  117.0 19.2 %collective-permute-done.16.other_ref = bf16[176,1024]{1,0:T(8,128)(2,1)S(1)} collective-permute-done((bf16[176,1024]{1,0:T(8,128)(2,1)S(1)}, bf16[176,1024]{1,0:T(8,128)(2,1)S(1)}, u32[]{:S(2)}, u32[]{:S(2)}) %collective-permute-start.16) | collective-permute-done | bytes 360480 | tf_op jit(solution)/shard_map/ppermute | solution.py:469
  136.2 3.5 %shard_map.79.refs_0_ = bf16[176,1024]{1,0:T(8,128)(2,1)S(1)} custom-call(s32[7]{0:T(128)S(1)} %stack.31.where_ref, bf16[176,1024]{1,0:T(8,128)(2,1)S(1)} %shard_map.77.own_ref, bf16[176,1024]{1,0:T(8,128)(2,1)S(1)} %collective-permute-done.16.other_ref, bf16[4,256,512]{2,1,0:T(8,128)(2,1)S(1)} %shard_map.66.refs_0_, ...), custom_call_target="tpu_custom_call" | custom-call | tf_op jit(solution)/shard_map/pallas_call | solution.py:313
  139.8 3.5 %shard_map.83.refs_8_ = bf16[512,1024]{1,0:T(8,128)(2,1)} custom-call(s32[7]{0:T(128)S(1)} %stack.31.where_ref, bf16[144,1024]{1,0:T(8,128)(2,1)S(1)} %shard_map.69.refs_0_.own_ref, bf16[144,1024]{1,0:T(8,128)(2,1)S(1)} %collective-permute-done.7.refs_1_.other_ref, bf16[144,1024]{1,0:T(8,128)(2,1)S(1)} %collective-permute-done.17.refs_1_.arrived_ref, ...), custom_call_target="tpu_custom_call" | custom-call | tf_op jit(solution)/shard_map/pallas_call | solution.py:313
  143.3 2.6 %shard_map.78.kept_ref = f32[176,1024]{1,0:T(8,128)S(1)} custom-call(s32[7]{0:T(128)S(1)} %stack.31.where_ref, bf16[176,1024]{1,0:T(8,128)(2,1)S(1)} %shard_map.77.own_ref, bf16[176,1024]{1,0:T(8,128)(2,1)S(1)} %collective-permute-done.16.other_ref, bf16[4,256,512]{2,1,0:T(8,128)(2,1)S(1)} %shard_map.66.refs_0_, bf16[4,256,512]{2,1,0:T(8,128)(2,1)S(1)} %shard_map.73.refs_1_, ...), custom_call_target="tpu_custom_call" | custom-call | tf_op jit(solution)/shard_map/pallas_call | solution.py:313
  145.9 3.4 %shard_map.84._ = bf16[512,1024]{1,0:T(8,128)(2,1)} custom-call(s32[7]{0:T(128)S(1)} %stack.31.where_ref, bf16[192,1024]{1,0:T(8,128)(2,1)S(1)} %shard_map.72.refs_8_.own_ref, bf16[192,1024]{1,0:T(8,128)(2,1)S(1)} %collective-permute-done.8.refs_1_.other_ref, ...), custom_call_target="tpu_custom_call", output_to_operand_aliasing={{}: (12, {})} | custom-call | tf_op jit(solution)/shard_map/pallas_call | solution.py:313
  149.3 7.9 %collective-permute-done.19.arrived_ref = bf16[176,1024]{1,0:T(8,128)(2,1)S(1)} collective-permute-done((bf16[176,1024]{1,0:T(8,128)(2,1)S(1)}, bf16[176,1024]{1,0:T(8,128)(2,1)S(1)}, u32[]{:S(2)}, u32[]{:S(2)}) %collective-permute-start.19) | collective-permute-done | bytes 360480 | tf_op jit(solution)/shard_map/ppermute | solution.py:479
  (48 shorter events, 21.2 us)
Async XLA Ops:
  0.0 11.9 %copy-start.1 = (bf16[1024,64]{0,1:T(8,128)(2,1)S(1)}, bf16[1024,64]{0,1:T(8,128)(2,1)}, u32[]{:S(2)}) copy-start(bf16[1024,64]{0,1:T(8,128)(2,1)} %param.11) | copy-start | bytes 393220
  2.9 36.5 %all-to-all-start = ((bf16[64,8,640]{2,1,0:T(8,128)(2,1)}), bf16[64,8,640]{2,1,0:T(8,128)(2,1)S(1)}, u32[]{:S(2)}, u32[]{:S(2)}) async-start(bf16[64,8,640]{2,1,0:T(8,128)(2,1)} %bitcast.9), calls=%async_computation | async-start | bytes 1310720 | tf_op jit(solution)/shard_map/all_to_all | solution.py:408
  11.9 11.4 %collective-permute-start.3 = (bf16[64,512]{1,0:T(8,128)(2,1)S(1)}, bf16[64,512]{1,0:T(8,128)(2,1)S(1)}, u32[]{:S(2)}, u32[]{:S(2)}) collective-permute-start(bf16[64,512]{1,0:T(8,128)(2,1)S(1)} %get-tuple-element.9), channel_id=1, source_target_pairs={{12,0},{76,1},{79,2},{15,3},{8,4},{72,5},{75,6},{11,7},{4,8},{68,9... | collective-permute-start | bytes 196616 | tf_op jit(solution)/shard_map/ppermute | solution.py:337
  12.1 11.2 %collective-permute-start = (bf16[64,512]{1,0:T(8,128)(2,1)S(1)}, bf16[64,512]{1,0:T(8,128)(2,1)S(1)}, u32[]{:S(2)}, u32[]{:S(2)}) collective-permute-start(bf16[64,512]{1,0:T(8,128)(2,1)S(1)} %get-tuple-element.10), channel_id=1, source_target_pairs={{0,0},{64,1},{67,2},{3,3},{4,4},{68,5},{71,6},{7,7},{8,8},{72,9},{... | collective-permute-start | bytes 196616 | tf_op jit(solution)/shard_map/ppermute | solution.py:337
  12.8 10.6 %collective-permute-start.1 = (bf16[64,512]{1,0:T(8,128)(2,1)S(1)}, bf16[64,512]{1,0:T(8,128)(2,1)S(1)}, u32[]{:S(2)}, u32[]{:S(2)}) collective-permute-start(bf16[64,512]{1,0:T(8,128)(2,1)S(1)} %get-tuple-element.9), channel_id=1, source_target_pairs={{4,0},{68,1},{71,2},{7,3},{0,4},{64,5},{67,6},{3,7},{12,8},{76,9},... | collective-permute-start | bytes 196616 | tf_op jit(solution)/shard_map/ppermute | solution.py:337
  13.3 11.5 %collective-permute-start.2 = (bf16[64,512]{1,0:T(8,128)(2,1)S(1)}, bf16[64,512]{1,0:T(8,128)(2,1)S(1)}, u32[]{:S(2)}, u32[]{:S(2)}) collective-permute-start(bf16[64,512]{1,0:T(8,128)(2,1)S(1)} %get-tuple-element.10), channel_id=1, source_target_pairs={{8,0},{72,1},{75,2},{11,3},{12,4},{76,5},{79,6},{15,7},{0,8},{64,9... | collective-permute-start | bytes 196616 | tf_op jit(solution)/shard_map/ppermute | solution.py:337
  25.4 9.5 %collective-permute-start.4 = (bf16[256,512]{1,0:T(8,128)(2,1)S(1)}, bf16[256,512]{1,0:T(8,128)(2,1)S(1)}, u32[]{:S(2)}, u32[]{:S(2)}) collective-permute-start(bf16[256,512]{1,0:T(8,128)(2,1)S(1)} %shard_map.65.refs_0_), channel_id=1, source_target_pairs={{16,0},{17,1},{18,2},{19,3},{68,4},{69,5},{70,6},{71,7},{24,8},{25... | collective-permute-start | bytes 786440 | tf_op jit(solution)/shard_map/ppermute | solution.py:337
  28.1 8.0 %collective-permute-start.5 = (bf16[256,512]{1,0:T(8,128)(2,1)S(1)}, bf16[256,512]{1,0:T(8,128)(2,1)S(1)}, u32[]{:S(2)}, u32[]{:S(2)}) collective-permute-start(bf16[256,512]{1,0:T(8,128)(2,1)S(1)} %shard_map.65.refs_0_), channel_id=1, source_target_pairs={{32,0},{33,1},{34,2},{35,3},{132,4},{133,5},{134,6},{135,7},{40,8}... | collective-permute-start | bytes 786440 | tf_op jit(solution)/shard_map/ppermute | solution.py:337
  29.0 9.8 %collective-permute-start.6 = (bf16[256,512]{1,0:T(8,128)(2,1)S(1)}, bf16[256,512]{1,0:T(8,128)(2,1)S(1)}, u32[]{:S(2)}, u32[]{:S(2)}) collective-permute-start(bf16[256,512]{1,0:T(8,128)(2,1)S(1)} %shard_map.65.refs_0_), channel_id=1, source_target_pairs={{48,0},{49,1},{50,2},{51,3},{196,4},{197,5},{198,6},{199,7},{56,8}... | collective-permute-start | bytes 786440 | tf_op jit(solution)/shard_map/ppermute | solution.py:337
  33.9 5.5 %copy-start = (f32[512,128]{1,0:T(8,128)S(1)}, f32[512,128]{1,0:T(8,128)}, u32[]{:S(2)}) copy-start(f32[512,128]{1,0:T(8,128)} %get-tuple-element.7.refs_1_.terms_hbm) | copy-start | bytes 786436
  42.8 27.1 %all-to-all-start.1 = ((bf16[64,8,640]{2,1,0:T(8,128)(2,1)}), bf16[64,8,640]{2,1,0:T(8,128)(2,1)}, u32[]{:S(2)}, u32[]{:S(2)}) async-start(bf16[64,8,640]{2,1,0:T(8,128)(2,1)} %bitcast.12), calls=%async_computation.1 | async-start | bytes 1310720 | tf_op jit(solution)/shard_map/all_to_all | solution.py:434
  57.1 21.9 %collective-permute-start.11 = (bf16[4,256,512]{2,1,0:T(8,128)(2,1)S(1)}, bf16[4,256,512]{2,1,0:T(8,128)(2,1)}, u32[]{:S(2)}, u32[]{:S(2)}) collective-permute-start(bf16[4,256,512]{2,1,0:T(8,128)(2,1)S(1)} %shard_map.66.refs_0_), channel_id=1, source_target_pairs={{192,0},{193,1},{194,2},{195,3},{52,4},{53,5},{54,6},{55,7},{200,8... | collective-permute-start | bytes 3145736 | tf_op jit(solution)/shard_map/ppermute | solution.py:337
  58.6 20.5 %collective-permute-start.9 = (bf16[4,256,512]{2,1,0:T(8,128)(2,1)S(1)}, bf16[4,256,512]{2,1,0:T(8,128)(2,1)S(1)}, u32[]{:S(2)}, u32[]{:S(2)}) collective-permute-start(bf16[4,256,512]{2,1,0:T(8,128)(2,1)S(1)} %shard_map.66.refs_0_), channel_id=1, source_target_pairs={{64,0},{65,1},{66,2},{67,3},{20,4},{21,5},{22,6},{23,7},{72,8},{73... | collective-permute-start | bytes 3145736 | tf_op jit(solution)/shard_map/ppermute | solution.py:337
  60.4 29.9 %collective-permute-start.10 = (bf16[4,256,512]{2,1,0:T(8,128)(2,1)S(1)}, bf16[4,256,512]{2,1,0:T(8,128)(2,1)S(1)}, u32[]{:S(2)}, u32[]{:S(2)}) collective-permute-start(bf16[4,256,512]{2,1,0:T(8,128)(2,1)S(1)} %shard_map.66.refs_0_), channel_id=1, source_target_pairs={{128,0},{129,1},{130,2},{131,3},{36,4},{37,5},{38,6},{39,7},{136,8... | collective-permute-start | bytes 3145736 | tf_op jit(solution)/shard_map/ppermute | solution.py:337
  71.9 18.4 %collective-permute-start.7 = (bf16[144,1024]{1,0:T(8,128)(2,1)S(1)}, bf16[144,1024]{1,0:T(8,128)(2,1)S(1)}, u32[]{:S(2)}, u32[]{:S(2)}) collective-permute-start(bf16[144,1024]{1,0:T(8,128)(2,1)S(1)} %shard_map.69.refs_0_.own_ref), channel_id=1, source_target_pairs={{0,1},{1,0},{2,3},{3,2},{4,5},{5,4},{6,7},{7,6},{8,9},{9,8},{10,11... | collective-permute-start | bytes 884744 | tf_op jit(solution)/shard_map/ppermute | solution.py:449
  72.0 18.4 %collective-permute-start.12 = (bf16[4,256,512]{2,1,0:T(8,128)(2,1)S(1)}, bf16[4,256,512]{2,1,0:T(8,128)(2,1)S(1)}, u32[]{:S(2)}, u32[]{:S(2)}) collective-permute-start(bf16[4,256,512]{2,1,0:T(8,128)(2,1)S(1)} %shard_map.66.refs_0_), channel_id=1, source_target_pairs={{0,4},{4,0},{1,5},{5,1},{2,6},{6,2},{3,7},{7,3},{8,12},{12,8},{9,1... | collective-permute-start | bytes 3145736 | tf_op jit(solution)/shard_map/ppermute | solution.py:454
  79.0 11.4 %collective-permute-start.15 = (bf16[4,256,512]{2,1,0:T(8,128)(2,1)}, bf16[4,256,512]{2,1,0:T(8,128)(2,1)S(1)}, u32[]{:S(2)}, u32[]{:S(2)}) collective-permute-start(bf16[4,256,512]{2,1,0:T(8,128)(2,1)} %shard_map.75.refs_3_), channel_id=1, source_target_pairs={{0,4},{4,0},{1,5},{5,1},{2,6},{6,2},{3,7},{7,3},{8,12},{12,8},{9,1... | collective-permute-start | bytes 3145736 | tf_op jit(solution)/shard_map/ppermute | solution.py:454
  79.1 11.3 %collective-permute-start.13 = (bf16[4,256,512]{2,1,0:T(8,128)(2,1)S(1)}, bf16[4,256,512]{2,1,0:T(8,128)(2,1)S(1)}, u32[]{:S(2)}, u32[]{:S(2)}) collective-permute-start(bf16[4,256,512]{2,1,0:T(8,128)(2,1)S(1)} %shard_map.73.refs_1_), channel_id=1, source_target_pairs={{0,4},{4,0},{1,5},{5,1},{2,6},{6,2},{3,7},{7,3},{8,12},{12,8},{9,1... | collective-permute-start | bytes 3145736 | tf_op jit(solution)/shard_map/ppermute | solution.py:454
  90.3 2.7 %collective-permute-start.14 = (bf16[4,256,512]{2,1,0:T(8,128)(2,1)S(1)}, bf16[4,256,512]{2,1,0:T(8,128)(2,1)S(1)}, u32[]{:S(2)}, u32[]{:S(2)}) collective-permute-start(bf16[4,256,512]{2,1,0:T(8,128)(2,1)S(1)} %shard_map.74.refs_2_), channel_id=1, source_target_pairs={{0,4},{4,0},{1,5},{5,1},{2,6},{6,2},{3,7},{7,3},{8,12},{12,8},{9,1... | collective-permute-start | bytes 3145736 | tf_op jit(solution)/shard_map/ppermute | solution.py:454
  90.4 17.6 %collective-permute-start.8 = (bf16[192,1024]{1,0:T(8,128)(2,1)S(1)}, bf16[192,1024]{1,0:T(8,128)(2,1)S(1)}, u32[]{:S(2)}, u32[]{:S(2)}) collective-permute-start(bf16[192,1024]{1,0:T(8,128)(2,1)S(1)} %shard_map.72.refs_8_.own_ref), channel_id=1, source_target_pairs={{0,1},{1,0},{2,3},{3,2},{4,5},{5,4},{6,7},{7,6},{8,9},{9,8},{10,11... | collective-permute-start | bytes 1179656 | tf_op jit(solution)/shard_map/ppermute | solution.py:469
  96.4 16.0 %collective-permute-start.17 = (bf16[144,1024]{1,0:T(8,128)(2,1)S(1)}, bf16[144,1024]{1,0:T(8,128)(2,1)S(1)}, u32[]{:S(2)}, u32[]{:S(2)}) collective-permute-start(bf16[144,1024]{1,0:T(8,128)(2,1)S(1)} %shard_map.76.refs_2_), channel_id=1, source_target_pairs={{0,3},{1,2},{2,1},{3,0},{4,7},{5,6},{6,5},{7,4},{8,11},{9,10},{10,... | collective-permute-start | bytes 884744 | tf_op jit(solution)/shard_map/ppermute | solution.py:479
  112.4 27.3 %collective-permute-start.18 = (bf16[192,1024]{1,0:T(8,128)(2,1)S(1)}, bf16[192,1024]{1,0:T(8,128)(2,1)S(1)}, u32[]{:S(2)}, u32[]{:S(2)}) collective-permute-start(bf16[192,1024]{1,0:T(8,128)(2,1)S(1)} %shard_map.81), channel_id=1, source_target_pairs={{0,3},{1,2},{2,1},{3,0},{4,7},{5,6},{6,5},{7,4},{8,11},{9,10},{10,... | collective-permute-start | bytes 1179656 | tf_op jit(solution)/shard_map/ppermute | solution.py:479
  117.0 19.2 %collective-permute-start.16 = (bf16[176,1024]{1,0:T(8,128)(2,1)S(1)}, bf16[176,1024]{1,0:T(8,128)(2,1)S(1)}, u32[]{:S(2)}, u32[]{:S(2)}) collective-permute-start(bf16[176,1024]{1,0:T(8,128)(2,1)S(1)} %shard_map.77.own_ref), channel_id=1, source_target_pairs={{0,1},{1,0},{2,3},{3,2},{4,5},{5,4},{6,7},{7,6},{8,9},{9,8},{10,11... | collective-permute-start | bytes 1081352 | tf_op jit(solution)/shard_map/ppermute | solution.py:469
  139.7 17.5 %collective-permute-start.19 = (bf16[176,1024]{1,0:T(8,128)(2,1)S(1)}, bf16[176,1024]{1,0:T(8,128)(2,1)S(1)}, u32[]{:S(2)}, u32[]{:S(2)}) collective-permute-start(bf16[176,1024]{1,0:T(8,128)(2,1)S(1)} %shard_map.82), channel_id=1, source_target_pairs={{0,3},{1,2},{2,1},{3,0},{4,7},{5,6},{6,5},{7,4},{8,11},{9,10},{10,... | collective-permute-start | bytes 1081352 | tf_op jit(solution)/shard_map/ppermute | solution.py:479

commit v6 on v5

--- a/solution.py
+++ b/solution.py
@@ -15,7 +15,7 @@
 SLICE = 8
 EXT = DH + 128
 SEQ = ("x", "y", "z", "c")
-SIZES_OUT = (144, 192, 176)
+SIZES_OUT = (160, 176, 176)
 F32 = jnp.float32
 BF16 = jnp.bfloat16
 SCALE = DK ** (-0.5)

time: 159 us -> 155 us (0.975)
  waiting for transfers between devices: 75.6 us -> 45.5 us
  starting transfers between devices: 43.3 us -> 69.9 us
    ppermute x10, waiting for transfers between devices: 27.7 us -> 12.5 us  [fetch(): lax.ppermute(a, NAMES, [(index[source_of(*p)], index[p]) for p in places])]
    ppermute x2, waiting for transfers between devices: 28.9 us -> 13.7 us  [per_device(): lax.ppermute(hidden, 'h', [(j, j ^ 1) for j in range(4)])]
    ppermute x4, starting transfers between devices: 0.72 us -> 13 us  [per_device(): pieces += [lax.ppermute(a, 'c', [(0, 1), (1, 0)]) for a in pieces]]
    ppermute x3, starting transfers between devices: 6.58 us -> 13.9 us  [per_device(): arrived = lax.ppermute(send, 'h', [(j, 3 - j) for j in range(4)])]
    ppermute x2, starting transfers between devices: 0.01 us -> 4.66 us  [per_device(): lax.ppermute(hidden, 'h', [(j, j ^ 1) for j in range(4)])]
  transfers between devices with their start and end apart: 22 -> 22, of which waited for: 13 -> 12; matrix products, arithmetic and copies ran while one was open for 0% -> 0% of each run, Pallas kernels for 20% -> 20%
where the time goes in v6:
time: 155 us
  starting transfers between devices  69.9 us (45%)
  waiting for transfers between devices  45.5 us (29%)
  Pallas kernels  38.7 us (25%)
    pallas_call x22, Pallas kernels, call(): pl.pallas_call(kernel, out_shape=out_shape, compiler_params=pltpu.Compile...  38.7 us
    all_to_all x1, starting transfers between devices, per_device(): lax.all_to_all(entering.reshape(BLOCKS, SLICE, EXT), SEQ, 0, 0, tiled=True)  14.3 us
    ppermute x3, starting transfers between devices, per_device(): arrived = lax.ppermute(send, 'h', [(j, 3 - j) for j in range(4)])  13.9 us
    ppermute x10, starting transfers between devices, fetch(): lax.ppermute(a, NAMES, [(index[source_of(*p)], index[p]) for p in places])  13.7 us
    ppermute x2, waiting for transfers between devices, per_device(): lax.ppermute(hidden, 'h', [(j, j ^ 1) for j in range(4)])  13.7 us
    ppermute x4, starting transfers between devices, per_device(): pieces += [lax.ppermute(a, 'c', [(0, 1), (1, 0)]) for a in pieces]  13 us
    ppermute x10, waiting for transfers between devices, fetch(): lax.ppermute(a, NAMES, [(index[source_of(*p)], index[p]) for p in places])  12.5 us
    ppermute x3, waiting for transfers between devices, per_device(): arrived = lax.ppermute(send, 'h', [(j, 3 - j) for j in range(4)])  9.3 us
  transfers between devices with their start and end apart: 22, of which 12 were waited for; matrix products, arithmetic and copies ran while one was open for 0% of the time, Pallas kernels for 20%

profile of v6, /device:TPU:32, one launch (start us, length us, event | category | flops | bytes accessed | tf_op | source)
XLA Modules:
  0.0 154.6 jit_solution(12850221314122188460)
XLA Ops:
  0.0 2.9 %shard_map.64.refs_4_ = bf16[512,640]{1,0:T(8,128)(2,1)} custom-call(bf16[512,512]{1,0:T(8,128)(2,1)} %k_hbm.3, bf16[512,1024]{1,0:T(8,128)(2,1)} %v_hbm.3, f32[2,512]{1,0:T(2,128)} %bitcast.16, f32[2,512]{1,0:T(2,128)} %bitcast.18), custom_call_target="tpu_custom_call" | custom-call | tf_op jit(solution)/shard_map/pallas_call | solution.py:313
  2.9 9.0 %all-to-all-start = ((bf16[64,8,640]{2,1,0:T(8,128)(2,1)}), bf16[64,8,640]{2,1,0:T(8,128)(2,1)S(1)}, u32[]{:S(2)}, u32[]{:S(2)}) async-start(bf16[64,8,640]{2,1,0:T(8,128)(2,1)} %bitcast.9), calls=%async_computation | async-start | bytes 1310720 | tf_op jit(solution)/shard_map/all_to_all | solution.py:408
  14.9 8.7 %collective-permute-done.3.refs_3_._ = bf16[64,512]{1,0:T(8,128)(2,1)S(1)} collective-permute-done((bf16[64,512]{1,0:T(8,128)(2,1)S(1)}, bf16[64,512]{1,0:T(8,128)(2,1)S(1)}, u32[]{:S(2)}, u32[]{:S(2)}) %collective-permute-start.3) | collective-permute-done | bytes 65568 | tf_op jit(solution)/shard_map/ppermute | solution.py:337
  27.6 2.7 %collective-permute-start.5 = (bf16[256,512]{1,0:T(8,128)(2,1)S(1)}, bf16[256,512]{1,0:T(8,128)(2,1)S(1)}, u32[]{:S(2)}, u32[]{:S(2)}) collective-permute-start(bf16[256,512]{1,0:T(8,128)(2,1)S(1)} %shard_map.65.refs_0_), channel_id=1, source_target_pairs={{32,0},{33,1},{34,2},{35,3},{132,4},{133,5},{134,6},{135,7},{40,8}... | collective-permute-start | bytes 786440 | tf_op jit(solution)/shard_map/ppermute | solution.py:337
  31.7 4.1 %shard_map.67 = (f32[512,1024]{1,0:T(8,128)}, f32[512,128]{1,0:T(8,128)}) custom-call(bf16[512,512]{1,0:T(8,128)(2,1)} %q_hbm.7, bf16[512,512]{1,0:T(8,128)(2,1)} %k_hbm.3, bf16[512,1024]{1,0:T(8,128)(2,1)} %v_hbm.3, f32[2,512]{1,0:T(2,128)} %bitcast.17, f32[2,512]{1,0:T(2,128)} %bitcast.19, bf16[64,512]{1,0:T(8,128)(2,1)S(1)} %collective-permute-done.3.refs_3_._), custom_call_target="tpu_custom_call" | custom-call | tf_op jit(solution)/shard_map/pallas_call | solution.py:313
  38.0 3.3 %shard_map.68 = bf16[512,640]{1,0:T(8,128)(2,1)} custom-call(bf16[512,640]{1,0:T(8,128)(2,1)S(1)} %bitcast.14, bf16[4,256,512]{2,1,0:T(8,128)(2,1)S(1)} %shard_map.66.refs_0_, f32[512,128]{1,0:T(8,128)S(1)} %copy-done), custom_call_target="tpu_custom_call" | custom-call | tf_op jit(solution)/shard_map/pallas_call | solution.py:313
  41.3 14.3 %all-to-all-start.1 = ((bf16[64,8,640]{2,1,0:T(8,128)(2,1)}), bf16[64,8,640]{2,1,0:T(8,128)(2,1)}, u32[]{:S(2)}, u32[]{:S(2)}) async-start(bf16[64,8,640]{2,1,0:T(8,128)(2,1)} %bitcast.12), calls=%async_computation.1 | async-start | bytes 1310720 | tf_op jit(solution)/shard_map/all_to_all | solution.py:434
  55.6 3.0 %collective-permute-start.9 = (bf16[4,256,512]{2,1,0:T(8,128)(2,1)S(1)}, bf16[4,256,512]{2,1,0:T(8,128)(2,1)}, u32[]{:S(2)}, u32[]{:S(2)}) collective-permute-start(bf16[4,256,512]{2,1,0:T(8,128)(2,1)S(1)} %shard_map.66.refs_0_), channel_id=1, source_target_pairs={{64,0},{65,1},{66,2},{67,3},{20,4},{21,5},{22,6},{23,7},{72,8},{73... | collective-permute-start | bytes 3145736 | tf_op jit(solution)/shard_map/ppermute | solution.py:337
  60.8 7.6 %all-to-all-done.1 = bf16[64,8,640]{2,1,0:T(8,128)(2,1)} async-done(((bf16[64,8,640]{2,1,0:T(8,128)(2,1)}), bf16[64,8,640]{2,1,0:T(8,128)(2,1)}, u32[]{:S(2)}, u32[]{:S(2)}) %all-to-all-start.1) | async-done | bytes 655392 | tf_op jit(solution)/shard_map/all_to_all | solution.py:434
  77.5 12.3 %collective-permute-start.15 = (bf16[4,256,512]{2,1,0:T(8,128)(2,1)S(1)}, bf16[4,256,512]{2,1,0:T(8,128)(2,1)S(1)}, u32[]{:S(2)}, u32[]{:S(2)}) collective-permute-start(bf16[4,256,512]{2,1,0:T(8,128)(2,1)S(1)} %shard_map.75.refs_3_), channel_id=1, source_target_pairs={{0,4},{4,0},{1,5},{5,1},{2,6},{6,2},{3,7},{7,3},{8,12},{12,8},{9,1... | collective-permute-start | bytes 3145736 | tf_op jit(solution)/shard_map/ppermute | solution.py:454
  93.6 2.6 %shard_map.76.refs_2_ = bf16[160,1024]{1,0:T(8,128)(2,1)S(1)} custom-call(s32[7]{0:T(128)S(1)} %stack.31.where_ref, bf16[160,1024]{1,0:T(8,128)(2,1)S(1)} %shard_map.69.refs_0_.own_ref, bf16[160,1024]{1,0:T(8,128)(2,1)S(1)} %collective-permute-done.7.refs_1_.other_ref, bf16[4,256,512]{2,1,0:T(8,128)(2,1)S(1)} %shard_map.66.refs_0_, ...), custom_call_target="tpu_custom_call" | custom-call | tf_op jit(solution)/shard_map/pallas_call | solution.py:313
  96.1 4.7 %collective-permute-start.17 = (bf16[160,1024]{1,0:T(8,128)(2,1)S(1)}, bf16[160,1024]{1,0:T(8,128)(2,1)S(1)}, u32[]{:S(2)}, u32[]{:S(2)}) collective-permute-start(bf16[160,1024]{1,0:T(8,128)(2,1)S(1)} %shard_map.76.refs_2_), channel_id=1, source_target_pairs={{0,3},{1,2},{2,1},{3,0},{4,7},{5,6},{6,5},{7,4},{8,11},{9,10},{10,... | collective-permute-start | bytes 983048 | tf_op jit(solution)/shard_map/ppermute | solution.py:479
  100.8 6.3 %collective-permute-done.8.refs_1_.other_ref = bf16[176,1024]{1,0:T(8,128)(2,1)S(1)} collective-permute-done((bf16[176,1024]{1,0:T(8,128)(2,1)S(1)}, bf16[176,1024]{1,0:T(8,128)(2,1)S(1)}, u32[]{:S(2)}, u32[]{:S(2)}) %collective-permute-start.8) | collective-permute-done | bytes 360480 | tf_op jit(solution)/shard_map/ppermute | solution.py:469
  107.1 3.4 %collective-permute-start.16 = (bf16[176,1024]{1,0:T(8,128)(2,1)S(1)}, bf16[176,1024]{1,0:T(8,128)(2,1)S(1)}, u32[]{:S(2)}, u32[]{:S(2)}) collective-permute-start(bf16[176,1024]{1,0:T(8,128)(2,1)S(1)} %shard_map.77.own_ref), channel_id=1, source_target_pairs={{0,1},{1,0},{2,3},{3,2},{4,5},{5,4},{6,7},{7,6},{8,9},{9,8},{10,11... | collective-permute-start | bytes 1081352 | tf_op jit(solution)/shard_map/ppermute | solution.py:469
  110.5 2.6 %shard_map.80.refs_0_ = bf16[176,1024]{1,0:T(8,128)(2,1)S(1)} custom-call(s32[7]{0:T(128)S(1)} %stack.31.where_ref, bf16[176,1024]{1,0:T(8,128)(2,1)S(1)} %shard_map.72.refs_8_.own_ref, bf16[176,1024]{1,0:T(8,128)(2,1)S(1)} %collective-permute-done.8.refs_1_.other_ref, bf16[4,256,512]{2,1,0:T(8,128)(2,1)S(1)} %shard_map.66.refs_0_, ...), custom_call_target="tpu_custom_call" | custom-call | tf_op jit(solution)/shard_map/pallas_call | solution.py:313
  114.0 4.6 %collective-permute-start.18 = (bf16[176,1024]{1,0:T(8,128)(2,1)S(1)}, bf16[176,1024]{1,0:T(8,128)(2,1)S(1)}, u32[]{:S(2)}, u32[]{:S(2)}) collective-permute-start(bf16[176,1024]{1,0:T(8,128)(2,1)S(1)} %shard_map.81), channel_id=1, source_target_pairs={{0,3},{1,2},{2,1},{3,0},{4,7},{5,6},{6,5},{7,4},{8,11},{9,10},{10,... | collective-permute-start | bytes 1081352 | tf_op jit(solution)/shard_map/ppermute | solution.py:479
  118.5 7.4 %collective-permute-done.16.other_ref = bf16[176,1024]{1,0:T(8,128)(2,1)S(1)} collective-permute-done((bf16[176,1024]{1,0:T(8,128)(2,1)S(1)}, bf16[176,1024]{1,0:T(8,128)(2,1)S(1)}, u32[]{:S(2)}, u32[]{:S(2)}) %collective-permute-start.16) | collective-permute-done | bytes 360480 | tf_op jit(solution)/shard_map/ppermute | solution.py:469
  126.0 2.6 %shard_map.79.refs_0_ = bf16[176,1024]{1,0:T(8,128)(2,1)S(1)} custom-call(s32[7]{0:T(128)S(1)} %stack.31.where_ref, bf16[176,1024]{1,0:T(8,128)(2,1)S(1)} %shard_map.77.own_ref, bf16[176,1024]{1,0:T(8,128)(2,1)S(1)} %collective-permute-done.16.other_ref, bf16[4,256,512]{2,1,0:T(8,128)(2,1)S(1)} %shard_map.66.refs_0_, ...), custom_call_target="tpu_custom_call" | custom-call | tf_op jit(solution)/shard_map/pallas_call | solution.py:313
  128.6 5.0 %collective-permute-done.18.refs_1_.arrived_ref = bf16[176,1024]{1,0:T(8,128)(2,1)S(1)} collective-permute-done((bf16[176,1024]{1,0:T(8,128)(2,1)S(1)}, bf16[176,1024]{1,0:T(8,128)(2,1)S(1)}, u32[]{:S(2)}, u32[]{:S(2)}) %collective-permute-start.18) | collective-permute-done | bytes 360480 | tf_op jit(solution)/shard_map/ppermute | solution.py:479
  133.5 4.7 %collective-permute-start.19 = (bf16[176,1024]{1,0:T(8,128)(2,1)S(1)}, bf16[176,1024]{1,0:T(8,128)(2,1)S(1)}, u32[]{:S(2)}, u32[]{:S(2)}) collective-permute-start(bf16[176,1024]{1,0:T(8,128)(2,1)S(1)} %shard_map.82), channel_id=1, source_target_pairs={{0,3},{1,2},{2,1},{3,0},{4,7},{5,6},{6,5},{7,4},{8,11},{9,10},{10,... | collective-permute-start | bytes 1081352 | tf_op jit(solution)/shard_map/ppermute | solution.py:479
  138.2 4.2 %shard_map.83.refs_8_ = bf16[512,1024]{1,0:T(8,128)(2,1)} custom-call(s32[7]{0:T(128)S(1)} %stack.31.where_ref, bf16[160,1024]{1,0:T(8,128)(2,1)S(1)} %shard_map.69.refs_0_.own_ref, bf16[160,1024]{1,0:T(8,128)(2,1)S(1)} %collective-permute-done.7.refs_1_.other_ref, bf16[160,1024]{1,0:T(8,128)(2,1)S(1)} %collective-permute-done.17.refs_1_.arrived_ref, ...), custom_call_target="tpu_custom_call" | custom-call | tf_op jit(solution)/shard_map/pallas_call | solution.py:313
  142.4 3.5 %shard_map.78.kept_ref = f32[176,1024]{1,0:T(8,128)S(1)} custom-call(s32[7]{0:T(128)S(1)} %stack.31.where_ref, bf16[176,1024]{1,0:T(8,128)(2,1)S(1)} %shard_map.77.own_ref, bf16[176,1024]{1,0:T(8,128)(2,1)S(1)} %collective-permute-done.16.other_ref, bf16[4,256,512]{2,1,0:T(8,128)(2,1)S(1)} %shard_map.66.refs_0_, bf16[4,256,512]{2,1,0:T(8,128)(2,1)} %shard_map.73.refs_1_, ...), custom_call_target="tpu_custom_call" | custom-call | tf_op jit(solution)/shard_map/pallas_call | solution.py:313
  145.9 4.2 %shard_map.84._ = bf16[512,1024]{1,0:T(8,128)(2,1)} custom-call(s32[7]{0:T(128)S(1)} %stack.31.where_ref, bf16[176,1024]{1,0:T(8,128)(2,1)S(1)} %shard_map.72.refs_8_.own_ref, bf16[176,1024]{1,0:T(8,128)(2,1)S(1)} %collective-permute-done.8.refs_1_.other_ref, ...), custom_call_target="tpu_custom_call", output_to_operand_aliasing={{}: (12, {})} | custom-call | tf_op jit(solution)/shard_map/pallas_call | solution.py:313
  150.2 3.5 %collective-permute-done.19.arrived_ref = bf16[176,1024]{1,0:T(8,128)(2,1)S(1)} collective-permute-done((bf16[176,1024]{1,0:T(8,128)(2,1)S(1)}, bf16[176,1024]{1,0:T(8,128)(2,1)S(1)}, u32[]{:S(2)}, u32[]{:S(2)}) %collective-permute-start.19) | collective-permute-done | bytes 360480 | tf_op jit(solution)/shard_map/ppermute | solution.py:479
  (48 shorter events, 27.2 us)
Async XLA Ops:
  0.0 11.9 %copy-start.1 = (bf16[1024,64]{0,1:T(8,128)(2,1)S(1)}, bf16[1024,64]{0,1:T(8,128)(2,1)}, u32[]{:S(2)}) copy-start(bf16[1024,64]{0,1:T(8,128)(2,1)} %param.11) | copy-start | bytes 393220
  2.9 35.1 %all-to-all-start = ((bf16[64,8,640]{2,1,0:T(8,128)(2,1)}), bf16[64,8,640]{2,1,0:T(8,128)(2,1)S(1)}, u32[]{:S(2)}, u32[]{:S(2)}) async-start(bf16[64,8,640]{2,1,0:T(8,128)(2,1)} %bitcast.9), calls=%async_computation | async-start | bytes 1310720 | tf_op jit(solution)/shard_map/all_to_all | solution.py:408
  11.9 11.7 %collective-permute-start.3 = (bf16[64,512]{1,0:T(8,128)(2,1)S(1)}, bf16[64,512]{1,0:T(8,128)(2,1)S(1)}, u32[]{:S(2)}, u32[]{:S(2)}) collective-permute-start(bf16[64,512]{1,0:T(8,128)(2,1)S(1)} %get-tuple-element.9), channel_id=1, source_target_pairs={{12,0},{76,1},{79,2},{15,3},{8,4},{72,5},{75,6},{11,7},{4,8},{68,9... | collective-permute-start | bytes 196616 | tf_op jit(solution)/shard_map/ppermute | solution.py:337
  12.1 11.5 %collective-permute-start.1 = (bf16[64,512]{1,0:T(8,128)(2,1)S(1)}, bf16[64,512]{1,0:T(8,128)(2,1)S(1)}, u32[]{:S(2)}, u32[]{:S(2)}) collective-permute-start(bf16[64,512]{1,0:T(8,128)(2,1)S(1)} %get-tuple-element.9), channel_id=1, source_target_pairs={{4,0},{68,1},{71,2},{7,3},{0,4},{64,5},{67,6},{3,7},{12,8},{76,9},... | collective-permute-start | bytes 196616 | tf_op jit(solution)/shard_map/ppermute | solution.py:337
  12.6 12.9 %collective-permute-start.2 = (bf16[64,512]{1,0:T(8,128)(2,1)S(1)}, bf16[64,512]{1,0:T(8,128)(2,1)S(1)}, u32[]{:S(2)}, u32[]{:S(2)}) collective-permute-start(bf16[64,512]{1,0:T(8,128)(2,1)S(1)} %get-tuple-element.10), channel_id=1, source_target_pairs={{8,0},{72,1},{75,2},{11,3},{12,4},{76,5},{79,6},{15,7},{0,8},{64,9... | collective-permute-start | bytes 196616 | tf_op jit(solution)/shard_map/ppermute | solution.py:337
  14.2 11.3 %collective-permute-start = (bf16[64,512]{1,0:T(8,128)(2,1)S(1)}, bf16[64,512]{1,0:T(8,128)(2,1)S(1)}, u32[]{:S(2)}, u32[]{:S(2)}) collective-permute-start(bf16[64,512]{1,0:T(8,128)(2,1)S(1)} %get-tuple-element.10), channel_id=1, source_target_pairs={{0,0},{64,1},{67,2},{3,3},{4,4},{68,5},{71,6},{7,7},{8,8},{72,9},{... | collective-permute-start | bytes 196616 | tf_op jit(solution)/shard_map/ppermute | solution.py:337
  26.0 9.8 %collective-permute-start.6 = (bf16[256,512]{1,0:T(8,128)(2,1)S(1)}, bf16[256,512]{1,0:T(8,128)(2,1)S(1)}, u32[]{:S(2)}, u32[]{:S(2)}) collective-permute-start(bf16[256,512]{1,0:T(8,128)(2,1)S(1)} %shard_map.65.refs_0_), channel_id=1, source_target_pairs={{48,0},{49,1},{50,2},{51,3},{196,4},{197,5},{198,6},{199,7},{56,8}... | collective-permute-start | bytes 786440 | tf_op jit(solution)/shard_map/ppermute | solution.py:337
  27.6 9.8 %collective-permute-start.5 = (bf16[256,512]{1,0:T(8,128)(2,1)S(1)}, bf16[256,512]{1,0:T(8,128)(2,1)S(1)}, u32[]{:S(2)}, u32[]{:S(2)}) collective-permute-start(bf16[256,512]{1,0:T(8,128)(2,1)S(1)} %shard_map.65.refs_0_), channel_id=1, source_target_pairs={{32,0},{33,1},{34,2},{35,3},{132,4},{133,5},{134,6},{135,7},{40,8}... | collective-permute-start | bytes 786440 | tf_op jit(solution)/shard_map/ppermute | solution.py:337
  30.2 7.2 %collective-permute-start.4 = (bf16[256,512]{1,0:T(8,128)(2,1)S(1)}, bf16[256,512]{1,0:T(8,128)(2,1)S(1)}, u32[]{:S(2)}, u32[]{:S(2)}) collective-permute-start(bf16[256,512]{1,0:T(8,128)(2,1)S(1)} %shard_map.65.refs_0_), channel_id=1, source_target_pairs={{16,0},{17,1},{18,2},{19,3},{68,4},{69,5},{70,6},{71,7},{24,8},{25... | collective-permute-start | bytes 786440 | tf_op jit(solution)/shard_map/ppermute | solution.py:337
  35.8 2.2 %copy-start = (f32[512,128]{1,0:T(8,128)S(1)}, f32[512,128]{1,0:T(8,128)}, u32[]{:S(2)}) copy-start(f32[512,128]{1,0:T(8,128)} %get-tuple-element.7.refs_1_.terms_hbm) | copy-start | bytes 786436
  41.3 27.1 %all-to-all-start.1 = ((bf16[64,8,640]{2,1,0:T(8,128)(2,1)}), bf16[64,8,640]{2,1,0:T(8,128)(2,1)}, u32[]{:S(2)}, u32[]{:S(2)}) async-start(bf16[64,8,640]{2,1,0:T(8,128)(2,1)} %bitcast.12), calls=%async_computation.1 | async-start | bytes 1310720 | tf_op jit(solution)/shard_map/all_to_all | solution.py:434
  55.6 20.8 %collective-permute-start.9 = (bf16[4,256,512]{2,1,0:T(8,128)(2,1)S(1)}, bf16[4,256,512]{2,1,0:T(8,128)(2,1)}, u32[]{:S(2)}, u32[]{:S(2)}) collective-permute-start(bf16[4,256,512]{2,1,0:T(8,128)(2,1)S(1)} %shard_map.66.refs_0_), channel_id=1, source_target_pairs={{64,0},{65,1},{66,2},{67,3},{20,4},{21,5},{22,6},{23,7},{72,8},{73... | collective-permute-start | bytes 3145736 | tf_op jit(solution)/shard_map/ppermute | solution.py:337
  58.6 18.9 %collective-permute-start.11 = (bf16[4,256,512]{2,1,0:T(8,128)(2,1)S(1)}, bf16[4,256,512]{2,1,0:T(8,128)(2,1)S(1)}, u32[]{:S(2)}, u32[]{:S(2)}) collective-permute-start(bf16[4,256,512]{2,1,0:T(8,128)(2,1)S(1)} %shard_map.66.refs_0_), channel_id=1, source_target_pairs={{192,0},{193,1},{194,2},{195,3},{52,4},{53,5},{54,6},{55,7},{200,8... | collective-permute-start | bytes 3145736 | tf_op jit(solution)/shard_map/ppermute | solution.py:337
  58.6 31.2 %collective-permute-start.10 = (bf16[4,256,512]{2,1,0:T(8,128)(2,1)S(1)}, bf16[4,256,512]{2,1,0:T(8,128)(2,1)S(1)}, u32[]{:S(2)}, u32[]{:S(2)}) collective-permute-start(bf16[4,256,512]{2,1,0:T(8,128)(2,1)S(1)} %shard_map.66.refs_0_), channel_id=1, source_target_pairs={{128,0},{129,1},{130,2},{131,3},{36,4},{37,5},{38,6},{39,7},{136,8... | collective-permute-start | bytes 3145736 | tf_op jit(solution)/shard_map/ppermute | solution.py:337
  70.7 19.1 %collective-permute-start.7 = (bf16[160,1024]{1,0:T(8,128)(2,1)S(1)}, bf16[160,1024]{1,0:T(8,128)(2,1)S(1)}, u32[]{:S(2)}, u32[]{:S(2)}) collective-permute-start(bf16[160,1024]{1,0:T(8,128)(2,1)S(1)} %shard_map.69.refs_0_.own_ref), channel_id=1, source_target_pairs={{0,1},{1,0},{2,3},{3,2},{4,5},{5,4},{6,7},{7,6},{8,9},{9,8},{10,11... | collective-permute-start | bytes 983048 | tf_op jit(solution)/shard_map/ppermute | solution.py:449
  72.0 19.1 %collective-permute-start.12 = (bf16[4,256,512]{2,1,0:T(8,128)(2,1)S(1)}, bf16[4,256,512]{2,1,0:T(8,128)(2,1)S(1)}, u32[]{:S(2)}, u32[]{:S(2)}) collective-permute-start(bf16[4,256,512]{2,1,0:T(8,128)(2,1)S(1)} %shard_map.66.refs_0_), channel_id=1, source_target_pairs={{0,4},{4,0},{1,5},{5,1},{2,6},{6,2},{3,7},{7,3},{8,12},{12,8},{9,1... | collective-permute-start | bytes 3145736 | tf_op jit(solution)/shard_map/ppermute | solution.py:454
  76.5 14.6 %collective-permute-start.13 = (bf16[4,256,512]{2,1,0:T(8,128)(2,1)}, bf16[4,256,512]{2,1,0:T(8,128)(2,1)S(1)}, u32[]{:S(2)}, u32[]{:S(2)}) collective-permute-start(bf16[4,256,512]{2,1,0:T(8,128)(2,1)} %shard_map.73.refs_1_), channel_id=1, source_target_pairs={{0,4},{4,0},{1,5},{5,1},{2,6},{6,2},{3,7},{7,3},{8,12},{12,8},{9,1... | collective-permute-start | bytes 3145736 | tf_op jit(solution)/shard_map/ppermute | solution.py:454
  77.5 14.6 %collective-permute-start.15 = (bf16[4,256,512]{2,1,0:T(8,128)(2,1)S(1)}, bf16[4,256,512]{2,1,0:T(8,128)(2,1)S(1)}, u32[]{:S(2)}, u32[]{:S(2)}) collective-permute-start(bf16[4,256,512]{2,1,0:T(8,128)(2,1)S(1)} %shard_map.75.refs_3_), channel_id=1, source_target_pairs={{0,4},{4,0},{1,5},{5,1},{2,6},{6,2},{3,7},{7,3},{8,12},{12,8},{9,1... | collective-permute-start | bytes 3145736 | tf_op jit(solution)/shard_map/ppermute | solution.py:454
  89.8 3.8 %collective-permute-start.14 = (bf16[4,256,512]{2,1,0:T(8,128)(2,1)S(1)}, bf16[4,256,512]{2,1,0:T(8,128)(2,1)S(1)}, u32[]{:S(2)}, u32[]{:S(2)}) collective-permute-start(bf16[4,256,512]{2,1,0:T(8,128)(2,1)S(1)} %shard_map.74.refs_2_), channel_id=1, source_target_pairs={{0,4},{4,0},{1,5},{5,1},{2,6},{6,2},{3,7},{7,3},{8,12},{12,8},{9,1... | collective-permute-start | bytes 3145736 | tf_op jit(solution)/shard_map/ppermute | solution.py:454
  89.9 17.2 %collective-permute-start.8 = (bf16[176,1024]{1,0:T(8,128)(2,1)S(1)}, bf16[176,1024]{1,0:T(8,128)(2,1)S(1)}, u32[]{:S(2)}, u32[]{:S(2)}) collective-permute-start(bf16[176,1024]{1,0:T(8,128)(2,1)S(1)} %shard_map.72.refs_8_.own_ref), channel_id=1, source_target_pairs={{0,1},{1,0},{2,3},{3,2},{4,5},{5,4},{6,7},{7,6},{8,9},{9,8},{10,11... | collective-permute-start | bytes 1081352 | tf_op jit(solution)/shard_map/ppermute | solution.py:469
  96.1 17.8 %collective-permute-start.17 = (bf16[160,1024]{1,0:T(8,128)(2,1)S(1)}, bf16[160,1024]{1,0:T(8,128)(2,1)S(1)}, u32[]{:S(2)}, u32[]{:S(2)}) collective-permute-start(bf16[160,1024]{1,0:T(8,128)(2,1)S(1)} %shard_map.76.refs_2_), channel_id=1, source_target_pairs={{0,3},{1,2},{2,1},{3,0},{4,7},{5,6},{6,5},{7,4},{8,11},{9,10},{10,... | collective-permute-start | bytes 983048 | tf_op jit(solution)/shard_map/ppermute | solution.py:479
  107.1 18.9 %collective-permute-start.16 = (bf16[176,1024]{1,0:T(8,128)(2,1)S(1)}, bf16[176,1024]{1,0:T(8,128)(2,1)S(1)}, u32[]{:S(2)}, u32[]{:S(2)}) collective-permute-start(bf16[176,1024]{1,0:T(8,128)(2,1)S(1)} %shard_map.77.own_ref), channel_id=1, source_target_pairs={{0,1},{1,0},{2,3},{3,2},{4,5},{5,4},{6,7},{7,6},{8,9},{9,8},{10,11... | collective-permute-start | bytes 1081352 | tf_op jit(solution)/shard_map/ppermute | solution.py:469
  114.0 19.6 %collective-permute-start.18 = (bf16[176,1024]{1,0:T(8,128)(2,1)S(1)}, bf16[176,1024]{1,0:T(8,128)(2,1)S(1)}, u32[]{:S(2)}, u32[]{:S(2)}) collective-permute-start(bf16[176,1024]{1,0:T(8,128)(2,1)S(1)} %shard_map.81), channel_id=1, source_target_pairs={{0,3},{1,2},{2,1},{3,0},{4,7},{5,6},{6,5},{7,4},{8,11},{9,10},{10,... | collective-permute-start | bytes 1081352 | tf_op jit(solution)/shard_map/ppermute | solution.py:479
  133.5 20.1 %collective-permute-start.19 = (bf16[176,1024]{1,0:T(8,128)(2,1)S(1)}, bf16[176,1024]{1,0:T(8,128)(2,1)S(1)}, u32[]{:S(2)}, u32[]{:S(2)}) collective-permute-start(bf16[176,1024]{1,0:T(8,128)(2,1)S(1)} %shard_map.82), channel_id=1, source_target_pairs={{0,3},{1,2},{2,1},{3,0},{4,7},{5,6},{6,5},{7,4},{8,11},{9,10},{10,... | collective-permute-start | bytes 1081352 | tf_op jit(solution)/shard_map/ppermute | solution.py:479
